TPU v7x, 512 devices: a whole 4x4x16 slice. The times are simulated.
512 devices in a mesh: dp: 16 (over x, y), expert: 32 (over z, core).
Axes of the slice: x: 4, y: 4, z: 16, core: 2. Of those that a mesh axis runs over, the one named last changes fastest.
Arguments:
- queries: bfloat16 [65536, 2048], P(('dp', 'expert')), may hold values from -8 to 8
- key_value: bfloat16 [65536, 2, 2048], P(('dp', 'expert')), may hold values from -20 to 20
- memory: bfloat16 [512, 128, 2, 2048], P(('dp', 'expert')), may hold values from -6 to 6
- memory_source: int32 [512], P(('dp', 'expert')), may hold values from 0 to 1
- routing: int32 [65536, 1], P(('dp', 'expert')), may hold values from 0 to 63; in each aligned block of 128 rows (0 to 127, 128 to 255, ...) at most 3 rows name the same one
- router_weight: float32 [65536, 1], P(('dp', 'expert')), may hold values from 0.25 to 1
- norm_gain: float32 [2048], replicated, may hold values from 0.25 to 1.75
- gate_matrix: bfloat16 [2048, 90112], P(None, ('dp', 'expert')), may hold values from -0.125 to 0.125
- up_matrix: bfloat16 [2048, 90112], P(None, ('dp', 'expert')), may hold values from -0.125 to 0.125
- down_matrix: bfloat16 [90112, 2048], P(('dp', 'expert')), may hold values from -0.15625 to 0.15625
Outputs:
- layer_out: bfloat16 [65536, 2048], P(('dp', 'expert'))
Inputs may be any that keep to these rules, and one draw needn't show every extreme that they name: `routing`: no expert is named by more than 3 tokens of one device; some expert is named by exactly 3 tokens of some device. A device's memory block is kept by the device 1 + memory_source places before it along dp, cyclically, with the same expert index.
All inputs are finite; a program needn't handle non-finite values.
Results may differ from a plain program's by a relative error of at most 0.023.
Values may be sent and summed in bfloat16 or wider, within the bound.
No kernel may reach another device: no remote copies, remote signals or barrier semaphores. Data moves between devices by JAX's collectives and lax.ppermute only.
A program may use at most 64 MiB of HBM per device.

v0:
```python
import math

import jax
import jax.numpy as jnp
from jax import lax
from jax.sharding import PartitionSpec as P

HEADS = 16
SLICES = 8


def passed_along(shard, axis, by):
    size = lax.axis_size(axis)
    return lax.ppermute(shard, axis, [(i, (i + by) % size) for i in range(size)])


def expert_dense(row_block, gate_matrix, up_matrix, down_matrix):
    gate_part = jnp.dot(row_block, gate_matrix, preferred_element_type=jnp.float32)
    up_part = jnp.dot(row_block, up_matrix, preferred_element_type=jnp.float32)
    activation = (jax.nn.silu(gate_part) * up_part).astype(jnp.bfloat16)
    return jnp.dot(activation, down_matrix, preferred_element_type=jnp.float32).astype(jnp.bfloat16)


def expert_part(arrived, gate_matrix, up_matrix, down_matrix):
    flat_rows = arrived.reshape(-1, arrived.shape[-1])
    output = expert_dense(flat_rows, gate_matrix, up_matrix, down_matrix)
    return output.reshape(arrived.shape)


def per_device(
    queries,
    key_value,
    memory,
    memory_source,
    routing,
    router_weight,
    norm_gain,
    gate_matrix,
    up_matrix,
    down_matrix,
):
    token_count = queries.shape[0]
    features = queries.shape[1]
    head_size = features // HEADS
    data_span = lax.axis_size("dp")
    expert_span = lax.axis_size("expert")
    row_experts = expert_span // SLICES
    expert_count = data_span * row_experts
    capacity = max(3, 3 * token_count // (2 * expert_count))
    nearer = passed_along(memory, "dp", 1)
    farther = passed_along(memory, "dp", 2)
    recalled = jnp.where(memory_source[0] == 0, nearer, farther)[0]
    keys_all = jnp.concatenate([recalled[:, 0], key_value[:, 0]], axis=0).reshape(
        -1, HEADS, head_size
    )
    values_all = jnp.concatenate([recalled[:, 1], key_value[:, 1]], axis=0).reshape(
        -1, HEADS, head_size
    )
    query_heads = queries.reshape(token_count, HEADS, head_size)
    scores = jnp.einsum(
        "thd,khd->htk", query_heads, keys_all, preferred_element_type=jnp.float32
    ) / math.sqrt(head_size)
    memory_rows = recalled.shape[0]
    key_index = jnp.arange(memory_rows + token_count)[None, :]
    query_index = jnp.arange(token_count)[:, None]
    allowed = (key_index < memory_rows) | (key_index - memory_rows <= query_index)
    scores = jnp.where(allowed[None], scores, -1e30)
    top_score = jnp.max(scores, axis=-1, keepdims=True)
    weights = jnp.exp(scores - top_score)
    weights = (weights / jnp.sum(weights, axis=-1, keepdims=True)).astype(jnp.bfloat16)
    hidden = jnp.einsum("htk,khd->thd", weights, values_all, preferred_element_type=jnp.float32)
    hidden = hidden.reshape(token_count, features).astype(jnp.bfloat16)
    hidden_wide = hidden.astype(jnp.float32)
    normed = (
        hidden_wide
        * lax.rsqrt(jnp.mean(hidden_wide * hidden_wide, axis=-1, keepdims=True) + 1e-06)
        * norm_gain
    ).astype(jnp.bfloat16)
    chosen_expert = routing[:, 0]
    one_hot = (chosen_expert[:, None] == jnp.arange(expert_count, dtype=jnp.int32)[None, :]).astype(
        jnp.int32
    )
    earlier = jnp.cumsum(one_hot, axis=0) - one_hot
    rank_within = jnp.sum(earlier * one_hot, axis=1)
    slot_index = chosen_expert * capacity + rank_within
    outgoing = (
        jnp.zeros((expert_count * capacity, features), jnp.bfloat16).at[slot_index].set(normed)
    )
    sectioned = outgoing.reshape(data_span, row_experts * capacity, features)
    landed = lax.all_to_all(sectioned, "dp", split_axis=0, concat_axis=0, tiled=True)
    grouped = landed.reshape(data_span, row_experts, capacity, features).transpose(1, 0, 2, 3)
    grouped = grouped.reshape(row_experts, 1, data_span * capacity, features)
    copies = jnp.broadcast_to(grouped, (row_experts, SLICES, data_span * capacity, features))
    copies = copies.reshape(expert_span, data_span * capacity, features)
    partial_out = expert_part(
        lax.all_to_all(copies, "expert", split_axis=0, concat_axis=0, tiled=True),
        gate_matrix,
        up_matrix,
        down_matrix,
    )
    partials = lax.all_to_all(partial_out, "expert", split_axis=0, concat_axis=0, tiled=True)
    summed = (
        partials.reshape(row_experts, SLICES, data_span, capacity, features)
        .astype(jnp.float32)
        .sum(axis=1)
    )
    summed = (
        summed.astype(jnp.bfloat16)
        .transpose(1, 0, 2, 3)
        .reshape(data_span, row_experts * capacity, features)
    )
    returned = lax.all_to_all(summed, "dp", split_axis=0, concat_axis=0, tiled=True).reshape(
        expert_count * capacity, features
    )
    expert_out = returned[slot_index]
    return (hidden_wide + router_weight * expert_out.astype(jnp.float32)).astype(jnp.bfloat16)


def solution(mesh):
    return jax.shard_map(
        per_device,
        mesh=mesh,
        in_specs=(
            P(("dp", "expert"), None),
            P(("dp", "expert"), None, None),
            P(("dp", "expert"), None, None, None),
            P(("dp", "expert")),
            P(("dp", "expert"), None),
            P(("dp", "expert"), None),
            P(),
            P(None, ("dp", "expert")),
            P(None, ("dp", "expert")),
            P(("dp", "expert"), None),
        ),
        out_specs=P(("dp", "expert"), None),
        check_vma=False,
    )
```

profile of v0, /device:TPU:6, one launch (start us, length us, event | category | flops | bytes accessed | tf_op | source)
XLA Modules:
  0.0 736.6 jit_solution(6579106832206538696)
XLA Ops:
  0.0 3.8 copy.31
  3.8 3.5 collective-permute-start
  7.3 4.8 collective-permute-start.1
  12.1 2.3 fusion.49
  15.1 2.4 copy.49
  17.8 0.9 copy.33
  19.3 36.2 %collective-permute-done = bf16[1,128,2,2048]{1,3,2,0:T(8,128)(2,1)} collective-permute-done((bf16[1,128,2,2048]{1,3,2,0:T(8,128)(2,1)}, bf16[1,128,2,2048]{1,3,2,0:T(8,128)(2,1)}, u32[]{:S(2)}, u32[]{:S(2)}) %collective-permute-start) | collective-permute-done | bytes 1048608 | tf_op jit(solution)/shard_map/ppermute | solution.py:14
  55.5 1.3 select_bitcast_fusion
  56.8 0.9 fusion.48
  58.0 3.3 fusion.50
  61.3 2.1 multiply_reduce_fusion
  64.0 2.4 scatter_custom_fusion
  66.4 1.3 reshape.103
  67.6 39.9 %all_to_all.20 = bf16[16,12,2048]{2,1,0:T(8,128)(2,1)S(1)} all-to-all(bf16[16,12,2048]{2,1,0:T(8,128)(2,1)S(1)} %reshape.103), channel_id=1, replica_groups=mesh['dp'=16,'expert'=32] {'dp'}, dimensions={0} | all-to-all | bytes 1572864 | tf_op jit(solution)/shard_map/all_to_all | solution.py:90
  107.6 0.4 copy.40
  108.0 0.6 copy.41
  108.6 0.4 copy.42
  109.1 0.8 broadcast_in_dim.36
  109.9 296.1 %all_to_all.21 = bf16[32,48,2048]{2,1,0:T(8,128)(2,1)S(1)} all-to-all(bf16[32,48,2048]{2,1,0:T(8,128)(2,1)S(1)} %bitcast.60), channel_id=1, replica_groups=mesh['dp'=16,'expert'=32] {'expert'}, dimensions={0} | all-to-all | bytes 12582912 | tf_op jit(solution)/shard_map/all_to_all | solution.py:96
  406.0 2.7 copy-done.1
  408.7 3.3 fusion.55
  411.9 10.9 %convolution_convert_fusion = bf16[1536,2048]{1,0:T(8,128)(2,1)} fusion(bf16[176,2048]{1,0:T(8,128)(2,1)S(1)} %copy-done, bf16[1536,2048]{1,0:T(8,128)(2,1)} %bitcast.62, bf16[2048,176]{0,1:T(8,128)(2,1)S(1)} %copy-done.8, f32[1536,176]{0,1:T(8,128)} %fusion.55), kind=kOutput, calls=%fused_computation.3 | convolution fusion | flops 2219360256 | bytes 15106048 | tf_op jit(solution)/shard_map/dot_general | solution.py:21
  422.9 285.3 %all_to_all.22 = bf16[32,48,2048]{2,1,0:T(8,128)(2,1)S(1)} all-to-all(bf16[32,48,2048]{2,1,0:T(8,128)(2,1)} %bitcast.63), channel_id=1, replica_groups=mesh['dp'=16,'expert'=32] {'expert'}, dimensions={0} | all-to-all | bytes 12582912 | tf_op jit(solution)/shard_map/all_to_all | solution.py:101
  708.2 1.2 bitcast_reduce_fusion
  709.4 0.6 copy.48
  710.0 0.4 copy.44
  710.4 1.5 copy.45
  711.9 6.3 all-to-all-start.3
  718.2 15.2 %all-to-all-done.3 = bf16[16,12,2048]{2,1,0:T(8,128)(2,1)} async-done(((bf16[16,12,2048]{2,1,0:T(8,128)(2,1)}), bf16[16,12,2048]{2,1,0:T(8,128)(2,1)}, u32[]{:S(2)}, u32[]{:S(2)}) %all-to-all-start.3) | async-done | bytes 786464 | tf_op jit(solution)/shard_map/all_to_all | solution.py:112
  733.4 1.3 reshape.110
  734.7 0.9 gather_fusion
  735.7 1.0 add_convert_fusion
  (30 shorter events, 1.9 us)
Async XLA Ops:
  0.0 411.9 %copy-start = (bf16[176,2048]{1,0:T(8,128)(2,1)S(1)}, bf16[176,2048]{1,0:T(8,128)(2,1)}, u32[]{:S(2)}) copy-start(bf16[176,2048]{1,0:T(8,128)(2,1)} %param.19) | copy-start | bytes 2162692
  0.0 12.1 %copy-start.2 = (bf16[128,2,2048]{2,1,0:T(2,128)(2,1)S(1)}, bf16[128,2,2048]{2,1,0:T(2,128)(2,1)}, u32[]{:S(2)}) copy-start(bf16[128,2,2048]{2,1,0:T(2,128)(2,1)} %param.11) | copy-start | bytes 3145732
  3.8 51.7 %collective-permute-start = (bf16[1,128,2,2048]{1,3,2,0:T(8,128)(2,1)}, bf16[1,128,2,2048]{1,3,2,0:T(8,128)(2,1)}, u32[]{:S(2)}, u32[]{:S(2)}) collective-permute-start(bf16[1,128,2,2048]{1,3,2,0:T(8,128)(2,1)} %copy.31), channel_id=1, source_target_pairs={{0,32},{32,64},{64,96},{96,128},{128,160},{160,192},{192,224},{224... | collective-permute-start | bytes 3145736 | tf_op jit(solution)/shard_map/ppermute | solution.py:14
  7.3 48.2 %collective-permute-start.1 = (bf16[1,128,2,2048]{1,3,2,0:T(8,128)(2,1)}, bf16[1,128,2,2048]{1,3,2,0:T(8,128)(2,1)}, u32[]{:S(2)}, u32[]{:S(2)}) collective-permute-start(bf16[1,128,2,2048]{1,3,2,0:T(8,128)(2,1)} %copy.31), channel_id=1, source_target_pairs={{0,64},{32,96},{64,128},{96,160},{128,192},{160,224},{192,256},{22... | collective-permute-start | bytes 3145736 | tf_op jit(solution)/shard_map/ppermute | solution.py:14
  15.1 3.6 copy-start.5
  58.0 3.3 copy-start.3
  63.3 0.7 copy-start.4
  109.9 298.8 %copy-start.7 = (bf16[2048,176]{0,1:T(8,128)(2,1)S(1)}, bf16[2048,176]{0,1:T(8,128)(2,1)}, u32[]{:S(2)}) copy-start(bf16[2048,176]{0,1:T(8,128)(2,1)} %param.17) | copy-start | bytes 2162692
  406.0 2.7 copy-start.1
  408.7 3.3 copy-start.8
  711.9 21.4 %all-to-all-start.3 = ((bf16[16,12,2048]{2,1,0:T(8,128)(2,1)}), bf16[16,12,2048]{2,1,0:T(8,128)(2,1)}, u32[]{:S(2)}, u32[]{:S(2)}) async-start(bf16[16,12,2048]{2,1,0:T(8,128)(2,1)} %copy.45), calls=%async_computation.3 | async-start | bytes 2097152 | tf_op jit(solution)/shard_map/all_to_all | solution.py:112
  734.7 1.0 copy-start.6
where the time goes:
time: 738 us; the launch traced here: 737 us
  blocking collectives  621 us (84%)
  waiting for transfers between devices  51.4 us (7%)
  local copies, waits for them, and re-layouts  22.5 us (3%)
  matrix products  19.5 us (3%)
  starting transfers between devices  14.5 us (2%)
    all_to_all x1, blocking collectives, per_device(): lax.all_to_all(copies, 'expert', split_axis=0, concat_axis=0, tiled=True)  296 us
    all_to_all x1, blocking collectives, per_device(): lax.all_to_all(partial_out, 'expert', split_axis=0, concat_axis=0, tiled=...  285 us
    all_to_all x1, blocking collectives, per_device(): lax.all_to_all(sectioned, 'dp', split_axis=0, concat_axis=0, tiled=True)  39.9 us
    ppermute x2, waiting for transfers between devices, passed_along(): lax.ppermute(shard, axis, [(i, (i + by) % size) for i in range(size)])  36.2 us
    all_to_all x1, waiting for transfers between devices, per_device(): lax.all_to_all(summed, 'dp', split_axis=0, concat_axis=0, tiled=True)  15.2 us
  transfers between devices with their start and end apart: 3, of which 2 were waited for; matrix products, arithmetic and copies ran while one was open for 1% of the time, Pallas kernels for 0%

commit v1 on v0

v1 whole, which is shorter than its diff:
```python
import functools
import math

import jax
import jax.numpy as jnp
import numpy as np
from jax import lax
from jax.experimental import pallas as pl
from jax.experimental.pallas import tpu as pltpu
from jax.sharding import Mesh
from jax.sharding import PartitionSpec as P

HEADS = 16
SLICES = 8
MOST = 3
LANES = 128
VMEM_BYTES = 52 * 1024 * 1024

PLACE = ((0, 2, 1, 3), (1, 3, 0, 2), (2, 0, 3, 1), (3, 1, 2, 0))


def spread_pairs():
    return [(PLACE[h][p] * 4 + p, h * 4 + p) for h in range(4) for p in range(4)]


def lift_pairs():
    return [(h * 4 + p, h * 4 + PLACE[h][p]) for h in range(4) for p in range(4)]


def ring(by):
    return [(i, (i + by) % 4) for i in range(4)]


def slots(chosen, rank):
    x = jnp.right_shift(chosen, 4)
    y = jnp.bitwise_and(jnp.right_shift(chosen, 2), 3)
    segment = jnp.bitwise_and(chosen, 3)
    return (y * 16 + segment * 4 + x) * MOST + rank.astype(jnp.int32)


def attend_kernel(
    source,
    queries,
    own_keys,
    own_values,
    near_keys,
    near_values,
    far_keys,
    far_values,
    chosen_column,
    chosen_row,
    gain,
    hidden_out,
    packed_out,
    keys,
    values,
    normed,
    rows,
    sems,
):
    tokens, features = queries.shape

    def fetch(from_keys, from_values):
        first = pltpu.make_async_copy(from_keys, keys, sems.at[0])
        second = pltpu.make_async_copy(from_values, values, sems.at[1])
        first.start()
        second.start()
        first.wait()
        second.wait()

    @pl.when(source[0] == 0)
    def _():
        fetch(near_keys, near_values)

    @pl.when(source[0] != 0)
    def _():
        fetch(far_keys, far_values)

    later = lax.broadcasted_iota(jnp.int32, (tokens, tokens), 1) > lax.broadcasted_iota(
        jnp.int32, (tokens, tokens), 0
    )
    scale = 1.0 / math.sqrt(features // HEADS)
    transposed = (((1,), (1,)), ((), ()))
    squares = jnp.zeros((tokens, LANES), jnp.float32)
    for head in range(HEADS):
        at = slice(head * LANES, (head + 1) * LANES)
        query = queries[:, at]
        far = scale * lax.dot_general(
            query, keys[:, at], transposed, preferred_element_type=jnp.float32
        )
        own = scale * lax.dot_general(
            query, own_keys[:, at], transposed, preferred_element_type=jnp.float32
        )
        own = jnp.where(later, -1e30, own)
        top = jnp.max(jnp.maximum(far, own), axis=1, keepdims=True)
        far = jnp.exp(far - top)
        own = jnp.exp(own - top)
        share = 1.0 / jnp.sum(far + own, axis=1, keepdims=True)
        hidden = jnp.dot(
            (far * share).astype(jnp.bfloat16), values[:, at], preferred_element_type=jnp.float32
        ) + jnp.dot(
            (own * share).astype(jnp.bfloat16),
            own_values[:, at],
            preferred_element_type=jnp.float32,
        )
        hidden = hidden.astype(jnp.bfloat16)
        hidden_out[:, at] = hidden
        wide = hidden.astype(jnp.float32)
        squares += wide * wide
    mean = jnp.sum(squares, axis=1, keepdims=True) / features
    factor = lax.rsqrt(mean + 1e-6)
    for head in range(HEADS):
        at = slice(head * LANES, (head + 1) * LANES)
        normed[:, at] = (hidden_out[:, at].astype(jnp.float32) * factor * gain[:, at]).astype(
            jnp.bfloat16
        )
    same = (chosen_column[...] == chosen_row[...]) & later
    rank = jnp.sum(jnp.where(same, 1.0, 0.0), axis=0, keepdims=True)
    slot = slots(chosen_row[...], rank)
    count = rows.shape[0] // (features // LANES)
    spread = jnp.where(lax.broadcasted_iota(jnp.int32, (count, tokens), 0) == slot, 1.0, 0.0)
    spread = spread.astype(jnp.bfloat16)
    blocks = features // LANES
    packed = jnp.dot(spread, normed[...], preferred_element_type=jnp.float32)
    for block in range(blocks):
        rows[pl.ds(block, count, stride=blocks), :] = packed[:, block * LANES : (block + 1) * LANES]
    packed_out[...] = rows[...].astype(jnp.bfloat16)


def attend(source, queries, own, near, far, chosen, gain):
    tokens, features = queries.shape
    blocks = features // LANES
    count = 64 * MOST
    vmem = pl.BlockSpec(memory_space=pltpu.VMEM)
    anywhere = pl.BlockSpec(memory_space=pl.ANY)
    return pl.pallas_call(
        attend_kernel,
        out_shape=(
            jax.ShapeDtypeStruct((tokens, features), jnp.bfloat16),
            jax.ShapeDtypeStruct((count * blocks, LANES), jnp.bfloat16),
        ),
        in_specs=[pl.BlockSpec(memory_space=pltpu.SMEM)]
        + [vmem] * 3
        + [anywhere] * 4
        + [vmem] * 3,
        out_specs=(vmem, vmem),
        scratch_shapes=[
            pltpu.VMEM((tokens, features), jnp.bfloat16),
            pltpu.VMEM((tokens, features), jnp.bfloat16),
            pltpu.VMEM((tokens, features), jnp.bfloat16),
            pltpu.VMEM((count * blocks, LANES), jnp.float32),
            pltpu.SemaphoreType.DMA((2,)),
        ],
        compiler_params=pltpu.CompilerParams(vmem_limit_bytes=VMEM_BYTES),
        cost_estimate=pl.CostEstimate(
            flops=4 * tokens * 2 * tokens * features,
            bytes_accessed=10 * tokens * features,
            transcendentals=2 * HEADS * tokens * tokens,
        ),
        name="attend",
    )(source, queries, *own, *near, *far, chosen, chosen.reshape(1, tokens), gain)


def experts_kernel(pieces, arrived, *refs):
    total = sum(len(half) for matrix in pieces for half in matrix)
    sources, (out, gate, up, down, rows, tokens, sems) = refs[:total], refs[total:]
    copies, number = [], 0
    for matrix, target in zip(pieces, (gate, up, down)):
        first = 0
        for half in matrix:
            group = []
            for size in half:
                group.append(
                    pltpu.make_async_copy(
                        sources[number], target.at[pl.ds(first, size)], sems.at[number]
                    )
                )
                first += size
                number += 1
            copies.append(group)
    for index in (0, 2, 1, 3, 4, 5):
        for copy in copies[index]:
            copy.start()
    count, features = tokens.shape
    blocks = features // LANES
    rows[...] = arrived[...].astype(jnp.float32)
    for block in range(blocks):
        tokens[:, block * LANES : (block + 1) * LANES] = rows[
            pl.ds(block, count, stride=blocks), :
        ].astype(jnp.bfloat16)
    transposed = (((1,), (1,)), ((), ()))
    middle = gate.shape[0] // 2
    acts = []
    for half in range(2):
        for copy in copies[half] + copies[2 + half]:
            copy.wait()
        at = slice(half * middle, (half + 1) * middle)
        gated = lax.dot_general(
            tokens[...], gate[at, :], transposed, preferred_element_type=jnp.float32
        )
        raised = lax.dot_general(
            tokens[...], up[at, :], transposed, preferred_element_type=jnp.float32
        )
        acts.append((gated / (1.0 + jnp.exp(-gated)) * raised).astype(jnp.bfloat16))
    for copy in copies[4] + copies[5]:
        copy.wait()
    made = jnp.dot(acts[0], down[:middle, :], preferred_element_type=jnp.float32) + jnp.dot(
        acts[1], down[middle:, :], preferred_element_type=jnp.float32
    )
    for block in range(blocks):
        rows[pl.ds(block, count, stride=blocks), :] = made[:, block * LANES : (block + 1) * LANES]
    out[...] = rows[...].astype(jnp.bfloat16)


def experts(arrived, weights):
    features = weights[0][0][0].shape[1]
    count = arrived.shape[0] * arrived.shape[1] // features
    pieces = [[[piece.shape[0] for piece in half] for half in matrix] for matrix in weights]
    units = sum(sum(half) for half in pieces[0])
    flat = [piece for matrix in weights for half in matrix for piece in half]
    vmem = pl.BlockSpec(memory_space=pltpu.VMEM)
    return pl.pallas_call(
        functools.partial(experts_kernel, pieces),
        out_shape=jax.ShapeDtypeStruct(arrived.shape, jnp.bfloat16),
        in_specs=[vmem] + [pl.BlockSpec(memory_space=pl.ANY)] * len(flat),
        out_specs=vmem,
        scratch_shapes=[pltpu.VMEM((units, features), jnp.bfloat16)] * 3
        + [
            pltpu.VMEM(arrived.shape, jnp.float32),
            pltpu.VMEM((count, features), jnp.bfloat16),
            pltpu.SemaphoreType.DMA((len(flat),)),
        ],
        compiler_params=pltpu.CompilerParams(vmem_limit_bytes=VMEM_BYTES),
        cost_estimate=pl.CostEstimate(
            flops=6 * count * features * units,
            bytes_accessed=6 * units * features,
            transcendentals=count * units,
        ),
        name="experts",
    )(arrived, *flat)


def combine_kernel(returned, hidden, chosen_column, chosen_row, weight, out, rows, outputs):
    tokens, features = hidden.shape
    count = outputs.shape[0]
    blocks = features // LANES
    rows[...] = returned[...].astype(jnp.float32)
    for block in range(blocks):
        outputs[:, block * LANES : (block + 1) * LANES] = rows[
            pl.ds(block, count, stride=blocks), :
        ].astype(jnp.bfloat16)
    earlier = lax.broadcasted_iota(jnp.int32, (tokens, tokens), 1) < lax.broadcasted_iota(
        jnp.int32, (tokens, tokens), 0
    )
    same = (chosen_column[...] == chosen_row[...]) & earlier
    rank = jnp.sum(jnp.where(same, 1.0, 0.0), axis=1, keepdims=True)
    slot = slots(chosen_column[...], rank)
    pick = jnp.where(lax.broadcasted_iota(jnp.int32, (tokens, count), 1) == slot, 1.0, 0.0)
    picked = jnp.dot(pick.astype(jnp.bfloat16), outputs[...], preferred_element_type=jnp.float32)
    out[...] = (hidden[...].astype(jnp.float32) + weight[...] * picked).astype(jnp.bfloat16)


def combine(returned, hidden, chosen, weight):
    tokens, features = hidden.shape
    count = 64 * MOST
    vmem = pl.BlockSpec(memory_space=pltpu.VMEM)
    return pl.pallas_call(
        combine_kernel,
        out_shape=jax.ShapeDtypeStruct(hidden.shape, jnp.bfloat16),
        in_specs=[vmem] * 5,
        out_specs=vmem,
        scratch_shapes=[
            pltpu.VMEM(returned.shape, jnp.float32),
            pltpu.VMEM((count, features), jnp.bfloat16),
        ],
        compiler_params=pltpu.CompilerParams(vmem_limit_bytes=VMEM_BYTES),
        name="combine",
    )(returned, hidden, chosen, chosen.reshape(1, tokens), weight)


def gathered(matrix, which):
    moved = lax.ppermute(matrix, ("x", "p"), spread_pairs())
    own = lax.ppermute(moved, ("x", "p"), lift_pairs())
    left = lax.ppermute(own, "x", ring(1))
    right = lax.ppermute(own, "x", ring(-1))
    if which == 0:
        far = [lax.ppermute(left, "x", ring(1))]
    elif which == 1:
        far = [lax.ppermute(right, "x", ring(-1))]
    else:
        cut = 96
        far = [lax.ppermute(left[:cut], "x", ring(1)), lax.ppermute(right[cut:], "x", ring(-1))]
    other = lambda piece: lax.ppermute(piece, "c", [(0, 1), (1, 0)])
    first, second = [own, left], [right, *far]
    return [first + [other(piece) for piece in first], second + [other(piece) for piece in second]]


def passed_along(block, by):
    return lax.ppermute(block, ("x", "y"), [(i, (i + by) % 16) for i in range(16)])


def per_device(
    queries,
    key_value,
    memory,
    memory_source,
    routing,
    router_weight,
    norm_gain,
    gate_matrix,
    up_matrix,
    down_matrix,
):
    features = queries.shape[1]
    kept = [memory[0, :, 0], memory[0, :, 1]]
    near = [passed_along(block, 1) for block in kept]
    far = [passed_along(block, 2) for block in kept]
    weights = [
        gathered(matrix, which)
        for which, matrix in enumerate((gate_matrix.T, up_matrix.T, down_matrix))
    ]
    own = [key_value[:, 0], key_value[:, 1]]
    hidden, packed = attend(
        memory_source, queries, own, near, far, routing, norm_gain.reshape(1, features)
    )
    chunks = packed.reshape(64, -1, LANES)
    arrived = lax.all_to_all(chunks, ("y", "s", "p"), 0, 0, tiled=True)
    made = experts(arrived.reshape(packed.shape), weights)
    returned = lax.all_to_all(made.reshape(chunks.shape), ("y", "s", "p"), 0, 0, tiled=True)
    return combine(returned.reshape(packed.shape), hidden, routing, router_weight)


def solution(mesh):
    every = ("x", "y", "s", "p", "c")
    fine = Mesh(np.asarray(mesh.devices).reshape(4, 4, 4, 4, 2), every)
    return jax.shard_map(
        per_device,
        mesh=fine,
        in_specs=(
            P(every, None),
            P(every, None, None),
            P(every, None, None, None),
            P(every),
            P(every, None),
            P(every, None),
            P(),
            P(None, every),
            P(None, every),
            P(every, None),
        ),
        out_specs=P(every, None),
        check_vma=False,
    )
```

time: 738 us -> 286 us (0.39)
  blocking collectives: 621 us -> 0 us
  starting transfers between devices: 14.5 us -> 176 us
  waiting for transfers between devices: 51.4 us -> 74.3 us
  Pallas kernels: 0 us -> 21.8 us
  matrix products: 19.5 us -> 0 us
  local copies, waits for them, and re-layouts: 22.5 us -> 10.6 us
    all_to_all x3 -> x0, blocking collectives: 621 us -> none  [the longest x1 296 us: per_device(): lax.all_to_all(copies, 'expert', split_axis=0, concat_axis=0, tiled=True)]
    ppermute x2 -> x33, starting transfers between devices: 8.28 us -> 118 us  [the longest x3 41.2 us: gathered(): own = lax.ppermute(moved, ('x', 'p'), lift_pairs())]
    all_to_all x1 -> x2, starting transfers between devices: 6.27 us -> 58.2 us  [the longest x1 43.3 us: per_device(): arrived = lax.all_to_all(chunks, ('y', 's', 'p'), 0, 0, tiled=True)]
    all_to_all x1 -> x2, waiting for transfers between devices: 15.2 us -> 43.1 us  [the longest x1 43.1 us: per_device(): lax.all_to_all(made.reshape(chunks.shape), ('y', 's', 'p'), 0, 0, tiled=T...]
    pallas_call x0 -> x3, Pallas kernels: none -> 21.8 us  [the longest x1 10.3 us: experts(): pl.pallas_call(functools.partial(experts_kernel, pieces), out_shape=jax.S...]
    dot_general x3 -> x0, matrix products: 16.3 us -> none  [the longest x1 10.9 us: expert_dense(): jnp.dot(activation, down_matrix, preferred_element_type=jnp.float32)]
    ppermute x2 -> x33, waiting for transfers between devices: 36.2 us -> 31.3 us  [the longest x3 12.1 us: gathered(): right = lax.ppermute(own, 'x', ring(-1))]
  transfers between devices with their start and end apart: 3 -> 35, of which waited for: 2 -> 8; matrix products, arithmetic and copies ran while one was open for 1% -> 3% of each run, Pallas kernels for 0% -> 3%
where the time goes in v1:
time: 286 us; the launch traced here: 284 us
  starting transfers between devices  176 us (62%)
  waiting for transfers between devices  74.3 us (26%)
  Pallas kernels  21.8 us (8%)
  local copies, waits for them, and re-layouts  10.6 us (4%)
    all_to_all x1, starting transfers between devices, per_device(): arrived = lax.all_to_all(chunks, ('y', 's', 'p'), 0, 0, tiled=True)  43.3 us
    all_to_all x1, waiting for transfers between devices, per_device(): lax.all_to_all(made.reshape(chunks.shape), ('y', 's', 'p'), 0, 0, tiled=T...  43.1 us
    ppermute x3, starting transfers between devices, gathered(): own = lax.ppermute(moved, ('x', 'p'), lift_pairs())  41.2 us
    ppermute x13, starting transfers between devices, gathered(): other = lambda piece: lax.ppermute(piece, 'c', [(0, 1), (1, 0)])  26.8 us
    all_to_all x1, starting transfers between devices, per_device(): lax.all_to_all(made.reshape(chunks.shape), ('y', 's', 'p'), 0, 0, tiled=T...  14.9 us
    ppermute x4, starting transfers between devices, passed_along(): lax.ppermute(block, ('x', 'y'), [(i, (i + by) % 16) for i in range(16)])  14.1 us
    ppermute x3, waiting for transfers between devices, gathered(): right = lax.ppermute(own, 'x', ring(-1))  12.1 us
    pallas_call x1, Pallas kernels, experts(): pl.pallas_call(functools.partial(experts_kernel, pieces), out_shape=jax.S...  10.3 us
  transfers between devices with their start and end apart: 35, of which 8 were waited for; matrix products, arithmetic and copies ran while one was open for 3% of the time, Pallas kernels for 3%

profile of v1, /device:TPU:6, one launch (start us, length us, event | category | flops | bytes accessed | tf_op | source)
XLA Modules:
  0.0 284.5 jit_solution(13851484173889303341)
XLA Ops:
  3.5 3.3 %fusion = (bf16[1,128,1,2048]{3,2,1,0:T(2,128)(2,1)S(1)}, bf16[1,128,1,2048]{3,2,1,0:T(2,128)(2,1)S(1)}) fusion(bf16[1,128,2,2048]{3,2,1,0:T(2,128)(2,1)} %param.12), kind=kLoop, calls=%fused_computation.4 | loop fusion | bytes 2097152 | tf_op jit(solution)/shard_map/slice | solution.py:315
  7.2 3.6 %collective-permute-start = (bf16[128,2048]{1,0:T(8,128)(2,1)S(1)}, bf16[128,2048]{1,0:T(8,128)(2,1)S(1)}, u32[]{:S(2)}, u32[]{:S(2)}) collective-permute-start(bf16[128,2048]{1,0:T(8,128)(2,1)S(1)} %bitcast.25), channel_id=1, source_target_pairs={{0,32},{32,64},{64,96},{96,128},{128,160},{160,192},{192,224},{224... | collective-permute-start | bytes 1572872 | tf_op jit(solution)/shard_map/ppermute | solution.py:299
  11.9 3.5 %collective-permute-start.1 = (bf16[128,2048]{1,0:T(8,128)(2,1)}, bf16[128,2048]{1,0:T(8,128)(2,1)S(1)}, u32[]{:S(2)}, u32[]{:S(2)}) collective-permute-start(bf16[128,2048]{1,0:T(8,128)(2,1)} %bitcast.16), channel_id=1, source_target_pairs={{0,32},{32,64},{64,96},{96,128},{128,160},{160,192},{192,224},{224... | collective-permute-start | bytes 1572872 | tf_op jit(solution)/shard_map/ppermute | solution.py:299
  17.0 11.9 %collective-permute-start.5 = (bf16[176,2048]{1,0:T(8,128)(2,1)S(1)}, bf16[176,2048]{1,0:T(8,128)(2,1)S(1)}, u32[]{:S(2)}, u32[]{:S(2)}) collective-permute-start(bf16[176,2048]{1,0:T(8,128)(2,1)S(1)} %collective-permute-done.4), channel_id=1, source_target_pairs={{0,0},{2,4},{4,2},{6,6},{128,130},{130,134},{132,128},{134,132},{2... | collective-permute-start | bytes 2162696 | tf_op jit(solution)/shard_map/ppermute | solution.py:283
  28.9 15.4 %collective-permute-start.14 = (bf16[176,2048]{1,0:T(8,128)(2,1)S(1)}, bf16[176,2048]{1,0:T(8,128)(2,1)S(1)}, u32[]{:S(2)}, u32[]{:S(2)}) collective-permute-start(bf16[176,2048]{1,0:T(8,128)(2,1)S(1)} %collective-permute-done.13), channel_id=1, source_target_pairs={{0,0},{2,4},{4,2},{6,6},{128,130},{130,134},{132,128},{134,132},{2... | collective-permute-start | bytes 2162696 | tf_op jit(solution)/shard_map/ppermute | solution.py:283
  44.3 5.1 %collective-permute-start.2 = (bf16[128,2048]{1,0:T(8,128)(2,1)S(1)}, bf16[128,2048]{1,0:T(8,128)(2,1)}, u32[]{:S(2)}, u32[]{:S(2)}) collective-permute-start(bf16[128,2048]{1,0:T(8,128)(2,1)S(1)} %bitcast.26), channel_id=1, source_target_pairs={{0,64},{32,96},{64,128},{96,160},{128,192},{160,224},{192,256},{22... | collective-permute-start | bytes 1572872 | tf_op jit(solution)/shard_map/ppermute | solution.py:299
  53.7 13.9 %collective-permute-start.23 = (bf16[176,2048]{1,0:T(8,128)(2,1)}, bf16[176,2048]{1,0:T(8,128)(2,1)}, u32[]{:S(2)}, u32[]{:S(2)}) collective-permute-start(bf16[176,2048]{1,0:T(8,128)(2,1)} %collective-permute-done.22), channel_id=1, source_target_pairs={{0,0},{2,4},{4,2},{6,6},{128,130},{130,134},{132,128},{134,132},{2... | collective-permute-start | bytes 2162696 | tf_op jit(solution)/shard_map/ppermute | solution.py:283
  69.6 3.9 %collective-permute-start.18 = (bf16[176,2048]{1,0:T(8,128)(2,1)S(1)}, bf16[176,2048]{1,0:T(8,128)(2,1)}, u32[]{:S(2)}, u32[]{:S(2)}) collective-permute-start(bf16[176,2048]{1,0:T(8,128)(2,1)S(1)} %collective-permute-done.14.refs_8_), channel_id=1, source_target_pairs={{0,384},{128,0},{256,128},{384,256},{1,385},{129,1},{257,129},{385... | collective-permute-start | bytes 2162696 | tf_op jit(solution)/shard_map/ppermute | solution.py:285
  75.8 9.6 %attend.1 = (bf16[128,2048]{1,0:T(8,128)(2,1)S(1)}, bf16[3072,128]{1,0:T(8,128)(2,1)}) custom-call(s32[1]{0:T(128)S(6)} %copy.28.source, bf16[128,2048]{1,0:T(8,128)(2,1)S(1)} %copy-done, bf16[128,2048]{1,0:T(8,128)(2,1)S(1)} %get-tuple-element.14.own_keys, bf16[128,2048]{1,0:T(8,128)(2,1)} %get-tuple-element.13.own_values, bf16[128,2048]{1,0:T(8,128)(2,1)} %copy-done.23, ...), custom_call_target="tpu_custom_call" | custom-call | flops 268435456 | bytes 2621440 | tf_op jit(solution)/shard_map/attend/pallas_call | solution.py:136
  85.4 43.3 %all-to-all-start = ((bf16[64,48,128]{2,1,0:T(8,128)(2,1)}), bf16[64,48,128]{2,1,0:T(8,128)(2,1)S(1)}, u32[]{:S(2)}, u32[]{:S(2)}) async-start(bf16[64,48,128]{2,1,0:T(8,128)(2,1)} %bitcast.24), calls=%async_computation | async-start | bytes 1572864 | tf_op jit(solution)/shard_map/all_to_all | solution.py:327
  128.8 3.1 %collective-permute-start.24 = (bf16[176,2048]{1,0:T(8,128)(2,1)}, bf16[176,2048]{1,0:T(8,128)(2,1)S(1)}, u32[]{:S(2)}, u32[]{:S(2)}) collective-permute-start(bf16[176,2048]{1,0:T(8,128)(2,1)} %collective-permute-done.23.refs_16_), channel_id=1, source_target_pairs={{0,128},{128,256},{256,384},{384,0},{1,129},{129,257},{257,385},{3... | collective-permute-start | bytes 2162696 | tf_op jit(solution)/shard_map/ppermute | solution.py:284
  131.9 2.7 collective-permute-start.27
  134.6 3.3 %collective-permute-start.9 = (bf16[176,2048]{1,0:T(8,128)(2,1)S(1)}, bf16[176,2048]{1,0:T(8,128)(2,1)S(1)}, u32[]{:S(2)}, u32[]{:S(2)}) collective-permute-start(bf16[176,2048]{1,0:T(8,128)(2,1)S(1)} %collective-permute-done.5.refs_0_), channel_id=1, source_target_pairs={{0,384},{128,0},{256,128},{384,256},{1,385},{129,1},{257,129},{385... | collective-permute-start | bytes 2162696 | tf_op jit(solution)/shard_map/ppermute | solution.py:285
  137.9 3.8 %collective-permute-start.15 = (bf16[176,2048]{1,0:T(8,128)(2,1)S(1)}, bf16[176,2048]{1,0:T(8,128)(2,1)S(1)}, u32[]{:S(2)}, u32[]{:S(2)}) collective-permute-start(bf16[176,2048]{1,0:T(8,128)(2,1)S(1)} %collective-permute-done.14.refs_8_), channel_id=1, source_target_pairs={{0,128},{128,256},{256,384},{384,0},{1,129},{129,257},{257,385},{3... | collective-permute-start | bytes 2162696 | tf_op jit(solution)/shard_map/ppermute | solution.py:284
  143.7 6.3 %collective-permute-done.24.refs_17_ = bf16[176,2048]{1,0:T(8,128)(2,1)S(1)} collective-permute-done((bf16[176,2048]{1,0:T(8,128)(2,1)}, bf16[176,2048]{1,0:T(8,128)(2,1)S(1)}, u32[]{:S(2)}, u32[]{:S(2)}) %collective-permute-start.24) | collective-permute-done | bytes 720928 | tf_op jit(solution)/shard_map/ppermute | solution.py:284
  151.9 2.4 collective-permute-done.27.refs_20_
  156.3 9.7 %collective-permute-done.9.refs_4_ = bf16[176,2048]{1,0:T(8,128)(2,1)S(1)} collective-permute-done((bf16[176,2048]{1,0:T(8,128)(2,1)S(1)}, bf16[176,2048]{1,0:T(8,128)(2,1)S(1)}, u32[]{:S(2)}, u32[]{:S(2)}) %collective-permute-start.9) | collective-permute-done | bytes 720928 | tf_op jit(solution)/shard_map/ppermute | solution.py:285
  166.0 2.9 %collective-permute-start.29 = (bf16[80,2048]{1,0:T(8,128)(2,1)S(1)}, bf16[80,2048]{1,0:T(8,128)(2,1)S(1)}, u32[]{:S(2)}, u32[]{:S(2)}) collective-permute-start(bf16[80,2048]{1,0:T(8,128)(2,1)S(1)} %slice.25), channel_id=1, source_target_pairs={{0,384},{128,0},{256,128},{384,256},{1,385},{129,1},{257,129},{385... | collective-permute-start | bytes 983048 | tf_op jit(solution)/shard_map/ppermute | solution.py:292
  168.9 4.2 %collective-permute-start.28 = (bf16[96,2048]{1,0:T(8,128)(2,1)S(1)}, bf16[96,2048]{1,0:T(8,128)(2,1)S(1)}, u32[]{:S(2)}, u32[]{:S(2)}) collective-permute-start(bf16[96,2048]{1,0:T(8,128)(2,1)S(1)} %slice.24), channel_id=1, source_target_pairs={{0,128},{128,256},{256,384},{384,0},{1,129},{129,257},{257,385},{3... | collective-permute-start | bytes 1179656 | tf_op jit(solution)/shard_map/ppermute | solution.py:292
  173.1 2.3 collective-permute-start.10
  178.1 2.8 collective-permute-start.19
  180.9 2.1 collective-permute-start.20
  183.1 2.2 collective-permute-start.26
  185.3 2.1 collective-permute-start.30
  187.5 7.6 %collective-permute-done.10.refs_5_ = bf16[176,2048]{1,0:T(8,128)(2,1)S(1)} collective-permute-done((bf16[176,2048]{1,0:T(8,128)(2,1)}, bf16[176,2048]{1,0:T(8,128)(2,1)S(1)}, u32[]{:S(2)}, u32[]{:S(2)}) %collective-permute-start.10) | collective-permute-done | bytes 720928 | tf_op jit(solution)/shard_map/ppermute | solution.py:287
  197.0 3.0 %collective-permute-done.19.refs_13_ = bf16[176,2048]{1,0:T(8,128)(2,1)S(1)} collective-permute-done((bf16[176,2048]{1,0:T(8,128)(2,1)}, bf16[176,2048]{1,0:T(8,128)(2,1)S(1)}, u32[]{:S(2)}, u32[]{:S(2)}) %collective-permute-start.19) | collective-permute-done | bytes 720928 | tf_op jit(solution)/shard_map/ppermute | solution.py:289
  201.9 2.4 collective-permute-start.17
  206.3 2.4 collective-permute-start.21
  208.7 2.1 collective-permute-start.31
  214.2 10.3 %experts.1 = bf16[3072,128]{1,0:T(8,128)(2,1)} custom-call(bf16[3072,128]{1,0:T(8,128)(2,1)} %bitcast.22, bf16[176,2048]{1,0:T(8,128)(2,1)} %copy-done.7, bf16[176,2048]{1,0:T(8,128)(2,1)} %collective-permute-done.6.refs_1_, bf16[176,2048]{1,0:T(8,128)(2,1)} %copy-done.13, bf16[176,2048]{1,0:T(8,128)(2,1)} %copy-done.19, bf16[176,2048]{1,0:T(8,128)(2,1)} %copy-done.9, ...), custom_call_target="tpu_custom_call" | custom-call | flops 3321888768 | bytes 17301504 | tf_op jit(solution)/shard_map/experts/pallas_call | solution.py:222
  224.5 14.9 %all-to-all-start.1 = ((bf16[64,48,128]{2,1,0:T(8,128)(2,1)}), bf16[64,48,128]{2,1,0:T(8,128)(2,1)S(1)}, u32[]{:S(2)}, u32[]{:S(2)}) async-start(bf16[64,48,128]{2,1,0:T(8,128)(2,1)} %bitcast.23), calls=%async_computation.1 | async-start | bytes 1572864 | tf_op jit(solution)/shard_map/all_to_all | solution.py:329
  239.5 43.1 %all-to-all-done.1 = bf16[64,48,128]{2,1,0:T(8,128)(2,1)S(1)} async-done(((bf16[64,48,128]{2,1,0:T(8,128)(2,1)}), bf16[64,48,128]{2,1,0:T(8,128)(2,1)S(1)}, u32[]{:S(2)}, u32[]{:S(2)}) %all-to-all-start.1) | async-done | bytes 786464 | tf_op jit(solution)/shard_map/all_to_all | solution.py:329
  (104 shorter events, 33.6 us)
Async XLA Ops:
  0.0 17.0 %collective-permute-start.4 = (bf16[176,2048]{1,0:T(8,128)(2,1)}, bf16[176,2048]{1,0:T(8,128)(2,1)S(1)}, u32[]{:S(2)}, u32[]{:S(2)}) collective-permute-start(bf16[176,2048]{1,0:T(8,128)(2,1)} %bitcast.27), channel_id=1, source_target_pairs={{0,0},{258,2},{132,4},{390,6},{128,128},{386,130},{4,132},{262,134... | collective-permute-start | bytes 2162696 | tf_op jit(solution)/shard_map/ppermute | solution.py:282
  1.8 27.1 %collective-permute-start.13 = (bf16[176,2048]{1,0:T(8,128)(2,1)}, bf16[176,2048]{1,0:T(8,128)(2,1)S(1)}, u32[]{:S(2)}, u32[]{:S(2)}) collective-permute-start(bf16[176,2048]{1,0:T(8,128)(2,1)} %bitcast.28), channel_id=1, source_target_pairs={{0,0},{258,2},{132,4},{390,6},{128,128},{386,130},{4,132},{262,134... | collective-permute-start | bytes 2162696 | tf_op jit(solution)/shard_map/ppermute | solution.py:282
  7.2 37.1 %collective-permute-start = (bf16[128,2048]{1,0:T(8,128)(2,1)S(1)}, bf16[128,2048]{1,0:T(8,128)(2,1)S(1)}, u32[]{:S(2)}, u32[]{:S(2)}) collective-permute-start(bf16[128,2048]{1,0:T(8,128)(2,1)S(1)} %bitcast.25), channel_id=1, source_target_pairs={{0,32},{32,64},{64,96},{96,128},{128,160},{160,192},{192,224},{224... | collective-permute-start | bytes 1572872 | tf_op jit(solution)/shard_map/ppermute | solution.py:299
  11.9 37.5 %collective-permute-start.1 = (bf16[128,2048]{1,0:T(8,128)(2,1)}, bf16[128,2048]{1,0:T(8,128)(2,1)S(1)}, u32[]{:S(2)}, u32[]{:S(2)}) collective-permute-start(bf16[128,2048]{1,0:T(8,128)(2,1)} %bitcast.16), channel_id=1, source_target_pairs={{0,32},{32,64},{64,96},{96,128},{128,160},{160,192},{192,224},{224... | collective-permute-start | bytes 1572872 | tf_op jit(solution)/shard_map/ppermute | solution.py:299
  15.4 38.3 %collective-permute-start.22 = (bf16[176,2048]{1,0:T(8,128)(2,1)S(1)}, bf16[176,2048]{1,0:T(8,128)(2,1)}, u32[]{:S(2)}, u32[]{:S(2)}) collective-permute-start(bf16[176,2048]{1,0:T(8,128)(2,1)S(1)} %copy-done.26), channel_id=1, source_target_pairs={{0,0},{258,2},{132,4},{390,6},{128,128},{386,130},{4,132},{262,134... | collective-permute-start | bytes 2162696 | tf_op jit(solution)/shard_map/ppermute | solution.py:282
  17.0 50.7 %collective-permute-start.5 = (bf16[176,2048]{1,0:T(8,128)(2,1)S(1)}, bf16[176,2048]{1,0:T(8,128)(2,1)S(1)}, u32[]{:S(2)}, u32[]{:S(2)}) collective-permute-start(bf16[176,2048]{1,0:T(8,128)(2,1)S(1)} %collective-permute-done.4), channel_id=1, source_target_pairs={{0,0},{2,4},{4,2},{6,6},{128,130},{130,134},{132,128},{134,132},{2... | collective-permute-start | bytes 2162696 | tf_op jit(solution)/shard_map/ppermute | solution.py:283
  28.9 40.7 %collective-permute-start.14 = (bf16[176,2048]{1,0:T(8,128)(2,1)S(1)}, bf16[176,2048]{1,0:T(8,128)(2,1)S(1)}, u32[]{:S(2)}, u32[]{:S(2)}) collective-permute-start(bf16[176,2048]{1,0:T(8,128)(2,1)S(1)} %collective-permute-done.13), channel_id=1, source_target_pairs={{0,0},{2,4},{4,2},{6,6},{128,130},{130,134},{132,128},{134,132},{2... | collective-permute-start | bytes 2162696 | tf_op jit(solution)/shard_map/ppermute | solution.py:283
  44.3 31.4 %collective-permute-start.2 = (bf16[128,2048]{1,0:T(8,128)(2,1)S(1)}, bf16[128,2048]{1,0:T(8,128)(2,1)}, u32[]{:S(2)}, u32[]{:S(2)}) collective-permute-start(bf16[128,2048]{1,0:T(8,128)(2,1)S(1)} %bitcast.26), channel_id=1, source_target_pairs={{0,64},{32,96},{64,128},{96,160},{128,192},{160,224},{192,256},{22... | collective-permute-start | bytes 1572872 | tf_op jit(solution)/shard_map/ppermute | solution.py:299
  50.3 25.5 %collective-permute-start.3 = (bf16[128,2048]{1,0:T(8,128)(2,1)}, bf16[128,2048]{1,0:T(8,128)(2,1)}, u32[]{:S(2)}, u32[]{:S(2)}) collective-permute-start(bf16[128,2048]{1,0:T(8,128)(2,1)} %bitcast.16), channel_id=1, source_target_pairs={{0,64},{32,96},{64,128},{96,160},{128,192},{160,224},{192,256},{22... | collective-permute-start | bytes 1572872 | tf_op jit(solution)/shard_map/ppermute | solution.py:299
  53.7 75.1 %collective-permute-start.23 = (bf16[176,2048]{1,0:T(8,128)(2,1)}, bf16[176,2048]{1,0:T(8,128)(2,1)}, u32[]{:S(2)}, u32[]{:S(2)}) collective-permute-start(bf16[176,2048]{1,0:T(8,128)(2,1)} %collective-permute-done.22), channel_id=1, source_target_pairs={{0,0},{2,4},{4,2},{6,6},{128,130},{130,134},{132,128},{134,132},{2... | collective-permute-start | bytes 2162696 | tf_op jit(solution)/shard_map/ppermute | solution.py:283
  67.7 70.3 %collective-permute-start.6 = (bf16[176,2048]{1,0:T(8,128)(2,1)S(1)}, bf16[176,2048]{1,0:T(8,128)(2,1)}, u32[]{:S(2)}, u32[]{:S(2)}) collective-permute-start(bf16[176,2048]{1,0:T(8,128)(2,1)S(1)} %collective-permute-done.5.refs_0_), channel_id=1, source_target_pairs={{0,128},{128,256},{256,384},{384,0},{1,129},{129,257},{257,385},{3... | collective-permute-start | bytes 2162696 | tf_op jit(solution)/shard_map/ppermute | solution.py:284
  69.6 72.1 %collective-permute-start.18 = (bf16[176,2048]{1,0:T(8,128)(2,1)S(1)}, bf16[176,2048]{1,0:T(8,128)(2,1)}, u32[]{:S(2)}, u32[]{:S(2)}) collective-permute-start(bf16[176,2048]{1,0:T(8,128)(2,1)S(1)} %collective-permute-done.14.refs_8_), channel_id=1, source_target_pairs={{0,384},{128,0},{256,128},{384,256},{1,385},{129,1},{257,129},{385... | collective-permute-start | bytes 2162696 | tf_op jit(solution)/shard_map/ppermute | solution.py:285
  85.4 127.9 %all-to-all-start = ((bf16[64,48,128]{2,1,0:T(8,128)(2,1)}), bf16[64,48,128]{2,1,0:T(8,128)(2,1)S(1)}, u32[]{:S(2)}, u32[]{:S(2)}) async-start(bf16[64,48,128]{2,1,0:T(8,128)(2,1)} %bitcast.24), calls=%async_computation | async-start | bytes 1572864 | tf_op jit(solution)/shard_map/all_to_all | solution.py:327
  128.8 21.2 %collective-permute-start.24 = (bf16[176,2048]{1,0:T(8,128)(2,1)}, bf16[176,2048]{1,0:T(8,128)(2,1)S(1)}, u32[]{:S(2)}, u32[]{:S(2)}) collective-permute-start(bf16[176,2048]{1,0:T(8,128)(2,1)} %collective-permute-done.23.refs_16_), channel_id=1, source_target_pairs={{0,128},{128,256},{256,384},{384,0},{1,129},{129,257},{257,385},{3... | collective-permute-start | bytes 2162696 | tf_op jit(solution)/shard_map/ppermute | solution.py:284
  131.9 22.4 %collective-permute-start.27 = (bf16[176,2048]{1,0:T(8,128)(2,1)}, bf16[176,2048]{1,0:T(8,128)(2,1)S(1)}, u32[]{:S(2)}, u32[]{:S(2)}) collective-permute-start(bf16[176,2048]{1,0:T(8,128)(2,1)} %collective-permute-done.23.refs_16_), channel_id=1, source_target_pairs={{0,384},{128,0},{256,128},{384,256},{1,385},{129,1},{257,129},{385... | collective-permute-start | bytes 2162696 | tf_op jit(solution)/shard_map/ppermute | solution.py:285
  134.6 31.3 %collective-permute-start.9 = (bf16[176,2048]{1,0:T(8,128)(2,1)S(1)}, bf16[176,2048]{1,0:T(8,128)(2,1)S(1)}, u32[]{:S(2)}, u32[]{:S(2)}) collective-permute-start(bf16[176,2048]{1,0:T(8,128)(2,1)S(1)} %collective-permute-done.5.refs_0_), channel_id=1, source_target_pairs={{0,384},{128,0},{256,128},{384,256},{1,385},{129,1},{257,129},{385... | collective-permute-start | bytes 2162696 | tf_op jit(solution)/shard_map/ppermute | solution.py:285
  137.9 31.0 %collective-permute-start.15 = (bf16[176,2048]{1,0:T(8,128)(2,1)S(1)}, bf16[176,2048]{1,0:T(8,128)(2,1)S(1)}, u32[]{:S(2)}, u32[]{:S(2)}) collective-permute-start(bf16[176,2048]{1,0:T(8,128)(2,1)S(1)} %collective-permute-done.14.refs_8_), channel_id=1, source_target_pairs={{0,128},{128,256},{256,384},{384,0},{1,129},{129,257},{257,385},{3... | collective-permute-start | bytes 2162696 | tf_op jit(solution)/shard_map/ppermute | solution.py:284
  141.7 31.3 %collective-permute-start.16 = (bf16[176,2048]{1,0:T(8,128)(2,1)S(1)}, bf16[176,2048]{1,0:T(8,128)(2,1)S(1)}, u32[]{:S(2)}, u32[]{:S(2)}) collective-permute-start(bf16[176,2048]{1,0:T(8,128)(2,1)S(1)} %collective-permute-done.14.refs_8_), channel_id=1, source_target_pairs={{0,1},{1,0},{2,3},{3,2},{4,5},{5,4},{6,7},{7,6},{8,9},{9,8},{10,11... | collective-permute-start | bytes 2162696 | tf_op jit(solution)/shard_map/ppermute | solution.py:293
  150.0 28.1 %collective-permute-start.25 = (bf16[176,2048]{1,0:T(8,128)(2,1)}, bf16[176,2048]{1,0:T(8,128)(2,1)S(1)}, u32[]{:S(2)}, u32[]{:S(2)}) collective-permute-start(bf16[176,2048]{1,0:T(8,128)(2,1)} %collective-permute-done.23.refs_16_), channel_id=1, source_target_pairs={{0,1},{1,0},{2,3},{3,2},{4,5},{5,4},{6,7},{7,6},{8,9},{9,8},{10,11... | collective-permute-start | bytes 2162696 | tf_op jit(solution)/shard_map/ppermute | solution.py:293
  154.3 26.6 %collective-permute-start.7 = (bf16[176,2048]{1,0:T(8,128)(2,1)S(1)}, bf16[176,2048]{1,0:T(8,128)(2,1)S(1)}, u32[]{:S(2)}, u32[]{:S(2)}) collective-permute-start(bf16[176,2048]{1,0:T(8,128)(2,1)S(1)} %collective-permute-done.5.refs_0_), channel_id=1, source_target_pairs={{0,1},{1,0},{2,3},{3,2},{4,5},{5,4},{6,7},{7,6},{8,9},{9,8},{10,11... | collective-permute-start | bytes 2162696 | tf_op jit(solution)/shard_map/ppermute | solution.py:293
  166.0 10.2 %collective-permute-start.29 = (bf16[80,2048]{1,0:T(8,128)(2,1)S(1)}, bf16[80,2048]{1,0:T(8,128)(2,1)S(1)}, u32[]{:S(2)}, u32[]{:S(2)}) collective-permute-start(bf16[80,2048]{1,0:T(8,128)(2,1)S(1)} %slice.25), channel_id=1, source_target_pairs={{0,384},{128,0},{256,128},{384,256},{1,385},{129,1},{257,129},{385... | collective-permute-start | bytes 983048 | tf_op jit(solution)/shard_map/ppermute | solution.py:292
  168.9 14.2 %collective-permute-start.28 = (bf16[96,2048]{1,0:T(8,128)(2,1)S(1)}, bf16[96,2048]{1,0:T(8,128)(2,1)S(1)}, u32[]{:S(2)}, u32[]{:S(2)}) collective-permute-start(bf16[96,2048]{1,0:T(8,128)(2,1)S(1)} %slice.24), channel_id=1, source_target_pairs={{0,128},{128,256},{256,384},{384,0},{1,129},{129,257},{257,385},{3... | collective-permute-start | bytes 1179656 | tf_op jit(solution)/shard_map/ppermute | solution.py:292
  173.1 22.0 %collective-permute-start.10 = (bf16[176,2048]{1,0:T(8,128)(2,1)}, bf16[176,2048]{1,0:T(8,128)(2,1)S(1)}, u32[]{:S(2)}, u32[]{:S(2)}) collective-permute-start(bf16[176,2048]{1,0:T(8,128)(2,1)} %collective-permute-done.6.refs_1_), channel_id=1, source_target_pairs={{0,128},{128,256},{256,384},{384,0},{1,129},{129,257},{257,385},{3... | collective-permute-start | bytes 2162696 | tf_op jit(solution)/shard_map/ppermute | solution.py:287
  176.1 9.2 %collective-permute-start.32 = (bf16[80,2048]{1,0:T(8,128)(2,1)S(1)}, bf16[80,2048]{1,0:T(8,128)(2,1)S(1)}, u32[]{:S(2)}, u32[]{:S(2)}) collective-permute-start(bf16[80,2048]{1,0:T(8,128)(2,1)S(1)} %collective-permute-done.29.refs_22_), channel_id=1, source_target_pairs={{0,1},{1,0},{2,3},{3,2},{4,5},{5,4},{6,7},{7,6},{8,9},{9,8},{10,11... | collective-permute-start | bytes 983048 | tf_op jit(solution)/shard_map/ppermute | solution.py:293
  178.1 21.9 %collective-permute-start.19 = (bf16[176,2048]{1,0:T(8,128)(2,1)}, bf16[176,2048]{1,0:T(8,128)(2,1)S(1)}, u32[]{:S(2)}, u32[]{:S(2)}) collective-permute-start(bf16[176,2048]{1,0:T(8,128)(2,1)} %collective-permute-done.18.refs_12_), channel_id=1, source_target_pairs={{0,384},{128,0},{256,128},{384,256},{1,385},{129,1},{257,129},{385... | collective-permute-start | bytes 2162696 | tf_op jit(solution)/shard_map/ppermute | solution.py:289
  180.9 20.9 %collective-permute-start.20 = (bf16[176,2048]{1,0:T(8,128)(2,1)}, bf16[176,2048]{1,0:T(8,128)(2,1)S(1)}, u32[]{:S(2)}, u32[]{:S(2)}) collective-permute-start(bf16[176,2048]{1,0:T(8,128)(2,1)} %collective-permute-done.18.refs_12_), channel_id=1, source_target_pairs={{0,1},{1,0},{2,3},{3,2},{4,5},{5,4},{6,7},{7,6},{8,9},{9,8},{10,11... | collective-permute-start | bytes 2162696 | tf_op jit(solution)/shard_map/ppermute | solution.py:293
  183.1 21.2 %collective-permute-start.26 = (bf16[176,2048]{1,0:T(8,128)(2,1)S(1)}, bf16[176,2048]{1,0:T(8,128)(2,1)S(1)}, u32[]{:S(2)}, u32[]{:S(2)}) collective-permute-start(bf16[176,2048]{1,0:T(8,128)(2,1)S(1)} %collective-permute-done.24.refs_17_), channel_id=1, source_target_pairs={{0,1},{1,0},{2,3},{3,2},{4,5},{5,4},{6,7},{7,6},{8,9},{9,8},{10,11... | collective-permute-start | bytes 2162696 | tf_op jit(solution)/shard_map/ppermute | solution.py:293
  185.3 20.9 %collective-permute-start.30 = (bf16[176,2048]{1,0:T(8,128)(2,1)S(1)}, bf16[176,2048]{1,0:T(8,128)(2,1)S(1)}, u32[]{:S(2)}, u32[]{:S(2)}) collective-permute-start(bf16[176,2048]{1,0:T(8,128)(2,1)S(1)} %collective-permute-done.27.refs_20_), channel_id=1, source_target_pairs={{0,1},{1,0},{2,3},{3,2},{4,5},{5,4},{6,7},{7,6},{8,9},{9,8},{10,11... | collective-permute-start | bytes 2162696 | tf_op jit(solution)/shard_map/ppermute | solution.py:293
  195.1 13.6 %collective-permute-start.8 = (bf16[176,2048]{1,0:T(8,128)(2,1)}, bf16[176,2048]{1,0:T(8,128)(2,1)S(1)}, u32[]{:S(2)}, u32[]{:S(2)}) collective-permute-start(bf16[176,2048]{1,0:T(8,128)(2,1)} %collective-permute-done.6.refs_1_), channel_id=1, source_target_pairs={{0,1},{1,0},{2,3},{3,2},{4,5},{5,4},{6,7},{7,6},{8,9},{9,8},{10,11... | collective-permute-start | bytes 2162696 | tf_op jit(solution)/shard_map/ppermute | solution.py:293
  199.9 10.9 %collective-permute-start.11 = (bf16[176,2048]{1,0:T(8,128)(2,1)S(1)}, bf16[176,2048]{1,0:T(8,128)(2,1)S(1)}, u32[]{:S(2)}, u32[]{:S(2)}) collective-permute-start(bf16[176,2048]{1,0:T(8,128)(2,1)S(1)} %collective-permute-done.9.refs_4_), channel_id=1, source_target_pairs={{0,1},{1,0},{2,3},{3,2},{4,5},{5,4},{6,7},{7,6},{8,9},{9,8},{10,11... | collective-permute-start | bytes 2162696 | tf_op jit(solution)/shard_map/ppermute | solution.py:293
  201.9 9.0 %collective-permute-start.17 = (bf16[176,2048]{1,0:T(8,128)(2,1)S(1)}, bf16[176,2048]{1,0:T(8,128)(2,1)S(1)}, u32[]{:S(2)}, u32[]{:S(2)}) collective-permute-start(bf16[176,2048]{1,0:T(8,128)(2,1)S(1)} %collective-permute-done.15.refs_9_), channel_id=1, source_target_pairs={{0,1},{1,0},{2,3},{3,2},{4,5},{5,4},{6,7},{7,6},{8,9},{9,8},{10,11... | collective-permute-start | bytes 2162696 | tf_op jit(solution)/shard_map/ppermute | solution.py:293
  224.5 58.1 %all-to-all-start.1 = ((bf16[64,48,128]{2,1,0:T(8,128)(2,1)}), bf16[64,48,128]{2,1,0:T(8,128)(2,1)S(1)}, u32[]{:S(2)}, u32[]{:S(2)}) async-start(bf16[64,48,128]{2,1,0:T(8,128)(2,1)} %bitcast.23), calls=%async_computation.1 | async-start | bytes 1572864 | tf_op jit(solution)/shard_map/all_to_all | solution.py:329
  (30 other events, 579.0 us)

commit v2 on v1

v2 whole, which is shorter than its diff:
```python
import math

import jax
import jax.numpy as jnp
import numpy as np
from jax import lax
from jax.experimental import pallas as pl
from jax.experimental.pallas import tpu as pltpu
from jax.sharding import Mesh
from jax.sharding import PartitionSpec as P

HEADS = 16
MOST = 3
LANES = 128
VMEM_BYTES = 32 * 1024 * 1024

PLACE = ((0, 2, 1, 3), (1, 3, 0, 2), (2, 0, 3, 1), (3, 1, 2, 0))


def spread_pairs():
    return [(PLACE[h][p] * 4 + p, h * 4 + p) for h in range(4) for p in range(4)]


def lift_pairs():
    return [(h * 4 + p, h * 4 + PLACE[h][p]) for h in range(4) for p in range(4)]


def ring(by):
    return [(i, (i + by) % 4) for i in range(4)]


def slots(chosen, rank):
    x = jnp.right_shift(chosen, 4)
    y = jnp.bitwise_and(jnp.right_shift(chosen, 2), 3)
    segment = jnp.bitwise_and(chosen, 3)
    return (y * 16 + segment * 4 + x) * MOST + rank.astype(jnp.int32)


def attend_kernel(
    source,
    queries,
    own,
    near,
    far_off,
    chosen_column,
    chosen_row,
    gain,
    hidden_out,
    packed_out,
    recalled,
    normed,
    rows,
    sem,
):
    tokens, features = queries.shape

    def fetch(block):
        copy = pltpu.make_async_copy(block, recalled, sem)
        copy.start()
        copy.wait()

    @pl.when(source[0] == 0)
    def _():
        fetch(near)

    @pl.when(source[0] != 0)
    def _():
        fetch(far_off)

    later = lax.broadcasted_iota(jnp.int32, (tokens, tokens), 1) > lax.broadcasted_iota(
        jnp.int32, (tokens, tokens), 0
    )
    scale = 1.0 / math.sqrt(features // HEADS)
    transposed = (((1,), (1,)), ((), ()))
    squares = jnp.zeros((tokens, LANES), jnp.float32)
    for head in range(HEADS):
        at = slice(head * LANES, (head + 1) * LANES)
        query = queries[:, at]
        far = scale * lax.dot_general(
            query, recalled[0, :, at], transposed, preferred_element_type=jnp.float32
        )
        here = scale * lax.dot_general(
            query, own[0, :, at], transposed, preferred_element_type=jnp.float32
        )
        here = jnp.where(later, -1e30, here)
        top = jnp.max(jnp.maximum(far, here), axis=1, keepdims=True)
        far = jnp.exp(far - top)
        here = jnp.exp(here - top)
        share = 1.0 / jnp.sum(far + here, axis=1, keepdims=True)
        hidden = jnp.dot(
            (far * share).astype(jnp.bfloat16),
            recalled[1, :, at],
            preferred_element_type=jnp.float32,
        ) + jnp.dot(
            (here * share).astype(jnp.bfloat16), own[1, :, at], preferred_element_type=jnp.float32
        )
        hidden = hidden.astype(jnp.bfloat16)
        hidden_out[:, at] = hidden
        wide = hidden.astype(jnp.float32)
        squares += wide * wide
    mean = jnp.sum(squares, axis=1, keepdims=True) / features
    factor = lax.rsqrt(mean + 1e-6)
    for head in range(HEADS):
        at = slice(head * LANES, (head + 1) * LANES)
        normed[:, at] = (hidden_out[:, at].astype(jnp.float32) * factor * gain[:, at]).astype(
            jnp.bfloat16
        )
    same = (chosen_column[...] == chosen_row[...]) & later
    rank = jnp.sum(jnp.where(same, 1.0, 0.0), axis=0, keepdims=True)
    slot = slots(chosen_row[...], rank)
    count = rows.shape[0] // (features // LANES)
    spread = jnp.where(lax.broadcasted_iota(jnp.int32, (count, tokens), 0) == slot, 1.0, 0.0)
    spread = spread.astype(jnp.bfloat16)
    blocks = features // LANES
    packed = jnp.dot(spread, normed[...], preferred_element_type=jnp.float32)
    for block in range(blocks):
        rows[pl.ds(block, count, stride=blocks), :] = packed[:, block * LANES : (block + 1) * LANES]
    packed_out[...] = rows[...].astype(jnp.bfloat16)


def attend(source, queries, own, near, far, chosen, gain):
    tokens, features = queries.shape
    blocks = features // LANES
    count = 64 * MOST
    vmem = pl.BlockSpec(memory_space=pltpu.VMEM)
    anywhere = pl.BlockSpec(memory_space=pl.ANY)
    return pl.pallas_call(
        attend_kernel,
        out_shape=(
            jax.ShapeDtypeStruct((tokens, features), jnp.bfloat16),
            jax.ShapeDtypeStruct((count * blocks, LANES), jnp.bfloat16),
        ),
        in_specs=[pl.BlockSpec(memory_space=pltpu.SMEM)]
        + [vmem] * 2
        + [anywhere] * 2
        + [vmem] * 3,
        out_specs=(vmem, vmem),
        scratch_shapes=[
            pltpu.VMEM((2, tokens, features), jnp.bfloat16),
            pltpu.VMEM((tokens, features), jnp.bfloat16),
            pltpu.VMEM((count * blocks, LANES), jnp.float32),
            pltpu.SemaphoreType.DMA,
        ],
        compiler_params=pltpu.CompilerParams(vmem_limit_bytes=VMEM_BYTES),
        cost_estimate=pl.CostEstimate(
            flops=4 * tokens * 2 * tokens * features,
            bytes_accessed=10 * tokens * features,
            transcendentals=2 * HEADS * tokens * tokens,
        ),
        name="attend",
    )(source, queries, own, near, far, chosen, chosen.reshape(1, tokens), gain)


def experts_kernel(arrived, *refs):
    gates, ups, downs, (out, rows, tokens) = refs[:4], refs[4:8], refs[8:13], refs[13:]
    count, features = tokens.shape
    blocks = features // LANES
    rows[...] = arrived[...].astype(jnp.float32)
    for block in range(blocks):
        tokens[:, block * LANES : (block + 1) * LANES] = rows[
            pl.ds(block, count, stride=blocks), :
        ].astype(jnp.bfloat16)
    transposed = (((1,), (1,)), ((), ()))
    acts = []
    for gate, up in zip(gates, ups):
        gated = lax.dot_general(
            tokens[...], gate[...], transposed, preferred_element_type=jnp.float32
        )
        raised = lax.dot_general(
            tokens[...], up[...], transposed, preferred_element_type=jnp.float32
        )
        acts.append((gated / (1.0 + jnp.exp(-gated)) * raised).astype(jnp.bfloat16))
    middle = features // 2
    for half in range(2):
        at = slice(half * middle, (half + 1) * middle)
        made = jnp.dot(acts[3], downs[3 + half][...], preferred_element_type=jnp.float32)
        for act, down in zip(acts[:3], downs[:3]):
            made += jnp.dot(act, down[:, at], preferred_element_type=jnp.float32)
        for block in range(blocks // 2):
            rows[pl.ds(half * (blocks // 2) + block, count, stride=blocks), :] = made[
                :, block * LANES : (block + 1) * LANES
            ]
    out[...] = rows[...].astype(jnp.bfloat16)


def experts(arrived, weights, name):
    gates, ups, downs = weights
    units, features = gates[0].shape
    count = arrived.shape[0] * arrived.shape[1] // features
    vmem = pl.BlockSpec(memory_space=pltpu.VMEM)
    return pl.pallas_call(
        experts_kernel,
        out_shape=jax.ShapeDtypeStruct(arrived.shape, jnp.bfloat16),
        in_specs=[vmem] * (1 + len(gates) + len(ups) + len(downs)),
        out_specs=vmem,
        scratch_shapes=[
            pltpu.VMEM(arrived.shape, jnp.float32),
            pltpu.VMEM((count, features), jnp.bfloat16),
        ],
        compiler_params=pltpu.CompilerParams(vmem_limit_bytes=VMEM_BYTES),
        cost_estimate=pl.CostEstimate(
            flops=6 * count * features * units * 4,
            bytes_accessed=6 * units * 4 * features,
            transcendentals=count * units * 4,
        ),
        name=name,
    )(arrived, *gates, *ups, *downs)


def combine_kernel(returned, hidden, chosen_column, chosen_row, weight, out, rows, outputs):
    tokens, features = hidden.shape
    count = outputs.shape[0]
    blocks = features // LANES
    rows[...] = returned[...].astype(jnp.float32)
    for block in range(blocks):
        outputs[:, block * LANES : (block + 1) * LANES] = rows[
            pl.ds(block, count, stride=blocks), :
        ].astype(jnp.bfloat16)
    earlier = lax.broadcasted_iota(jnp.int32, (tokens, tokens), 1) < lax.broadcasted_iota(
        jnp.int32, (tokens, tokens), 0
    )
    same = (chosen_column[...] == chosen_row[...]) & earlier
    rank = jnp.sum(jnp.where(same, 1.0, 0.0), axis=1, keepdims=True)
    slot = slots(chosen_column[...], rank)
    pick = jnp.where(lax.broadcasted_iota(jnp.int32, (tokens, count), 1) == slot, 1.0, 0.0)
    picked = jnp.dot(pick.astype(jnp.bfloat16), outputs[...], preferred_element_type=jnp.float32)
    out[...] = (hidden[...].astype(jnp.float32) + weight[...] * picked).astype(jnp.bfloat16)


def combine(returned, hidden, chosen, weight):
    tokens, features = hidden.shape
    count = 64 * MOST
    vmem = pl.BlockSpec(memory_space=pltpu.VMEM)
    return pl.pallas_call(
        combine_kernel,
        out_shape=jax.ShapeDtypeStruct(hidden.shape, jnp.bfloat16),
        in_specs=[vmem] * 5,
        out_specs=vmem,
        scratch_shapes=[
            pltpu.VMEM(returned.shape, jnp.float32),
            pltpu.VMEM((count, features), jnp.bfloat16),
        ],
        compiler_params=pltpu.CompilerParams(vmem_limit_bytes=VMEM_BYTES),
        name="combine",
    )(returned, hidden, chosen, chosen.reshape(1, tokens), weight)


def after(value, *others):
    return lax.optimization_barrier((value, *others))[0]


def swapped(rows):
    return lax.ppermute(rows, "c", [(0, 1), (1, 0)])


def passed_along(block, by):
    return lax.ppermute(block, ("x", "y"), [(i, (i + by) % 16) for i in range(16)])


def per_device(
    queries,
    key_value,
    memory,
    memory_source,
    routing,
    router_weight,
    norm_gain,
    gate_matrix,
    up_matrix,
    down_matrix,
):
    features = queries.shape[1]
    kept = memory[0].transpose(1, 0, 2)
    near = passed_along(kept, 1)
    far = passed_along(kept, 2)
    moved = [
        lax.ppermute(matrix, ("x", "p"), spread_pairs())
        for matrix in (gate_matrix.T, up_matrix.T, down_matrix)
    ]
    placed = [lax.ppermute(matrix, ("x", "p"), lift_pairs()) for matrix in moved]
    left = [lax.ppermute(matrix, "x", ring(1)) for matrix in placed]
    right = [lax.ppermute(matrix, "x", ring(-1)) for matrix in placed]
    middle = features // 2
    across = [
        [lax.ppermute(left[0], "x", ring(1))],
        [lax.ppermute(right[1], "x", ring(-1))],
        [
            lax.ppermute(left[2][:, :middle], "x", ring(1)),
            lax.ppermute(right[2][:, middle:], "x", ring(-1)),
        ],
    ]
    weights = [
        [own, before, behind, *beyond]
        for own, before, behind, beyond in zip(placed, left, right, across)
    ]
    hidden, packed = attend(
        memory_source,
        after(queries, placed[0], placed[1], moved[2]),
        key_value.transpose(1, 0, 2),
        near,
        far,
        routing,
        norm_gain.reshape(1, features),
    )
    packed = after(packed, left[0], right[0], placed[2], left[1], right[1])
    chunks = packed.reshape(64, -1, LANES)
    arrived = lax.all_to_all(chunks, ("y", "s", "p"), 0, 0, tiled=True).reshape(packed.shape)
    partner = swapped(after(arrived, across[0], across[1], across[2]))
    lent = swapped(experts(partner, weights, "partner_experts"))
    made = experts(arrived, weights, "own_experts")
    made = (made.astype(jnp.float32) + lent.astype(jnp.float32)).astype(jnp.bfloat16)
    returned = lax.all_to_all(made.reshape(chunks.shape), ("y", "s", "p"), 0, 0, tiled=True)
    return combine(returned.reshape(packed.shape), hidden, routing, router_weight)


def solution(mesh):
    every = ("x", "y", "s", "p", "c")
    fine = Mesh(np.asarray(mesh.devices).reshape(4, 4, 4, 4, 2), every)
    return jax.shard_map(
        per_device,
        mesh=fine,
        in_specs=(
            P(every, None),
            P(every, None, None),
            P(every, None, None, None),
            P(every),
            P(every, None),
            P(every, None),
            P(),
            P(None, every),
            P(None, every),
            P(every, None),
        ),
        out_specs=P(every, None),
        check_vma=False,
    )
```

time: 286 us -> 317 us (1.11)
  starting transfers between devices: 176 us -> 194 us
  local copies, waits for them, and re-layouts: 10.6 us -> 18.2 us
  waiting for transfers between devices: 74.3 us -> 81.5 us
  Pallas kernels: 21.8 us -> 18.6 us
    all_to_all x1, starting transfers between devices: 43.3 us -> 83.3 us  [per_device(): lax.all_to_all(chunks, ('y', 's', 'p'), 0, 0, tiled=True)]
    ppermute x29 -> x18, starting transfers between devices: 104 us -> 87.9 us  [the longest x3 43.6 us: per_device(): lax.ppermute(matrix, ('x', 'p'), lift_pairs())]
    unnamed x58 -> x60, local copies, waits for them, and re-layouts: 4.3 us -> 18.2 us
    ppermute x29 -> x18, waiting for transfers between devices: 31.3 us -> 38.1 us  [the longest x3 18.5 us: per_device(): left = [lax.ppermute(matrix, 'x', ring(1)) for matrix in placed]]
    ppermute x4 -> x2, starting transfers between devices: 14.1 us -> 8.29 us  [passed_along(): lax.ppermute(block, ('x', 'y'), [(i, (i + by) % 16) for i in range(16)])]
    slice x4 -> x2, local copies, waits for them, and re-layouts: 4.9 us -> 0.05 us  [the longest x1 0.03 us: per_device(): right[2][:, middle:]]
    pallas_call x1 -> x2, Pallas kernels: 10.3 us -> 10.2 us  [experts(): pl.pallas_call(experts_kernel, out_shape=jax.ShapeDtypeStruct(arrived.sha...]
  transfers between devices with their start and end apart: 35 -> 22, of which waited for: 8 -> 6; matrix products, arithmetic and copies ran while one was open for 3% -> 1% of each run, Pallas kernels for 3% -> 4%
where the time goes in v2:
time: 317 us; the launch traced here: 315 us
  starting transfers between devices  194 us (61%)
  waiting for transfers between devices  81.5 us (26%)
  Pallas kernels  18.6 us (6%)
  local copies, waits for them, and re-layouts  18.2 us (6%)
    all_to_all x1, starting transfers between devices, per_device(): lax.all_to_all(chunks, ('y', 's', 'p'), 0, 0, tiled=True)  83.3 us
    ppermute x3, starting transfers between devices, per_device(): lax.ppermute(matrix, ('x', 'p'), lift_pairs())  43.6 us
    all_to_all x1, waiting for transfers between devices, per_device(): lax.all_to_all(made.reshape(chunks.shape), ('y', 's', 'p'), 0, 0, tiled=T...  43.4 us
    ppermute x3, waiting for transfers between devices, per_device(): left = [lax.ppermute(matrix, 'x', ring(1)) for matrix in placed]  18.5 us
    unnamed x60, local copies, waits for them, and re-layouts  18.2 us
    all_to_all x1, starting transfers between devices, per_device(): lax.all_to_all(made.reshape(chunks.shape), ('y', 's', 'p'), 0, 0, tiled=T...  15 us
    ppermute x3, starting transfers between devices, per_device(): left = [lax.ppermute(matrix, 'x', ring(1)) for matrix in placed]  12.7 us
    ppermute x1, waiting for transfers between devices, per_device(): lax.ppermute(left[2][:, :middle], 'x', ring(1))  12 us
  transfers between devices with their start and end apart: 22, of which 6 were waited for; matrix products, arithmetic and copies ran while one was open for 1% of the time, Pallas kernels for 4%

profile of v2, /device:TPU:6, one launch (start us, length us, event | category | flops | bytes accessed | tf_op | source)
XLA Modules:
  0.0 315.0 jit_solution(18121038850991063013)
XLA Ops:
  0.0 1.8 collective-permute-start.2
  1.8 1.9 collective-permute-start
  5.2 3.5 %collective-permute-start.5 = (bf16[2,128,2048]{2,1,0:T(8,128)(2,1)S(1)}, bf16[2,128,2048]{2,1,0:T(8,128)(2,1)S(1)}, u32[]{:S(2)}, u32[]{:S(2)}) collective-permute-start(bf16[2,128,2048]{2,1,0:T(8,128)(2,1)S(1)} %bitcast.24), channel_id=1, source_target_pairs={{0,32},{32,64},{64,96},{96,128},{128,160},{160,192},{192,224},{224... | collective-permute-start | bytes 3145736 | tf_op jit(solution)/shard_map/ppermute | solution.py:257
  8.7 4.8 %collective-permute-start.6 = (bf16[2,128,2048]{2,1,0:T(8,128)(2,1)S(1)}, bf16[2,128,2048]{2,1,0:T(8,128)(2,1)S(1)}, u32[]{:S(2)}, u32[]{:S(2)}) collective-permute-start(bf16[2,128,2048]{2,1,0:T(8,128)(2,1)S(1)} %bitcast.25), channel_id=1, source_target_pairs={{0,64},{32,96},{64,128},{96,160},{128,192},{160,224},{192,256},{22... | collective-permute-start | bytes 3145736 | tf_op jit(solution)/shard_map/ppermute | solution.py:257
  15.1 13.8 %collective-permute-start.3 = (bf16[176,2048]{1,0:T(8,128)(2,1)S(1)}, bf16[176,2048]{1,0:T(8,128)(2,1)S(1)}, u32[]{:S(2)}, u32[]{:S(2)}) collective-permute-start(bf16[176,2048]{1,0:T(8,128)(2,1)S(1)} %collective-permute-done.2), channel_id=1, source_target_pairs={{0,0},{2,4},{4,2},{6,6},{128,130},{130,134},{132,128},{134,132},{2... | collective-permute-start | bytes 2162696 | tf_op jit(solution)/shard_map/ppermute | solution.py:280
  28.9 15.4 %collective-permute-start.1 = (bf16[176,2048]{1,0:T(8,128)(2,1)S(1)}, bf16[176,2048]{1,0:T(8,128)(2,1)S(1)}, u32[]{:S(2)}, u32[]{:S(2)}) collective-permute-start(bf16[176,2048]{1,0:T(8,128)(2,1)S(1)} %collective-permute-done), channel_id=1, source_target_pairs={{0,0},{2,4},{4,2},{6,6},{128,130},{130,134},{132,128},{134,132},{2... | collective-permute-start | bytes 2162696 | tf_op jit(solution)/shard_map/ppermute | solution.py:280
  44.3 14.4 %collective-permute-start.9 = (bf16[176,2048]{1,0:T(8,128)(2,1)}, bf16[176,2048]{1,0:T(8,128)(2,1)}, u32[]{:S(2)}, u32[]{:S(2)}) collective-permute-start(bf16[176,2048]{1,0:T(8,128)(2,1)} %collective-permute-done.4), channel_id=1, source_target_pairs={{0,0},{2,4},{4,2},{6,6},{128,130},{130,134},{132,128},{134,132},{2... | collective-permute-start | bytes 2162696 | tf_op jit(solution)/shard_map/ppermute | solution.py:280
  58.7 1.9 collective-permute-start.11
  61.6 5.1 %collective-permute-start.10 = (bf16[176,2048]{1,0:T(8,128)(2,1)S(1)}, bf16[176,2048]{1,0:T(8,128)(2,1)S(1)}, u32[]{:S(2)}, u32[]{:S(2)}) collective-permute-start(bf16[176,2048]{1,0:T(8,128)(2,1)S(1)} %collective-permute-done.3.refs_4_), channel_id=1, source_target_pairs={{0,128},{128,256},{256,384},{384,0},{1,129},{129,257},{257,385},{3... | collective-permute-start | bytes 2162696 | tf_op jit(solution)/shard_map/ppermute | solution.py:281
  66.8 1.9 collective-permute-start.7
  69.8 3.9 %collective-permute-start.8 = (bf16[176,2048]{1,0:T(8,128)(2,1)S(1)}, bf16[176,2048]{1,0:T(8,128)(2,1)}, u32[]{:S(2)}, u32[]{:S(2)}) collective-permute-start(bf16[176,2048]{1,0:T(8,128)(2,1)S(1)} %collective-permute-done.1.refs_0_), channel_id=1, source_target_pairs={{0,384},{128,0},{256,128},{384,256},{1,385},{129,1},{257,129},{385... | collective-permute-start | bytes 2162696 | tf_op jit(solution)/shard_map/ppermute | solution.py:282
  73.8 1.7 copy.19
  77.3 6.6 %attend.1 = (bf16[128,2048]{1,0:T(8,128)(2,1)S(1)}, bf16[3072,128]{1,0:T(8,128)(2,1)S(1)}) custom-call(s32[1]{0:T(128)S(6)} %copy.20.source, bf16[128,2048]{1,0:T(8,128)(2,1)S(1)} %copy-done.23, bf16[2,128,2048]{2,1,0:T(8,128)(2,1)S(1)} %bitcast.16, bf16[2,128,2048]{2,1,0:T(8,128)(2,1)S(1)} %copy-done.17, bf16[2,128,2048]{2,1,0:T(8,128)(2,1)S(1)} %copy-done.19, ...), custom_call_target="tpu_custom_call" | custom-call | flops 268435456 | bytes 2621440 | tf_op jit(solution)/shard_map/attend/pallas_call | solution.py:127
  85.5 10.6 %collective-permute-done.7.refs_1_ = bf16[176,2048]{1,0:T(8,128)(2,1)} collective-permute-done((bf16[176,2048]{1,0:T(8,128)(2,1)S(1)}, bf16[176,2048]{1,0:T(8,128)(2,1)}, u32[]{:S(2)}, u32[]{:S(2)}) %collective-permute-start.7) | collective-permute-done | bytes 720928 | tf_op jit(solution)/shard_map/ppermute | solution.py:281
  97.0 83.3 %all-to-all-start = ((bf16[64,48,128]{2,1,0:T(8,128)(2,1)}), bf16[64,48,128]{2,1,0:T(8,128)(2,1)S(1)}, u32[]{:S(2)}, u32[]{:S(2)}) async-start(bf16[64,48,128]{2,1,0:T(8,128)(2,1)} %bitcast.20), calls=%async_computation | async-start | bytes 1572864 | tf_op jit(solution)/shard_map/all_to_all | solution.py:307
  180.4 5.7 %collective-permute-start.14 = (bf16[176,2048]{1,0:T(8,128)(2,1)}, bf16[176,2048]{1,0:T(8,128)(2,1)S(1)}, u32[]{:S(2)}, u32[]{:S(2)}) collective-permute-start(bf16[176,2048]{1,0:T(8,128)(2,1)} %collective-permute-done.9.refs_8_), channel_id=1, source_target_pairs={{0,128},{128,256},{256,384},{384,0},{1,129},{129,257},{257,385},{3... | collective-permute-start | bytes 2162696 | tf_op jit(solution)/shard_map/ppermute | solution.py:281
  186.1 1.9 collective-permute-start.15
  188.0 5.1 %collective-permute-start.12 = (bf16[176,2048]{1,0:T(8,128)(2,1)}, bf16[176,2048]{1,0:T(8,128)(2,1)S(1)}, u32[]{:S(2)}, u32[]{:S(2)}) collective-permute-start(bf16[176,2048]{1,0:T(8,128)(2,1)} %collective-permute-done.7.refs_1_), channel_id=1, source_target_pairs={{0,128},{128,256},{256,384},{384,0},{1,129},{129,257},{257,385},{3... | collective-permute-start | bytes 2162696 | tf_op jit(solution)/shard_map/ppermute | solution.py:285
  193.2 1.9 collective-permute-start.13
  195.1 7.9 %collective-permute-done.14.refs_9_ = bf16[176,2048]{1,0:T(8,128)(2,1)S(1)} collective-permute-done((bf16[176,2048]{1,0:T(8,128)(2,1)}, bf16[176,2048]{1,0:T(8,128)(2,1)S(1)}, u32[]{:S(2)}, u32[]{:S(2)}) %collective-permute-start.14) | collective-permute-done | bytes 720928 | tf_op jit(solution)/shard_map/ppermute | solution.py:281
  203.0 5.5 %collective-permute-start.16 = (bf16[176,1024]{1,0:T(8,128)(2,1)S(1)}, bf16[176,1024]{1,0:T(8,128)(2,1)S(1)}, u32[]{:S(2)}, u32[]{:S(2)}) collective-permute-start(bf16[176,1024]{1,0:T(8,128)(2,1)S(1)} %slice.8), channel_id=1, source_target_pairs={{0,128},{128,256},{256,384},{384,0},{1,129},{129,257},{257,385},{3... | collective-permute-start | bytes 1081352 | tf_op jit(solution)/shard_map/ppermute | solution.py:288
  208.6 1.9 collective-permute-start.17
  210.5 12.0 %collective-permute-done.16.refs_11_ = bf16[176,1024]{1,0:T(8,128)(2,1)S(1)} collective-permute-done((bf16[176,1024]{1,0:T(8,128)(2,1)S(1)}, bf16[176,1024]{1,0:T(8,128)(2,1)S(1)}, u32[]{:S(2)}, u32[]{:S(2)}) %collective-permute-start.16) | collective-permute-done | bytes 360480 | tf_op jit(solution)/shard_map/ppermute | solution.py:288
  222.5 5.3 %collective-permute-done.17.refs_12_ = bf16[176,1024]{1,0:T(8,128)(2,1)S(1)} collective-permute-done((bf16[176,1024]{1,0:T(8,128)(2,1)S(1)}, bf16[176,1024]{1,0:T(8,128)(2,1)S(1)}, u32[]{:S(2)}, u32[]{:S(2)}) %collective-permute-start.17) | collective-permute-done | bytes 360480 | tf_op jit(solution)/shard_map/ppermute | solution.py:289
  230.3 1.9 collective-permute-start.18
  232.3 2.3 collective-permute-done.18.arrived
  241.1 5.2 %partner_experts.1 = bf16[3072,128]{1,0:T(8,128)(2,1)S(1)} custom-call(bf16[3072,128]{1,0:T(8,128)(2,1)S(1)} %collective-permute-done.18.arrived, bf16[176,2048]{1,0:T(8,128)(2,1)S(1)} %copy-done.1, bf16[176,2048]{1,0:T(8,128)(2,1)} %collective-permute-done.7.refs_1_, bf16[176,2048]{1,0:T(8,128)(2,1)} %collective-permute-done.8.refs_2_, ...), custom_call_target="tpu_custom_call" | custom-call | flops 1660944384 | bytes 8650752 | tf_op jit(solution)/shard_map/partner_experts/pallas_call | solution.py:191
  246.2 2.2 collective-permute-start.19
  248.5 5.0 %own_experts.1 = bf16[3072,128]{1,0:T(8,128)(2,1)S(1)} custom-call(bf16[3072,128]{1,0:T(8,128)(2,1)S(1)} %bitcast.18, bf16[176,2048]{1,0:T(8,128)(2,1)S(1)} %copy-done.2, bf16[176,2048]{1,0:T(8,128)(2,1)} %collective-permute-done.7.refs_1_, bf16[176,2048]{1,0:T(8,128)(2,1)} %collective-permute-done.8.refs_2_, bf16[176,2048]{1,0:T(8,128)(2,1)S(1)} %copy-done.10, ...), custom_call_target="tpu_custom_call" | custom-call | flops 1660944384 | bytes 8650752 | tf_op jit(solution)/shard_map/own_experts/pallas_call | solution.py:191
  254.6 15.0 %all-to-all-start.1 = ((bf16[64,48,128]{2,1,0:T(8,128)(2,1)}), bf16[64,48,128]{2,1,0:T(8,128)(2,1)S(1)}, u32[]{:S(2)}, u32[]{:S(2)}) async-start(bf16[64,48,128]{2,1,0:T(8,128)(2,1)} %bitcast.10), calls=%async_computation.1 | async-start | bytes 1572864 | tf_op jit(solution)/shard_map/all_to_all | solution.py:312
  269.8 43.4 %all-to-all-done.1 = bf16[64,48,128]{2,1,0:T(8,128)(2,1)S(1)} async-done(((bf16[64,48,128]{2,1,0:T(8,128)(2,1)}), bf16[64,48,128]{2,1,0:T(8,128)(2,1)S(1)}, u32[]{:S(2)}, u32[]{:S(2)}) %all-to-all-start.1) | async-done | bytes 786464 | tf_op jit(solution)/shard_map/all_to_all | solution.py:312
  313.1 1.9 combine.1
  (79 shorter events, 19.2 us)
Async XLA Ops:
  0.0 15.1 %collective-permute-start.2 = (bf16[176,2048]{1,0:T(8,128)(2,1)}, bf16[176,2048]{1,0:T(8,128)(2,1)S(1)}, u32[]{:S(2)}, u32[]{:S(2)}) collective-permute-start(bf16[176,2048]{1,0:T(8,128)(2,1)} %bitcast.26), channel_id=1, source_target_pairs={{0,0},{258,2},{132,4},{390,6},{128,128},{386,130},{4,132},{262,134... | collective-permute-start | bytes 2162696 | tf_op jit(solution)/shard_map/ppermute | solution.py:277
  1.8 11.8 %copy-start.27 = (bf16[176,2048]{1,0:T(8,128)(2,1)S(1)}, bf16[176,2048]{1,0:T(8,128)(2,1)}, u32[]{:S(2)}) copy-start(bf16[176,2048]{1,0:T(8,128)(2,1)} %param.19) | copy-start | bytes 2162692
  1.8 71.9 %copy-start.25 = (s32[128,1]{0,1:T(1,128)S(1)}, s32[128,1]{0,1:T(1,128)}, u32[]{:S(2)}) copy-start(s32[128,1]{0,1:T(1,128)} %param.14) | copy-start | bytes 1540
  1.8 27.1 %collective-permute-start = (bf16[176,2048]{1,0:T(8,128)(2,1)}, bf16[176,2048]{1,0:T(8,128)(2,1)S(1)}, u32[]{:S(2)}, u32[]{:S(2)}) collective-permute-start(bf16[176,2048]{1,0:T(8,128)(2,1)} %bitcast.27), channel_id=1, source_target_pairs={{0,0},{258,2},{132,4},{390,6},{128,128},{386,130},{4,132},{262,134... | collective-permute-start | bytes 2162696 | tf_op jit(solution)/shard_map/ppermute | solution.py:277
  5.2 55.4 %collective-permute-start.5 = (bf16[2,128,2048]{2,1,0:T(8,128)(2,1)S(1)}, bf16[2,128,2048]{2,1,0:T(8,128)(2,1)S(1)}, u32[]{:S(2)}, u32[]{:S(2)}) collective-permute-start(bf16[2,128,2048]{2,1,0:T(8,128)(2,1)S(1)} %bitcast.24), channel_id=1, source_target_pairs={{0,32},{32,64},{64,96},{96,128},{128,160},{160,192},{192,224},{224... | collective-permute-start | bytes 3145736 | tf_op jit(solution)/shard_map/ppermute | solution.py:257
  8.7 60.0 %collective-permute-start.6 = (bf16[2,128,2048]{2,1,0:T(8,128)(2,1)S(1)}, bf16[2,128,2048]{2,1,0:T(8,128)(2,1)S(1)}, u32[]{:S(2)}, u32[]{:S(2)}) collective-permute-start(bf16[2,128,2048]{2,1,0:T(8,128)(2,1)S(1)} %bitcast.25), channel_id=1, source_target_pairs={{0,64},{32,96},{64,128},{96,160},{128,192},{160,224},{192,256},{22... | collective-permute-start | bytes 3145736 | tf_op jit(solution)/shard_map/ppermute | solution.py:257
  13.5 30.8 %collective-permute-start.4 = (bf16[176,2048]{1,0:T(8,128)(2,1)S(1)}, bf16[176,2048]{1,0:T(8,128)(2,1)}, u32[]{:S(2)}, u32[]{:S(2)}) collective-permute-start(bf16[176,2048]{1,0:T(8,128)(2,1)S(1)} %copy-done.27), channel_id=1, source_target_pairs={{0,0},{258,2},{132,4},{390,6},{128,128},{386,130},{4,132},{262,134... | collective-permute-start | bytes 2162696 | tf_op jit(solution)/shard_map/ppermute | solution.py:277
  15.1 43.6 %collective-permute-start.3 = (bf16[176,2048]{1,0:T(8,128)(2,1)S(1)}, bf16[176,2048]{1,0:T(8,128)(2,1)S(1)}, u32[]{:S(2)}, u32[]{:S(2)}) collective-permute-start(bf16[176,2048]{1,0:T(8,128)(2,1)S(1)} %collective-permute-done.2), channel_id=1, source_target_pairs={{0,0},{2,4},{4,2},{6,6},{128,130},{130,134},{132,128},{134,132},{2... | collective-permute-start | bytes 2162696 | tf_op jit(solution)/shard_map/ppermute | solution.py:280
  28.9 37.9 %collective-permute-start.1 = (bf16[176,2048]{1,0:T(8,128)(2,1)S(1)}, bf16[176,2048]{1,0:T(8,128)(2,1)S(1)}, u32[]{:S(2)}, u32[]{:S(2)}) collective-permute-start(bf16[176,2048]{1,0:T(8,128)(2,1)S(1)} %collective-permute-done), channel_id=1, source_target_pairs={{0,0},{2,4},{4,2},{6,6},{128,130},{130,134},{132,128},{134,132},{2... | collective-permute-start | bytes 2162696 | tf_op jit(solution)/shard_map/ppermute | solution.py:280
  44.3 41.2 %collective-permute-start.9 = (bf16[176,2048]{1,0:T(8,128)(2,1)}, bf16[176,2048]{1,0:T(8,128)(2,1)}, u32[]{:S(2)}, u32[]{:S(2)}) collective-permute-start(bf16[176,2048]{1,0:T(8,128)(2,1)} %collective-permute-done.4), channel_id=1, source_target_pairs={{0,0},{2,4},{4,2},{6,6},{128,130},{130,134},{132,128},{134,132},{2... | collective-permute-start | bytes 2162696 | tf_op jit(solution)/shard_map/ppermute | solution.py:280
  58.7 26.8 %collective-permute-start.11 = (bf16[176,2048]{1,0:T(8,128)(2,1)S(1)}, bf16[176,2048]{1,0:T(8,128)(2,1)S(1)}, u32[]{:S(2)}, u32[]{:S(2)}) collective-permute-start(bf16[176,2048]{1,0:T(8,128)(2,1)S(1)} %collective-permute-done.3.refs_4_), channel_id=1, source_target_pairs={{0,384},{128,0},{256,128},{384,256},{1,385},{129,1},{257,129},{385... | collective-permute-start | bytes 2162696 | tf_op jit(solution)/shard_map/ppermute | solution.py:282
  61.6 34.5 %collective-permute-start.10 = (bf16[176,2048]{1,0:T(8,128)(2,1)S(1)}, bf16[176,2048]{1,0:T(8,128)(2,1)S(1)}, u32[]{:S(2)}, u32[]{:S(2)}) collective-permute-start(bf16[176,2048]{1,0:T(8,128)(2,1)S(1)} %collective-permute-done.3.refs_4_), channel_id=1, source_target_pairs={{0,128},{128,256},{256,384},{384,0},{1,129},{129,257},{257,385},{3... | collective-permute-start | bytes 2162696 | tf_op jit(solution)/shard_map/ppermute | solution.py:281
  66.8 8.8 %copy-start = (bf16[176,2048]{1,0:T(8,128)(2,1)}, bf16[176,2048]{1,0:T(8,128)(2,1)S(1)}, u32[]{:S(2)}) copy-start(bf16[176,2048]{1,0:T(8,128)(2,1)S(1)} %collective-permute-done.1.refs_0_) | copy-start | bytes 2162692
  66.8 29.4 %collective-permute-start.7 = (bf16[176,2048]{1,0:T(8,128)(2,1)S(1)}, bf16[176,2048]{1,0:T(8,128)(2,1)}, u32[]{:S(2)}, u32[]{:S(2)}) collective-permute-start(bf16[176,2048]{1,0:T(8,128)(2,1)S(1)} %collective-permute-done.1.refs_0_), channel_id=1, source_target_pairs={{0,128},{128,256},{256,384},{384,0},{1,129},{129,257},{257,385},{3... | collective-permute-start | bytes 2162696 | tf_op jit(solution)/shard_map/ppermute | solution.py:281
  69.8 26.4 %collective-permute-start.8 = (bf16[176,2048]{1,0:T(8,128)(2,1)S(1)}, bf16[176,2048]{1,0:T(8,128)(2,1)}, u32[]{:S(2)}, u32[]{:S(2)}) collective-permute-start(bf16[176,2048]{1,0:T(8,128)(2,1)S(1)} %collective-permute-done.1.refs_0_), channel_id=1, source_target_pairs={{0,384},{128,0},{256,128},{384,256},{1,385},{129,1},{257,129},{385... | collective-permute-start | bytes 2162696 | tf_op jit(solution)/shard_map/ppermute | solution.py:282
  85.5 10.6 %copy-start.3 = (bf16[176,2048]{1,0:T(8,128)(2,1)}, bf16[176,2048]{1,0:T(8,128)(2,1)S(1)}, u32[]{:S(2)}) copy-start(bf16[176,2048]{1,0:T(8,128)(2,1)S(1)} %collective-permute-done.11.refs_6_) | copy-start | bytes 2162692
  97.0 133.3 %all-to-all-start = ((bf16[64,48,128]{2,1,0:T(8,128)(2,1)}), bf16[64,48,128]{2,1,0:T(8,128)(2,1)S(1)}, u32[]{:S(2)}, u32[]{:S(2)}) async-start(bf16[64,48,128]{2,1,0:T(8,128)(2,1)} %bitcast.20), calls=%async_computation | async-start | bytes 1572864 | tf_op jit(solution)/shard_map/all_to_all | solution.py:307
  180.4 22.6 %collective-permute-start.14 = (bf16[176,2048]{1,0:T(8,128)(2,1)}, bf16[176,2048]{1,0:T(8,128)(2,1)S(1)}, u32[]{:S(2)}, u32[]{:S(2)}) collective-permute-start(bf16[176,2048]{1,0:T(8,128)(2,1)} %collective-permute-done.9.refs_8_), channel_id=1, source_target_pairs={{0,128},{128,256},{256,384},{384,0},{1,129},{129,257},{257,385},{3... | collective-permute-start | bytes 2162696 | tf_op jit(solution)/shard_map/ppermute | solution.py:281
  186.1 22.4 %collective-permute-start.15 = (bf16[176,2048]{1,0:T(8,128)(2,1)}, bf16[176,2048]{1,0:T(8,128)(2,1)S(1)}, u32[]{:S(2)}, u32[]{:S(2)}) collective-permute-start(bf16[176,2048]{1,0:T(8,128)(2,1)} %collective-permute-done.9.refs_8_), channel_id=1, source_target_pairs={{0,384},{128,0},{256,128},{384,256},{1,385},{129,1},{257,129},{385... | collective-permute-start | bytes 2162696 | tf_op jit(solution)/shard_map/ppermute | solution.py:282
  188.0 40.5 %collective-permute-start.12 = (bf16[176,2048]{1,0:T(8,128)(2,1)}, bf16[176,2048]{1,0:T(8,128)(2,1)S(1)}, u32[]{:S(2)}, u32[]{:S(2)}) collective-permute-start(bf16[176,2048]{1,0:T(8,128)(2,1)} %collective-permute-done.7.refs_1_), channel_id=1, source_target_pairs={{0,128},{128,256},{256,384},{384,0},{1,129},{129,257},{257,385},{3... | collective-permute-start | bytes 2162696 | tf_op jit(solution)/shard_map/ppermute | solution.py:285
  193.2 36.3 %collective-permute-start.13 = (bf16[176,2048]{1,0:T(8,128)(2,1)}, bf16[176,2048]{1,0:T(8,128)(2,1)S(1)}, u32[]{:S(2)}, u32[]{:S(2)}) collective-permute-start(bf16[176,2048]{1,0:T(8,128)(2,1)} %copy-done.3), channel_id=1, source_target_pairs={{0,384},{128,0},{256,128},{384,256},{1,385},{129,1},{257,129},{385... | collective-permute-start | bytes 2162696 | tf_op jit(solution)/shard_map/ppermute | solution.py:286
  203.0 19.5 %collective-permute-start.16 = (bf16[176,1024]{1,0:T(8,128)(2,1)S(1)}, bf16[176,1024]{1,0:T(8,128)(2,1)S(1)}, u32[]{:S(2)}, u32[]{:S(2)}) collective-permute-start(bf16[176,1024]{1,0:T(8,128)(2,1)S(1)} %slice.8), channel_id=1, source_target_pairs={{0,128},{128,256},{256,384},{384,0},{1,129},{129,257},{257,385},{3... | collective-permute-start | bytes 1081352 | tf_op jit(solution)/shard_map/ppermute | solution.py:288
  208.6 19.3 %collective-permute-start.17 = (bf16[176,1024]{1,0:T(8,128)(2,1)S(1)}, bf16[176,1024]{1,0:T(8,128)(2,1)S(1)}, u32[]{:S(2)}, u32[]{:S(2)}) collective-permute-start(bf16[176,1024]{1,0:T(8,128)(2,1)S(1)} %slice.9), channel_id=1, source_target_pairs={{0,384},{128,0},{256,128},{384,256},{1,385},{129,1},{257,129},{385... | collective-permute-start | bytes 1081352 | tf_op jit(solution)/shard_map/ppermute | solution.py:289
  230.3 4.2 %collective-permute-start.18 = (bf16[3072,128]{1,0:T(8,128)(2,1)S(1)}, bf16[3072,128]{1,0:T(8,128)(2,1)S(1)}, u32[]{:S(2)}, u32[]{:S(2)}) collective-permute-start(bf16[3072,128]{1,0:T(8,128)(2,1)S(1)} %bitcast.17), channel_id=1, source_target_pairs={{0,1},{1,0},{2,3},{3,2},{4,5},{5,4},{6,7},{7,6},{8,9},{9,8},{10,11... | collective-permute-start | bytes 2359304 | tf_op jit(solution)/shard_map/ppermute | solution.py:253
  241.1 7.4 %copy-start.2 = (bf16[176,2048]{1,0:T(8,128)(2,1)S(1)}, bf16[176,2048]{1,0:T(8,128)(2,1)}, u32[]{:S(2)}) copy-start(bf16[176,2048]{1,0:T(8,128)(2,1)} %copy-done) | copy-start | bytes 2162692
  241.1 7.4 %copy-start.7 = (bf16[176,2048]{1,0:T(8,128)(2,1)S(1)}, bf16[176,2048]{1,0:T(8,128)(2,1)}, u32[]{:S(2)}) copy-start(bf16[176,2048]{1,0:T(8,128)(2,1)} %copy-done.5) | copy-start | bytes 2162692
  241.1 7.4 %copy-start.10 = (bf16[176,2048]{1,0:T(8,128)(2,1)S(1)}, bf16[176,2048]{1,0:T(8,128)(2,1)}, u32[]{:S(2)}) copy-start(bf16[176,2048]{1,0:T(8,128)(2,1)} %copy-done.8) | copy-start | bytes 2162692
  241.1 7.4 %copy-start.13 = (bf16[176,2048]{1,0:T(8,128)(2,1)S(1)}, bf16[176,2048]{1,0:T(8,128)(2,1)}, u32[]{:S(2)}) copy-start(bf16[176,2048]{1,0:T(8,128)(2,1)} %copy-done.11) | copy-start | bytes 2162692
  246.2 7.3 %collective-permute-start.19 = (bf16[3072,128]{1,0:T(8,128)(2,1)S(1)}, bf16[3072,128]{1,0:T(8,128)(2,1)S(1)}, u32[]{:S(2)}, u32[]{:S(2)}) collective-permute-start(bf16[3072,128]{1,0:T(8,128)(2,1)S(1)} %partner_experts.1), channel_id=1, source_target_pairs={{0,1},{1,0},{2,3},{3,2},{4,5},{5,4},{6,7},{7,6},{8,9},{9,8},{10,11... | collective-permute-start | bytes 2359304 | tf_op jit(solution)/shard_map/ppermute | solution.py:253
  254.6 15.0 %copy-start.26 = (f32[128,1]{0,1:T(1,128)S(1)}, f32[128,1]{0,1:T(1,128)}, u32[]{:S(2)}) copy-start(f32[128,1]{0,1:T(1,128)} %param.15) | copy-start | bytes 1540
  254.6 58.5 %copy-start.22 = (bf16[128,2048]{1,0:T(8,128)(2,1)S(1)}, bf16[128,2048]{1,0:T(8,128)(2,1)}, u32[]{:S(2)}) copy-start(bf16[128,2048]{1,0:T(8,128)(2,1)} %copy-done.21) | copy-start | bytes 1572868
  254.6 58.5 %all-to-all-start.1 = ((bf16[64,48,128]{2,1,0:T(8,128)(2,1)}), bf16[64,48,128]{2,1,0:T(8,128)(2,1)S(1)}, u32[]{:S(2)}, u32[]{:S(2)}) async-start(bf16[64,48,128]{2,1,0:T(8,128)(2,1)} %bitcast.10), calls=%async_computation.1 | async-start | bytes 1572864 | tf_op jit(solution)/shard_map/all_to_all | solution.py:312
  (18 other events, 22.0 us)

commit v3 on v2

--- a/solution.py
+++ b/solution.py
@@ -12,7 +12,7 @@
 HEADS = 16
 MOST = 3
 LANES = 128
-VMEM_BYTES = 32 * 1024 * 1024
+VMEM_BYTES = 14 * 1024 * 1024
 
 PLACE = ((0, 2, 1, 3), (1, 3, 0, 2), (2, 0, 3, 1), (3, 1, 2, 0))
 
@@ -152,7 +152,7 @@
 
 
 def experts_kernel(arrived, *refs):
-    gates, ups, downs, (out, rows, tokens) = refs[:4], refs[4:8], refs[8:13], refs[13:]
+    gates, ups, downs, (out, rows, tokens) = refs[:4], refs[4:8], refs[8:12], refs[12:]
     count, features = tokens.shape
     blocks = features // LANES
     rows[...] = arrived[...].astype(jnp.float32)
@@ -170,16 +170,11 @@
             tokens[...], up[...], transposed, preferred_element_type=jnp.float32
         )
         acts.append((gated / (1.0 + jnp.exp(-gated)) * raised).astype(jnp.bfloat16))
-    middle = features // 2
-    for half in range(2):
-        at = slice(half * middle, (half + 1) * middle)
-        made = jnp.dot(acts[3], downs[3 + half][...], preferred_element_type=jnp.float32)
-        for act, down in zip(acts[:3], downs[:3]):
-            made += jnp.dot(act, down[:, at], preferred_element_type=jnp.float32)
-        for block in range(blocks // 2):
-            rows[pl.ds(half * (blocks // 2) + block, count, stride=blocks), :] = made[
-                :, block * LANES : (block + 1) * LANES
-            ]
+    made = jnp.zeros((count, features), jnp.float32)
+    for act, down in zip(acts, downs):
+        made += jnp.dot(act, down[...], preferred_element_type=jnp.float32)
+    for block in range(blocks):
+        rows[pl.ds(block, count, stride=blocks), :] = made[:, block * LANES : (block + 1) * LANES]
     out[...] = rows[...].astype(jnp.bfloat16)
 
 
@@ -253,8 +248,8 @@
     return lax.ppermute(rows, "c", [(0, 1), (1, 0)])
 
 
-def passed_along(block, by):
-    return lax.ppermute(block, ("x", "y"), [(i, (i + by) % 16) for i in range(16)])
+def passed_along(block):
+    return lax.ppermute(block, ("x", "y"), [(i, (i + 1) % 16) for i in range(16)])
 
 
 def per_device(
@@ -271,8 +266,8 @@
 ):
     features = queries.shape[1]
     kept = memory[0].transpose(1, 0, 2)
-    near = passed_along(kept, 1)
-    far = passed_along(kept, 2)
+    near = passed_along(kept)
+    far = passed_along(near)
     moved = [
         lax.ppermute(matrix, ("x", "p"), spread_pairs())
         for matrix in (gate_matrix.T, up_matrix.T, down_matrix)
@@ -280,17 +275,9 @@
     placed = [lax.ppermute(matrix, ("x", "p"), lift_pairs()) for matrix in moved]
     left = [lax.ppermute(matrix, "x", ring(1)) for matrix in placed]
     right = [lax.ppermute(matrix, "x", ring(-1)) for matrix in placed]
-    middle = features // 2
-    across = [
-        [lax.ppermute(left[0], "x", ring(1))],
-        [lax.ppermute(right[1], "x", ring(-1))],
-        [
-            lax.ppermute(left[2][:, :middle], "x", ring(1)),
-            lax.ppermute(right[2][:, middle:], "x", ring(-1)),
-        ],
-    ]
+    across = [lax.ppermute(matrix, "x", ring(-1)) for matrix in right]
     weights = [
-        [own, before, behind, *beyond]
+        [own, before, behind, beyond]
         for own, before, behind, beyond in zip(placed, left, right, across)
     ]
     hidden, packed = attend(
@@ -302,10 +289,10 @@
         routing,
         norm_gain.reshape(1, features),
     )
-    packed = after(packed, left[0], right[0], placed[2], left[1], right[1])
+    packed = after(packed, *left, *right)
     chunks = packed.reshape(64, -1, LANES)
     arrived = lax.all_to_all(chunks, ("y", "s", "p"), 0, 0, tiled=True).reshape(packed.shape)
-    partner = swapped(after(arrived, across[0], across[1], across[2]))
+    partner = swapped(after(arrived, *across))
     lent = swapped(experts(partner, weights, "partner_experts"))
     made = experts(arrived, weights, "own_experts")
     made = (made.astype(jnp.float32) + lent.astype(jnp.float32)).astype(jnp.bfloat16)

time: 317 us -> 299 us (0.943)
  starting transfers between devices: 194 us -> 151 us
  waiting for transfers between devices: 81.5 us -> 108 us
    all_to_all x1, starting transfers between devices: 83.3 us -> 35.6 us  [per_device(): lax.all_to_all(chunks, ('y', 's', 'p'), 0, 0, tiled=True)]
    ppermute x6 -> x5, waiting for transfers between devices: 17.3 us -> 43.5 us  [the longest x3 40.1 us: per_device(): across = [lax.ppermute(matrix, 'x', ring(-1)) for matrix in right]]
    ppermute x3, starting transfers between devices: 7.75 us -> 28 us  [per_device(): right = [lax.ppermute(matrix, 'x', ring(-1)) for matrix in placed]]
    ppermute x6 -> x5, starting transfers between devices: 22.8 us -> 15 us  [the longest x3 9.61 us: per_device(): across = [lax.ppermute(matrix, 'x', ring(-1)) for matrix in right]]
    ppermute x3, starting transfers between devices: 12.7 us -> 5.74 us  [per_device(): left = [lax.ppermute(matrix, 'x', ring(1)) for matrix in placed]]
    ppermute x3, waiting for transfers between devices: 0.01 us -> 4.06 us  [per_device(): right = [lax.ppermute(matrix, 'x', ring(-1)) for matrix in placed]]
    ppermute x3, waiting for transfers between devices: 18.5 us -> 14.8 us  [per_device(): left = [lax.ppermute(matrix, 'x', ring(1)) for matrix in placed]]
    unnamed x60 -> x50, local copies, waits for them, and re-layouts: 18.2 us -> 16.5 us
  transfers between devices with their start and end apart: 22 -> 21, of which waited for: 6 -> 9; matrix products, arithmetic and copies ran while one was open for 1% -> 1% of each run, Pallas kernels for 4% -> 4%
where the time goes in v3:
time: 299 us; the launch traced here: 296 us
  starting transfers between devices  151 us (51%)
  waiting for transfers between devices  108 us (36%)
  Pallas kernels  18.9 us (6%)
  local copies, waits for them, and re-layouts  16.5 us (6%)
    ppermute x3, starting transfers between devices, per_device(): lax.ppermute(matrix, ('x', 'p'), lift_pairs())  44 us
    all_to_all x1, waiting for transfers between devices, per_device(): lax.all_to_all(made.reshape(chunks.shape), ('y', 's', 'p'), 0, 0, tiled=T...  43.4 us
    ppermute x3, waiting for transfers between devices, per_device(): across = [lax.ppermute(matrix, 'x', ring(-1)) for matrix in right]  40.1 us
    all_to_all x1, starting transfers between devices, per_device(): lax.all_to_all(chunks, ('y', 's', 'p'), 0, 0, tiled=True)  35.6 us
    ppermute x3, starting transfers between devices, per_device(): right = [lax.ppermute(matrix, 'x', ring(-1)) for matrix in placed]  28 us
    unnamed x50, local copies, waits for them, and re-layouts  16.5 us
    all_to_all x1, starting transfers between devices, per_device(): lax.all_to_all(made.reshape(chunks.shape), ('y', 's', 'p'), 0, 0, tiled=T...  15 us
    ppermute x3, waiting for transfers between devices, per_device(): left = [lax.ppermute(matrix, 'x', ring(1)) for matrix in placed]  14.8 us
  transfers between devices with their start and end apart: 21, of which 9 were waited for; matrix products, arithmetic and copies ran while one was open for 1% of the time, Pallas kernels for 4%

profile of v3, /device:TPU:6, one launch (start us, length us, event | category | flops | bytes accessed | tf_op | source)
XLA Modules:
  0.0 296.4 jit_solution(1974733142744487136)
XLA Ops:
  0.0 1.9 collective-permute-start
  3.5 3.5 %collective-permute-start.5 = (bf16[2,128,2048]{2,1,0:T(8,128)(2,1)S(1)}, bf16[2,128,2048]{2,1,0:T(8,128)(2,1)S(1)}, u32[]{:S(2)}, u32[]{:S(2)}) collective-permute-start(bf16[2,128,2048]{2,1,0:T(8,128)(2,1)S(1)} %bitcast.24), channel_id=1, source_target_pairs={{0,32},{32,64},{64,96},{96,128},{128,160},{160,192},{192,224},{224... | collective-permute-start | bytes 3145736 | tf_op jit(solution)/shard_map/ppermute | solution.py:252
  8.4 20.6 %collective-permute-start.1 = (bf16[176,2048]{1,0:T(8,128)(2,1)S(1)}, bf16[176,2048]{1,0:T(8,128)(2,1)S(1)}, u32[]{:S(2)}, u32[]{:S(2)}) collective-permute-start(bf16[176,2048]{1,0:T(8,128)(2,1)S(1)} %collective-permute-done), channel_id=1, source_target_pairs={{0,0},{2,4},{4,2},{6,6},{128,130},{130,134},{132,128},{134,132},{2... | collective-permute-start | bytes 2162696 | tf_op jit(solution)/shard_map/ppermute | solution.py:275
  29.0 3.4 %collective-permute-done.5.near = bf16[2,128,2048]{2,1,0:T(8,128)(2,1)S(1)} collective-permute-done((bf16[2,128,2048]{2,1,0:T(8,128)(2,1)S(1)}, bf16[2,128,2048]{2,1,0:T(8,128)(2,1)S(1)}, u32[]{:S(2)}, u32[]{:S(2)}) %collective-permute-start.5) | collective-permute-done | bytes 1048608 | tf_op jit(solution)/shard_map/ppermute | solution.py:252
  32.4 1.9 collective-permute-start.6
  35.3 9.2 %collective-permute-start.9 = (bf16[176,2048]{1,0:T(8,128)(2,1)S(1)}, bf16[176,2048]{1,0:T(8,128)(2,1)S(1)}, u32[]{:S(2)}, u32[]{:S(2)}) collective-permute-start(bf16[176,2048]{1,0:T(8,128)(2,1)S(1)} %collective-permute-done.4), channel_id=1, source_target_pairs={{0,0},{2,4},{4,2},{6,6},{128,130},{130,134},{132,128},{134,132},{2... | collective-permute-start | bytes 2162696 | tf_op jit(solution)/shard_map/ppermute | solution.py:275
  44.5 14.3 %collective-permute-start.3 = (bf16[176,2048]{1,0:T(8,128)(2,1)S(1)}, bf16[176,2048]{1,0:T(8,128)(2,1)S(1)}, u32[]{:S(2)}, u32[]{:S(2)}) collective-permute-start(bf16[176,2048]{1,0:T(8,128)(2,1)S(1)} %collective-permute-done.2), channel_id=1, source_target_pairs={{0,0},{2,4},{4,2},{6,6},{128,130},{130,134},{132,128},{134,132},{2... | collective-permute-start | bytes 2162696 | tf_op jit(solution)/shard_map/ppermute | solution.py:275
  58.8 2.1 collective-permute-start.11
  60.9 13.2 %collective-permute-start.13 = (bf16[176,2048]{1,0:T(8,128)(2,1)S(1)}, bf16[176,2048]{1,0:T(8,128)(2,1)S(1)}, u32[]{:S(2)}, u32[]{:S(2)}) collective-permute-start(bf16[176,2048]{1,0:T(8,128)(2,1)S(1)} %collective-permute-done.9.refs_8_), channel_id=1, source_target_pairs={{0,384},{128,0},{256,128},{384,256},{1,385},{129,1},{257,129},{385... | collective-permute-start | bytes 2162696 | tf_op jit(solution)/shard_map/ppermute | solution.py:277
  74.0 1.9 collective-permute-start.10
  76.0 12.8 %collective-permute-start.12 = (bf16[176,2048]{1,0:T(8,128)(2,1)S(1)}, bf16[176,2048]{1,0:T(8,128)(2,1)}, u32[]{:S(2)}, u32[]{:S(2)}) collective-permute-start(bf16[176,2048]{1,0:T(8,128)(2,1)S(1)} %collective-permute-done.3.refs_4_), channel_id=1, source_target_pairs={{0,384},{128,0},{256,128},{384,256},{1,385},{129,1},{257,129},{385... | collective-permute-start | bytes 2162696 | tf_op jit(solution)/shard_map/ppermute | solution.py:277
  89.8 1.9 collective-permute-start.7
  92.5 1.9 collective-permute-start.8
  94.6 1.7 copy.19
  98.1 6.6 %attend.1 = (bf16[128,2048]{1,0:T(8,128)(2,1)S(1)}, bf16[3072,128]{1,0:T(8,128)(2,1)S(1)}) custom-call(s32[1]{0:T(128)S(6)} %copy.20.source, bf16[128,2048]{1,0:T(8,128)(2,1)S(1)} %copy-done.17, bf16[2,128,2048]{2,1,0:T(8,128)(2,1)S(1)} %bitcast.16, bf16[2,128,2048]{2,1,0:T(8,128)(2,1)S(1)} %copy-done.13, bf16[2,128,2048]{2,1,0:T(8,128)(2,1)S(1)} %copy-done.15, ...), custom_call_target="tpu_custom_call" | custom-call | flops 268435456 | bytes 2621440 | tf_op jit(solution)/shard_map/attend/pallas_call | solution.py:127
  105.5 4.1 %collective-permute-done.12.refs_6_ = bf16[176,2048]{1,0:T(8,128)(2,1)} collective-permute-done((bf16[176,2048]{1,0:T(8,128)(2,1)S(1)}, bf16[176,2048]{1,0:T(8,128)(2,1)}, u32[]{:S(2)}, u32[]{:S(2)}) %collective-permute-start.12) | collective-permute-done | bytes 720928 | tf_op jit(solution)/shard_map/ppermute | solution.py:277
  110.8 13.6 %collective-permute-done.8.refs_5_ = bf16[176,2048]{1,0:T(8,128)(2,1)} collective-permute-done((bf16[176,2048]{1,0:T(8,128)(2,1)S(1)}, bf16[176,2048]{1,0:T(8,128)(2,1)}, u32[]{:S(2)}, u32[]{:S(2)}) %collective-permute-start.8) | collective-permute-done | bytes 720928 | tf_op jit(solution)/shard_map/ppermute | solution.py:276
  124.4 35.6 %all-to-all-start = ((bf16[64,48,128]{2,1,0:T(8,128)(2,1)}), bf16[64,48,128]{2,1,0:T(8,128)(2,1)S(1)}, u32[]{:S(2)}, u32[]{:S(2)}) async-start(bf16[64,48,128]{2,1,0:T(8,128)(2,1)} %bitcast.20), calls=%async_computation | async-start | bytes 1572864 | tf_op jit(solution)/shard_map/all_to_all | solution.py:294
  160.1 4.7 %collective-permute-start.14 = (bf16[176,2048]{1,0:T(8,128)(2,1)}, bf16[176,2048]{1,0:T(8,128)(2,1)S(1)}, u32[]{:S(2)}, u32[]{:S(2)}) collective-permute-start(bf16[176,2048]{1,0:T(8,128)(2,1)} %copy-done), channel_id=1, source_target_pairs={{0,384},{128,0},{256,128},{384,256},{1,385},{129,1},{257,129},{385... | collective-permute-start | bytes 2162696 | tf_op jit(solution)/shard_map/ppermute | solution.py:278
  164.8 2.5 collective-permute-start.15
  167.3 2.4 collective-permute-start.16
  169.7 12.8 %collective-permute-done.14.refs_3_ = bf16[176,2048]{1,0:T(8,128)(2,1)S(1)} collective-permute-done((bf16[176,2048]{1,0:T(8,128)(2,1)}, bf16[176,2048]{1,0:T(8,128)(2,1)S(1)}, u32[]{:S(2)}, u32[]{:S(2)}) %collective-permute-start.14) | collective-permute-done | bytes 720928 | tf_op jit(solution)/shard_map/ppermute | solution.py:278
  183.3 14.6 %collective-permute-done.15.refs_7_ = bf16[176,2048]{1,0:T(8,128)(2,1)S(1)} collective-permute-done((bf16[176,2048]{1,0:T(8,128)(2,1)}, bf16[176,2048]{1,0:T(8,128)(2,1)S(1)}, u32[]{:S(2)}, u32[]{:S(2)}) %collective-permute-start.15) | collective-permute-done | bytes 720928 | tf_op jit(solution)/shard_map/ppermute | solution.py:278
  198.8 12.8 %collective-permute-done.16.refs_11_ = bf16[176,2048]{1,0:T(8,128)(2,1)S(1)} collective-permute-done((bf16[176,2048]{1,0:T(8,128)(2,1)}, bf16[176,2048]{1,0:T(8,128)(2,1)S(1)}, u32[]{:S(2)}, u32[]{:S(2)}) %collective-permute-start.16) | collective-permute-done | bytes 720928 | tf_op jit(solution)/shard_map/ppermute | solution.py:278
  212.5 1.9 collective-permute-start.17
  214.4 2.3 collective-permute-done.17.arrived
  222.2 5.3 %partner_experts.1 = bf16[3072,128]{1,0:T(8,128)(2,1)S(1)} custom-call(bf16[3072,128]{1,0:T(8,128)(2,1)S(1)} %collective-permute-done.17.arrived, bf16[176,2048]{1,0:T(8,128)(2,1)S(1)} %collective-permute-done.1.refs_0_, bf16[176,2048]{1,0:T(8,128)(2,1)} %collective-permute-done.7.refs_1_, bf16[176,2048]{1,0:T(8,128)(2,1)S(1)} %copy-done.1, ...), custom_call_target="tpu_custom_call" | custom-call | flops 1660944384 | bytes 8650752 | tf_op jit(solution)/shard_map/partner_experts/pallas_call | solution.py:186
  227.5 2.2 collective-permute-start.18
  229.7 5.2 %own_experts.1 = bf16[3072,128]{1,0:T(8,128)(2,1)S(1)} custom-call(bf16[3072,128]{1,0:T(8,128)(2,1)S(1)} %bitcast.18, bf16[176,2048]{1,0:T(8,128)(2,1)S(1)} %collective-permute-done.1.refs_0_, bf16[176,2048]{1,0:T(8,128)(2,1)} %collective-permute-done.7.refs_1_, bf16[176,2048]{1,0:T(8,128)(2,1)S(1)} %copy-done.1, bf16[176,2048]{1,0:T(8,128)(2,1)S(1)} %copy-done.6, ...), custom_call_target="tpu_custom_call" | custom-call | flops 1660944384 | bytes 8650752 | tf_op jit(solution)/shard_map/own_experts/pallas_call | solution.py:186
  236.0 15.0 %all-to-all-start.1 = ((bf16[64,48,128]{2,1,0:T(8,128)(2,1)}), bf16[64,48,128]{2,1,0:T(8,128)(2,1)S(1)}, u32[]{:S(2)}, u32[]{:S(2)}) async-start(bf16[64,48,128]{2,1,0:T(8,128)(2,1)} %bitcast.9), calls=%async_computation.1 | async-start | bytes 1572864 | tf_op jit(solution)/shard_map/all_to_all | solution.py:299
  251.1 43.4 %all-to-all-done.1 = bf16[64,48,128]{2,1,0:T(8,128)(2,1)S(1)} async-done(((bf16[64,48,128]{2,1,0:T(8,128)(2,1)}), bf16[64,48,128]{2,1,0:T(8,128)(2,1)S(1)}, u32[]{:S(2)}, u32[]{:S(2)}) %all-to-all-start.1) | async-done | bytes 786464 | tf_op jit(solution)/shard_map/all_to_all | solution.py:299
  294.5 1.9 combine.1
  (65 shorter events, 18.5 us)
Async XLA Ops:
  0.0 7.0 %copy-start.21 = (bf16[176,2048]{1,0:T(8,128)(2,1)S(1)}, bf16[176,2048]{1,0:T(8,128)(2,1)}, u32[]{:S(2)}) copy-start(bf16[176,2048]{1,0:T(8,128)(2,1)} %param.19) | copy-start | bytes 2162692
  0.0 7.7 %copy-start.22 = (bf16[2048,176]{0,1:T(8,128)(2,1)S(1)}, bf16[2048,176]{0,1:T(8,128)(2,1)}, u32[]{:S(2)}) copy-start(bf16[2048,176]{0,1:T(8,128)(2,1)} %param.18) | copy-start | bytes 2162692
  0.0 94.5 %copy-start.19 = (s32[128,1]{0,1:T(1,128)S(1)}, s32[128,1]{0,1:T(1,128)}, u32[]{:S(2)}) copy-start(s32[128,1]{0,1:T(1,128)} %param.14) | copy-start | bytes 1540
  0.0 8.4 %collective-permute-start = (bf16[176,2048]{1,0:T(8,128)(2,1)}, bf16[176,2048]{1,0:T(8,128)(2,1)S(1)}, u32[]{:S(2)}, u32[]{:S(2)}) collective-permute-start(bf16[176,2048]{1,0:T(8,128)(2,1)} %bitcast.25), channel_id=1, source_target_pairs={{0,0},{258,2},{132,4},{390,6},{128,128},{386,130},{4,132},{262,134... | collective-permute-start | bytes 2162696 | tf_op jit(solution)/shard_map/ppermute | solution.py:272
  3.5 28.9 %collective-permute-start.5 = (bf16[2,128,2048]{2,1,0:T(8,128)(2,1)S(1)}, bf16[2,128,2048]{2,1,0:T(8,128)(2,1)S(1)}, u32[]{:S(2)}, u32[]{:S(2)}) collective-permute-start(bf16[2,128,2048]{2,1,0:T(8,128)(2,1)S(1)} %bitcast.24), channel_id=1, source_target_pairs={{0,32},{32,64},{64,96},{96,128},{128,160},{160,192},{192,224},{224... | collective-permute-start | bytes 3145736 | tf_op jit(solution)/shard_map/ppermute | solution.py:252
  7.0 28.3 %collective-permute-start.4 = (bf16[176,2048]{1,0:T(8,128)(2,1)S(1)}, bf16[176,2048]{1,0:T(8,128)(2,1)S(1)}, u32[]{:S(2)}, u32[]{:S(2)}) collective-permute-start(bf16[176,2048]{1,0:T(8,128)(2,1)S(1)} %copy-done.21), channel_id=1, source_target_pairs={{0,0},{258,2},{132,4},{390,6},{128,128},{386,130},{4,132},{262,134... | collective-permute-start | bytes 2162696 | tf_op jit(solution)/shard_map/ppermute | solution.py:272
  7.7 36.7 %collective-permute-start.2 = (bf16[176,2048]{1,0:T(8,128)(2,1)S(1)}, bf16[176,2048]{1,0:T(8,128)(2,1)S(1)}, u32[]{:S(2)}, u32[]{:S(2)}) collective-permute-start(bf16[176,2048]{1,0:T(8,128)(2,1)S(1)} %bitcast.26), channel_id=1, source_target_pairs={{0,0},{258,2},{132,4},{390,6},{128,128},{386,130},{4,132},{262,134... | collective-permute-start | bytes 2162696 | tf_op jit(solution)/shard_map/ppermute | solution.py:272
  8.4 50.3 %collective-permute-start.1 = (bf16[176,2048]{1,0:T(8,128)(2,1)S(1)}, bf16[176,2048]{1,0:T(8,128)(2,1)S(1)}, u32[]{:S(2)}, u32[]{:S(2)}) collective-permute-start(bf16[176,2048]{1,0:T(8,128)(2,1)S(1)} %collective-permute-done), channel_id=1, source_target_pairs={{0,0},{2,4},{4,2},{6,6},{128,130},{130,134},{132,128},{134,132},{2... | collective-permute-start | bytes 2162696 | tf_op jit(solution)/shard_map/ppermute | solution.py:275
  32.4 56.4 %collective-permute-start.6 = (bf16[2,128,2048]{2,1,0:T(8,128)(2,1)S(1)}, bf16[2,128,2048]{2,1,0:T(8,128)(2,1)S(1)}, u32[]{:S(2)}, u32[]{:S(2)}) collective-permute-start(bf16[2,128,2048]{2,1,0:T(8,128)(2,1)S(1)} %collective-permute-done.5.near), channel_id=1, source_target_pairs={{0,32},{32,64},{64,96},{96,128},{128,160},{160,192},{192,224},{224... | collective-permute-start | bytes 3145736 | tf_op jit(solution)/shard_map/ppermute | solution.py:252
  35.3 25.6 %collective-permute-start.9 = (bf16[176,2048]{1,0:T(8,128)(2,1)S(1)}, bf16[176,2048]{1,0:T(8,128)(2,1)S(1)}, u32[]{:S(2)}, u32[]{:S(2)}) collective-permute-start(bf16[176,2048]{1,0:T(8,128)(2,1)S(1)} %collective-permute-done.4), channel_id=1, source_target_pairs={{0,0},{2,4},{4,2},{6,6},{128,130},{130,134},{132,128},{134,132},{2... | collective-permute-start | bytes 2162696 | tf_op jit(solution)/shard_map/ppermute | solution.py:275
  44.5 31.5 %collective-permute-start.3 = (bf16[176,2048]{1,0:T(8,128)(2,1)S(1)}, bf16[176,2048]{1,0:T(8,128)(2,1)S(1)}, u32[]{:S(2)}, u32[]{:S(2)}) collective-permute-start(bf16[176,2048]{1,0:T(8,128)(2,1)S(1)} %collective-permute-done.2), channel_id=1, source_target_pairs={{0,0},{2,4},{4,2},{6,6},{128,130},{130,134},{132,128},{134,132},{2... | collective-permute-start | bytes 2162696 | tf_op jit(solution)/shard_map/ppermute | solution.py:275
  58.8 32.9 %collective-permute-start.11 = (bf16[176,2048]{1,0:T(8,128)(2,1)S(1)}, bf16[176,2048]{1,0:T(8,128)(2,1)S(1)}, u32[]{:S(2)}, u32[]{:S(2)}) collective-permute-start(bf16[176,2048]{1,0:T(8,128)(2,1)S(1)} %collective-permute-done.1.refs_0_), channel_id=1, source_target_pairs={{0,384},{128,0},{256,128},{384,256},{1,385},{129,1},{257,129},{385... | collective-permute-start | bytes 2162696 | tf_op jit(solution)/shard_map/ppermute | solution.py:277
  60.9 48.7 %collective-permute-start.13 = (bf16[176,2048]{1,0:T(8,128)(2,1)S(1)}, bf16[176,2048]{1,0:T(8,128)(2,1)S(1)}, u32[]{:S(2)}, u32[]{:S(2)}) collective-permute-start(bf16[176,2048]{1,0:T(8,128)(2,1)S(1)} %collective-permute-done.9.refs_8_), channel_id=1, source_target_pairs={{0,384},{128,0},{256,128},{384,256},{1,385},{129,1},{257,129},{385... | collective-permute-start | bytes 2162696 | tf_op jit(solution)/shard_map/ppermute | solution.py:277
  74.0 35.6 %collective-permute-start.10 = (bf16[176,2048]{1,0:T(8,128)(2,1)S(1)}, bf16[176,2048]{1,0:T(8,128)(2,1)}, u32[]{:S(2)}, u32[]{:S(2)}) collective-permute-start(bf16[176,2048]{1,0:T(8,128)(2,1)S(1)} %collective-permute-done.9.refs_8_), channel_id=1, source_target_pairs={{0,128},{128,256},{256,384},{384,0},{1,129},{129,257},{257,385},{3... | collective-permute-start | bytes 2162696 | tf_op jit(solution)/shard_map/ppermute | solution.py:276
  76.0 33.6 %collective-permute-start.12 = (bf16[176,2048]{1,0:T(8,128)(2,1)S(1)}, bf16[176,2048]{1,0:T(8,128)(2,1)}, u32[]{:S(2)}, u32[]{:S(2)}) collective-permute-start(bf16[176,2048]{1,0:T(8,128)(2,1)S(1)} %collective-permute-done.3.refs_4_), channel_id=1, source_target_pairs={{0,384},{128,0},{256,128},{384,256},{1,385},{129,1},{257,129},{385... | collective-permute-start | bytes 2162696 | tf_op jit(solution)/shard_map/ppermute | solution.py:277
  89.8 21.1 %collective-permute-start.7 = (bf16[176,2048]{1,0:T(8,128)(2,1)S(1)}, bf16[176,2048]{1,0:T(8,128)(2,1)}, u32[]{:S(2)}, u32[]{:S(2)}) collective-permute-start(bf16[176,2048]{1,0:T(8,128)(2,1)S(1)} %collective-permute-done.1.refs_0_), channel_id=1, source_target_pairs={{0,128},{128,256},{256,384},{384,0},{1,129},{129,257},{257,385},{3... | collective-permute-start | bytes 2162696 | tf_op jit(solution)/shard_map/ppermute | solution.py:276
  92.5 31.9 %collective-permute-start.8 = (bf16[176,2048]{1,0:T(8,128)(2,1)S(1)}, bf16[176,2048]{1,0:T(8,128)(2,1)}, u32[]{:S(2)}, u32[]{:S(2)}) collective-permute-start(bf16[176,2048]{1,0:T(8,128)(2,1)S(1)} %collective-permute-done.3.refs_4_), channel_id=1, source_target_pairs={{0,128},{128,256},{256,384},{384,0},{1,129},{129,257},{257,385},{3... | collective-permute-start | bytes 2162696 | tf_op jit(solution)/shard_map/ppermute | solution.py:276
  94.5 2.5 copy-start.18
  94.6 2.4 copy-start.13
  94.6 2.4 copy-start.15
  109.6 14.8 %copy-start.2 = (bf16[176,2048]{1,0:T(8,128)(2,1)}, bf16[176,2048]{1,0:T(8,128)(2,1)S(1)}, u32[]{:S(2)}) copy-start(bf16[176,2048]{1,0:T(8,128)(2,1)S(1)} %collective-permute-done.13.refs_10_) | copy-start | bytes 2162692
  124.4 88.0 %all-to-all-start = ((bf16[64,48,128]{2,1,0:T(8,128)(2,1)}), bf16[64,48,128]{2,1,0:T(8,128)(2,1)S(1)}, u32[]{:S(2)}, u32[]{:S(2)}) async-start(bf16[64,48,128]{2,1,0:T(8,128)(2,1)} %bitcast.20), calls=%async_computation | async-start | bytes 1572864 | tf_op jit(solution)/shard_map/all_to_all | solution.py:294
  160.1 22.4 %collective-permute-start.14 = (bf16[176,2048]{1,0:T(8,128)(2,1)}, bf16[176,2048]{1,0:T(8,128)(2,1)S(1)}, u32[]{:S(2)}, u32[]{:S(2)}) collective-permute-start(bf16[176,2048]{1,0:T(8,128)(2,1)} %copy-done), channel_id=1, source_target_pairs={{0,384},{128,0},{256,128},{384,256},{1,385},{129,1},{257,129},{385... | collective-permute-start | bytes 2162696 | tf_op jit(solution)/shard_map/ppermute | solution.py:278
  164.8 33.1 %collective-permute-start.15 = (bf16[176,2048]{1,0:T(8,128)(2,1)}, bf16[176,2048]{1,0:T(8,128)(2,1)S(1)}, u32[]{:S(2)}, u32[]{:S(2)}) collective-permute-start(bf16[176,2048]{1,0:T(8,128)(2,1)} %collective-permute-done.12.refs_6_), channel_id=1, source_target_pairs={{0,384},{128,0},{256,128},{384,256},{1,385},{129,1},{257,129},{385... | collective-permute-start | bytes 2162696 | tf_op jit(solution)/shard_map/ppermute | solution.py:278
  167.3 44.3 %collective-permute-start.16 = (bf16[176,2048]{1,0:T(8,128)(2,1)}, bf16[176,2048]{1,0:T(8,128)(2,1)S(1)}, u32[]{:S(2)}, u32[]{:S(2)}) collective-permute-start(bf16[176,2048]{1,0:T(8,128)(2,1)} %copy-done.2), channel_id=1, source_target_pairs={{0,384},{128,0},{256,128},{384,256},{1,385},{129,1},{257,129},{385... | collective-permute-start | bytes 2162696 | tf_op jit(solution)/shard_map/ppermute | solution.py:278
  212.5 4.2 %collective-permute-start.17 = (bf16[3072,128]{1,0:T(8,128)(2,1)S(1)}, bf16[3072,128]{1,0:T(8,128)(2,1)S(1)}, u32[]{:S(2)}, u32[]{:S(2)}) collective-permute-start(bf16[3072,128]{1,0:T(8,128)(2,1)S(1)} %bitcast.17), channel_id=1, source_target_pairs={{0,1},{1,0},{2,3},{3,2},{4,5},{5,4},{6,7},{7,6},{8,9},{9,8},{10,11... | collective-permute-start | bytes 2359304 | tf_op jit(solution)/shard_map/ppermute | solution.py:248
  216.6 1.1 copy-start.1
  222.2 7.5 %copy-start.6 = (bf16[176,2048]{1,0:T(8,128)(2,1)S(1)}, bf16[176,2048]{1,0:T(8,128)(2,1)}, u32[]{:S(2)}) copy-start(bf16[176,2048]{1,0:T(8,128)(2,1)} %copy-done.4) | copy-start | bytes 2162692
  222.2 7.5 %copy-start.9 = (bf16[176,2048]{1,0:T(8,128)(2,1)S(1)}, bf16[176,2048]{1,0:T(8,128)(2,1)}, u32[]{:S(2)}) copy-start(bf16[176,2048]{1,0:T(8,128)(2,1)} %copy-done.7) | copy-start | bytes 2162692
  227.5 7.4 %collective-permute-start.18 = (bf16[3072,128]{1,0:T(8,128)(2,1)S(1)}, bf16[3072,128]{1,0:T(8,128)(2,1)S(1)}, u32[]{:S(2)}, u32[]{:S(2)}) collective-permute-start(bf16[3072,128]{1,0:T(8,128)(2,1)S(1)} %partner_experts.1), channel_id=1, source_target_pairs={{0,1},{1,0},{2,3},{3,2},{4,5},{5,4},{6,7},{7,6},{8,9},{9,8},{10,11... | collective-permute-start | bytes 2359304 | tf_op jit(solution)/shard_map/ppermute | solution.py:248
  236.0 15.0 %copy-start.20 = (f32[128,1]{0,1:T(1,128)S(1)}, f32[128,1]{0,1:T(1,128)}, u32[]{:S(2)}) copy-start(f32[128,1]{0,1:T(1,128)} %param.15) | copy-start | bytes 1540
  236.0 58.5 %all-to-all-start.1 = ((bf16[64,48,128]{2,1,0:T(8,128)(2,1)}), bf16[64,48,128]{2,1,0:T(8,128)(2,1)S(1)}, u32[]{:S(2)}, u32[]{:S(2)}) async-start(bf16[64,48,128]{2,1,0:T(8,128)(2,1)} %bitcast.9), calls=%async_computation.1 | async-start | bytes 1572864 | tf_op jit(solution)/shard_map/all_to_all | solution.py:299
  (12 other events, 11.8 us)

commit v4 on v2

--- a/solution.py
+++ b/solution.py
@@ -1,3 +1,4 @@
+import functools
 import math
 
 import jax
@@ -12,7 +13,7 @@
 HEADS = 16
 MOST = 3
 LANES = 128
-VMEM_BYTES = 32 * 1024 * 1024
+VMEM_BYTES = 16 * 1024 * 1024
 
 PLACE = ((0, 2, 1, 3), (1, 3, 0, 2), (2, 0, 3, 1), (3, 1, 2, 0))
 
@@ -151,60 +152,78 @@
     )(source, queries, own, near, far, chosen, chosen.reshape(1, tokens), gain)
 
 
-def experts_kernel(arrived, *refs):
-    gates, ups, downs, (out, rows, tokens) = refs[:4], refs[4:8], refs[8:13], refs[13:]
-    count, features = tokens.shape
+def experts_kernel(pieces, arrived, partner, *refs):
+    sources = refs[: len(pieces)]
+    out, lent, gate, up, down, rows, tokens, sems = refs[len(pieces) :]
+    copies = ([], [], [])
+    for number, (source, (matrix, row, column)) in enumerate(zip(sources, pieces)):
+        units, width = source.shape
+        target = (gate, up, down)[matrix].at[pl.ds(row, units), pl.ds(column, width)]
+        copy = pltpu.make_async_copy(source, target, sems.at[number])
+        copy.start()
+        copies[matrix].append(copy)
+    count, features = tokens.shape[0] // 2, tokens.shape[1]
     blocks = features // LANES
-    rows[...] = arrived[...].astype(jnp.float32)
-    for block in range(blocks):
-        tokens[:, block * LANES : (block + 1) * LANES] = rows[
-            pl.ds(block, count, stride=blocks), :
-        ].astype(jnp.bfloat16)
+    for half, block_rows in enumerate((arrived, partner)):
+        rows[half] = block_rows[...].astype(jnp.float32)
+        for block in range(blocks):
+            tokens[half * count : (half + 1) * count, block * LANES : (block + 1) * LANES] = rows[
+                half, pl.ds(block, count, stride=blocks), :
+            ].astype(jnp.bfloat16)
+    for copy in copies[0] + copies[1]:
+        copy.wait()
     transposed = (((1,), (1,)), ((), ()))
-    acts = []
-    for gate, up in zip(gates, ups):
-        gated = lax.dot_general(
-            tokens[...], gate[...], transposed, preferred_element_type=jnp.float32
-        )
-        raised = lax.dot_general(
-            tokens[...], up[...], transposed, preferred_element_type=jnp.float32
-        )
-        acts.append((gated / (1.0 + jnp.exp(-gated)) * raised).astype(jnp.bfloat16))
-    middle = features // 2
-    for half in range(2):
-        at = slice(half * middle, (half + 1) * middle)
-        made = jnp.dot(acts[3], downs[3 + half][...], preferred_element_type=jnp.float32)
-        for act, down in zip(acts[:3], downs[:3]):
-            made += jnp.dot(act, down[:, at], preferred_element_type=jnp.float32)
-        for block in range(blocks // 2):
-            rows[pl.ds(half * (blocks // 2) + block, count, stride=blocks), :] = made[
+    gated = lax.dot_general(
+        tokens[...], gate[...], transposed, preferred_element_type=jnp.float32
+    )
+    raised = lax.dot_general(tokens[...], up[...], transposed, preferred_element_type=jnp.float32)
+    act = (gated / (1.0 + jnp.exp(-gated)) * raised).astype(jnp.bfloat16)
+    for copy in copies[2]:
+        copy.wait()
+    for half, target in ((1, lent), (0, out)):
+        made = jnp.dot(
+            act[half * count : (half + 1) * count], down[...], preferred_element_type=jnp.float32
+        )
+        for block in range(blocks):
+            rows[half, pl.ds(block, count, stride=blocks), :] = made[
                 :, block * LANES : (block + 1) * LANES
             ]
-    out[...] = rows[...].astype(jnp.bfloat16)
-
-
-def experts(arrived, weights, name):
-    gates, ups, downs = weights
-    units, features = gates[0].shape
+        target[...] = rows[half].astype(jnp.bfloat16)
+
+
+def experts(arrived, partner, weights):
+    features = weights[0][0].shape[1]
     count = arrived.shape[0] * arrived.shape[1] // features
+    pieces, flat, units = [], [], 0
+    for matrix, parts in enumerate(weights):
+        row, column = 0, 0
+        for part in parts:
+            flat.append(part)
+            pieces.append((matrix, row, column))
+            column += part.shape[1]
+            if column == features:
+                row, column = row + part.shape[0], 0
+        units = row
     vmem = pl.BlockSpec(memory_space=pltpu.VMEM)
     return pl.pallas_call(
-        experts_kernel,
-        out_shape=jax.ShapeDtypeStruct(arrived.shape, jnp.bfloat16),
-        in_specs=[vmem] * (1 + len(gates) + len(ups) + len(downs)),
-        out_specs=vmem,
-        scratch_shapes=[
-            pltpu.VMEM(arrived.shape, jnp.float32),
-            pltpu.VMEM((count, features), jnp.bfloat16),
+        functools.partial(experts_kernel, pieces),
+        out_shape=(jax.ShapeDtypeStruct(arrived.shape, jnp.bfloat16),) * 2,
+        in_specs=[vmem] * 2 + [pl.BlockSpec(memory_space=pl.ANY)] * len(flat),
+        out_specs=(vmem,) * 2,
+        scratch_shapes=[pltpu.VMEM((units, features), jnp.bfloat16)] * 3
+        + [
+            pltpu.VMEM((2, *arrived.shape), jnp.float32),
+            pltpu.VMEM((2 * count, features), jnp.bfloat16),
+            pltpu.SemaphoreType.DMA((len(flat),)),
         ],
-        compiler_params=pltpu.CompilerParams(vmem_limit_bytes=VMEM_BYTES),
+        compiler_params=pltpu.CompilerParams(vmem_limit_bytes=2 * VMEM_BYTES),
         cost_estimate=pl.CostEstimate(
-            flops=6 * count * features * units * 4,
-            bytes_accessed=6 * units * 4 * features,
-            transcendentals=count * units * 4,
+            flops=12 * count * features * units,
+            bytes_accessed=6 * units * features,
+            transcendentals=2 * count * units,
         ),
-        name=name,
-    )(arrived, *gates, *ups, *downs)
+        name="experts",
+    )(arrived, partner, *flat)
 
 
 def combine_kernel(returned, hidden, chosen_column, chosen_row, weight, out, rows, outputs):
@@ -278,6 +297,16 @@
         for matrix in (gate_matrix.T, up_matrix.T, down_matrix)
     ]
     placed = [lax.ppermute(matrix, ("x", "p"), lift_pairs()) for matrix in moved]
+    hidden, packed = attend(
+        memory_source,
+        after(queries, *moved),
+        key_value.transpose(1, 0, 2),
+        near,
+        far,
+        routing,
+        norm_gain.reshape(1, features),
+    )
+    packed, *placed = lax.optimization_barrier((packed, *placed))
     left = [lax.ppermute(matrix, "x", ring(1)) for matrix in placed]
     right = [lax.ppermute(matrix, "x", ring(-1)) for matrix in placed]
     middle = features // 2
@@ -293,22 +322,11 @@
         [own, before, behind, *beyond]
         for own, before, behind, beyond in zip(placed, left, right, across)
     ]
-    hidden, packed = attend(
-        memory_source,
-        after(queries, placed[0], placed[1], moved[2]),
-        key_value.transpose(1, 0, 2),
-        near,
-        far,
-        routing,
-        norm_gain.reshape(1, features),
-    )
-    packed = after(packed, left[0], right[0], placed[2], left[1], right[1])
     chunks = packed.reshape(64, -1, LANES)
     arrived = lax.all_to_all(chunks, ("y", "s", "p"), 0, 0, tiled=True).reshape(packed.shape)
-    partner = swapped(after(arrived, across[0], across[1], across[2]))
-    lent = swapped(experts(partner, weights, "partner_experts"))
-    made = experts(arrived, weights, "own_experts")
-    made = (made.astype(jnp.float32) + lent.astype(jnp.float32)).astype(jnp.bfloat16)
+    partner = swapped(after(arrived, *sum(weights, [])))
+    made, lent = experts(arrived, partner, weights)
+    made = (made.astype(jnp.float32) + swapped(lent).astype(jnp.float32)).astype(jnp.bfloat16)
     returned = lax.all_to_all(made.reshape(chunks.shape), ("y", "s", "p"), 0, 0, tiled=True)
     return combine(returned.reshape(packed.shape), hidden, routing, router_weight)
 

time: 317 us -> 313 us (0.987)
  starting transfers between devices: 194 us -> 170 us
  waiting for transfers between devices: 81.5 us -> 103 us
    all_to_all x1, starting transfers between devices: 83.3 us -> 58.8 us  [per_device(): lax.all_to_all(chunks, ('y', 's', 'p'), 0, 0, tiled=True)]
    ppermute x3, starting transfers between devices: 43.6 us -> 27.1 us  [per_device(): lax.ppermute(matrix, ('x', 'p'), lift_pairs())]
    ppermute x3, starting transfers between devices: 5.17 us -> 20.7 us  [per_device(): lax.ppermute(matrix, ('x', 'p'), spread_pairs())]
    ppermute x2, waiting for transfers between devices: 0.01 us -> 15 us  [passed_along(): lax.ppermute(block, ('x', 'y'), [(i, (i + by) % 16) for i in range(16)])]
    ppermute x1, waiting for transfers between devices: 12 us -> 16.5 us  [per_device(): lax.ppermute(left[2][:, :middle], 'x', ring(1))]
    ppermute x1, waiting for transfers between devices: 5.33 us -> 2.12 us  [per_device(): lax.ppermute(right[2][:, middle:], 'x', ring(-1))]
    unnamed x60 -> x42, local copies, waits for them, and re-layouts: 18.2 us -> 15 us
    pallas_call x2 -> x1, Pallas kernels: 10.2 us -> 8.64 us  [experts(): pl.pallas_call(functools.partial(experts_kernel, pieces), out_shape=(jax....]
  transfers between devices with their start and end apart: 22 -> 22, of which waited for: 6 -> 10; matrix products, arithmetic and copies ran while one was open for 1% -> 1% of each run, Pallas kernels for 4% -> 2%
where the time goes in v4:
time: 313 us; the launch traced here: 308 us
  starting transfers between devices  170 us (54%)
  waiting for transfers between devices  103 us (33%)
  Pallas kernels  17.9 us (6%)
  local copies, waits for them, and re-layouts  15.1 us (5%)
    all_to_all x1, starting transfers between devices, per_device(): lax.all_to_all(chunks, ('y', 's', 'p'), 0, 0, tiled=True)  58.8 us
    all_to_all x1, waiting for transfers between devices, per_device(): lax.all_to_all(made.reshape(chunks.shape), ('y', 's', 'p'), 0, 0, tiled=T...  43.1 us
    ppermute x3, starting transfers between devices, per_device(): lax.ppermute(matrix, ('x', 'p'), lift_pairs())  27.1 us
    ppermute x3, waiting for transfers between devices, per_device(): left = [lax.ppermute(matrix, 'x', ring(1)) for matrix in placed]  21 us
    ppermute x3, starting transfers between devices, per_device(): lax.ppermute(matrix, ('x', 'p'), spread_pairs())  20.7 us
    ppermute x1, waiting for transfers between devices, per_device(): lax.ppermute(left[2][:, :middle], 'x', ring(1))  16.5 us
    unnamed x42, local copies, waits for them, and re-layouts  15 us
    all_to_all x1, starting transfers between devices, per_device(): lax.all_to_all(made.reshape(chunks.shape), ('y', 's', 'p'), 0, 0, tiled=T...  15 us
  transfers between devices with their start and end apart: 22, of which 10 were waited for; matrix products, arithmetic and copies ran while one was open for 1% of the time, Pallas kernels for 2%

profile of v4, /device:TPU:6, one launch (start us, length us, event | category | flops | bytes accessed | tf_op | source)
XLA Modules:
  0.0 307.9 jit_solution(8353271388975756473)
XLA Ops:
  0.0 6.8 %collective-permute-start = (bf16[176,2048]{1,0:T(8,128)(2,1)}, bf16[176,2048]{1,0:T(8,128)(2,1)}, u32[]{:S(2)}, u32[]{:S(2)}) collective-permute-start(bf16[176,2048]{1,0:T(8,128)(2,1)} %bitcast.23), channel_id=1, source_target_pairs={{0,0},{258,2},{132,4},{390,6},{128,128},{386,130},{4,132},{262,134... | collective-permute-start | bytes 2162696 | tf_op jit(solution)/shard_map/ppermute | solution.py:296
  6.8 7.0 %collective-permute-start.1 = (bf16[176,2048]{1,0:T(8,128)(2,1)}, bf16[176,2048]{1,0:T(8,128)(2,1)}, u32[]{:S(2)}, u32[]{:S(2)}) collective-permute-start(bf16[176,2048]{1,0:T(8,128)(2,1)} %bitcast.24), channel_id=1, source_target_pairs={{0,0},{258,2},{132,4},{390,6},{128,128},{386,130},{4,132},{262,134... | collective-permute-start | bytes 2162696 | tf_op jit(solution)/shard_map/ppermute | solution.py:296
  13.8 6.9 %collective-permute-start.2 = (bf16[176,2048]{1,0:T(8,128)(2,1)}, bf16[176,2048]{1,0:T(8,128)(2,1)}, u32[]{:S(2)}, u32[]{:S(2)}) collective-permute-start(bf16[176,2048]{1,0:T(8,128)(2,1)} %param.19), channel_id=1, source_target_pairs={{0,0},{258,2},{132,4},{390,6},{128,128},{386,130},{4,132},{262,134... | collective-permute-start | bytes 2162696 | tf_op jit(solution)/shard_map/ppermute | solution.py:296
  20.7 2.6 copy.18
  23.3 3.5 %collective-permute-start.3 = (bf16[2,128,2048]{2,1,0:T(8,128)(2,1)}, bf16[2,128,2048]{2,1,0:T(8,128)(2,1)S(1)}, u32[]{:S(2)}, u32[]{:S(2)}) collective-permute-start(bf16[2,128,2048]{2,1,0:T(8,128)(2,1)} %bitcast.14), channel_id=1, source_target_pairs={{0,32},{32,64},{64,96},{96,128},{128,160},{160,192},{192,224},{224... | collective-permute-start | bytes 3145736 | tf_op jit(solution)/shard_map/ppermute | solution.py:276
  26.7 4.8 %collective-permute-start.4 = (bf16[2,128,2048]{2,1,0:T(8,128)(2,1)}, bf16[2,128,2048]{2,1,0:T(8,128)(2,1)S(1)}, u32[]{:S(2)}, u32[]{:S(2)}) collective-permute-start(bf16[2,128,2048]{2,1,0:T(8,128)(2,1)} %bitcast.14), channel_id=1, source_target_pairs={{0,64},{32,96},{64,128},{96,160},{128,192},{160,224},{192,256},{22... | collective-permute-start | bytes 3145736 | tf_op jit(solution)/shard_map/ppermute | solution.py:276
  33.5 10.9 %collective-permute-start.6 = (bf16[176,2048]{1,0:T(8,128)(2,1)}, bf16[176,2048]{1,0:T(8,128)(2,1)}, u32[]{:S(2)}, u32[]{:S(2)}) collective-permute-start(bf16[176,2048]{1,0:T(8,128)(2,1)} %collective-permute-done.1), channel_id=1, source_target_pairs={{0,0},{2,4},{4,2},{6,6},{128,130},{130,134},{132,128},{134,132},{2... | collective-permute-start | bytes 2162696 | tf_op jit(solution)/shard_map/ppermute | solution.py:299
  44.4 14.3 %collective-permute-start.7 = (bf16[176,2048]{1,0:T(8,128)(2,1)}, bf16[176,2048]{1,0:T(8,128)(2,1)}, u32[]{:S(2)}, u32[]{:S(2)}) collective-permute-start(bf16[176,2048]{1,0:T(8,128)(2,1)} %collective-permute-done.2), channel_id=1, source_target_pairs={{0,0},{2,4},{4,2},{6,6},{128,130},{130,134},{132,128},{134,132},{2... | collective-permute-start | bytes 2162696 | tf_op jit(solution)/shard_map/ppermute | solution.py:299
  59.9 15.0 %collective-permute-done.3.near = bf16[2,128,2048]{2,1,0:T(8,128)(2,1)S(1)} collective-permute-done((bf16[2,128,2048]{2,1,0:T(8,128)(2,1)}, bf16[2,128,2048]{2,1,0:T(8,128)(2,1)S(1)}, u32[]{:S(2)}, u32[]{:S(2)}) %collective-permute-start.3) | collective-permute-done | bytes 1048608 | tf_op jit(solution)/shard_map/ppermute | solution.py:276
  74.8 7.5 %attend.1 = (bf16[128,2048]{1,0:T(8,128)(2,1)S(1)}, bf16[3072,128]{1,0:T(8,128)(2,1)}) custom-call(s32[1]{0:T(128)S(6)} %copy.20.source, bf16[128,2048]{1,0:T(8,128)(2,1)S(1)} %copy-done, bf16[2,128,2048]{2,1,0:T(8,128)(2,1)S(1)} %bitcast.16, bf16[2,128,2048]{2,1,0:T(8,128)(2,1)S(1)} %collective-permute-done.3.near, ...), custom_call_target="tpu_custom_call" | custom-call | flops 268435456 | bytes 2621440 | tf_op jit(solution)/shard_map/attend/pallas_call | solution.py:128
  83.8 58.8 %all-to-all-start = ((bf16[64,48,128]{2,1,0:T(8,128)(2,1)}), bf16[64,48,128]{2,1,0:T(8,128)(2,1)S(1)}, u32[]{:S(2)}, u32[]{:S(2)}) async-start(bf16[64,48,128]{2,1,0:T(8,128)(2,1)} %bitcast.8), calls=%async_computation | async-start | bytes 1572864 | tf_op jit(solution)/shard_map/all_to_all | solution.py:326
  142.6 3.2 %collective-permute-start.8 = (bf16[176,2048]{1,0:T(8,128)(2,1)}, bf16[176,2048]{1,0:T(8,128)(2,1)S(1)}, u32[]{:S(2)}, u32[]{:S(2)}) collective-permute-start(bf16[176,2048]{1,0:T(8,128)(2,1)} %collective-permute-done.5.refs_0_), channel_id=1, source_target_pairs={{0,128},{128,256},{256,384},{384,0},{1,129},{129,257},{257,385},{3... | collective-permute-start | bytes 2162696 | tf_op jit(solution)/shard_map/ppermute | solution.py:310
  145.9 3.3 %collective-permute-start.12 = (bf16[176,2048]{1,0:T(8,128)(2,1)}, bf16[176,2048]{1,0:T(8,128)(2,1)S(1)}, u32[]{:S(2)}, u32[]{:S(2)}) collective-permute-start(bf16[176,2048]{1,0:T(8,128)(2,1)} %collective-permute-done.6.refs_4_), channel_id=1, source_target_pairs={{0,384},{128,0},{256,128},{384,256},{1,385},{129,1},{257,129},{385... | collective-permute-start | bytes 2162696 | tf_op jit(solution)/shard_map/ppermute | solution.py:311
  149.2 3.7 %collective-permute-start.14 = (bf16[176,2048]{1,0:T(8,128)(2,1)}, bf16[176,2048]{1,0:T(8,128)(2,1)S(1)}, u32[]{:S(2)}, u32[]{:S(2)}) collective-permute-start(bf16[176,2048]{1,0:T(8,128)(2,1)} %collective-permute-done.7.refs_8_), channel_id=1, source_target_pairs={{0,128},{128,256},{256,384},{384,0},{1,129},{129,257},{257,385},{3... | collective-permute-start | bytes 2162696 | tf_op jit(solution)/shard_map/ppermute | solution.py:310
  152.9 2.1 collective-permute-start.15
  155.1 4.9 %collective-permute-start.11 = (bf16[176,2048]{1,0:T(8,128)(2,1)}, bf16[176,2048]{1,0:T(8,128)(2,1)S(1)}, u32[]{:S(2)}, u32[]{:S(2)}) collective-permute-start(bf16[176,2048]{1,0:T(8,128)(2,1)} %collective-permute-done.6.refs_4_), channel_id=1, source_target_pairs={{0,128},{128,256},{256,384},{384,0},{1,129},{129,257},{257,385},{3... | collective-permute-start | bytes 2162696 | tf_op jit(solution)/shard_map/ppermute | solution.py:310
  160.0 4.4 %collective-permute-done.8.refs_1_ = bf16[176,2048]{1,0:T(8,128)(2,1)S(1)} collective-permute-done((bf16[176,2048]{1,0:T(8,128)(2,1)}, bf16[176,2048]{1,0:T(8,128)(2,1)S(1)}, u32[]{:S(2)}, u32[]{:S(2)}) %collective-permute-start.8) | collective-permute-done | bytes 720928 | tf_op jit(solution)/shard_map/ppermute | solution.py:310
  164.5 4.0 %collective-permute-start.9 = (bf16[176,2048]{1,0:T(8,128)(2,1)}, bf16[176,2048]{1,0:T(8,128)(2,1)S(1)}, u32[]{:S(2)}, u32[]{:S(2)}) collective-permute-start(bf16[176,2048]{1,0:T(8,128)(2,1)} %collective-permute-done.5.refs_0_), channel_id=1, source_target_pairs={{0,384},{128,0},{256,128},{384,256},{1,385},{129,1},{257,129},{385... | collective-permute-start | bytes 2162696 | tf_op jit(solution)/shard_map/ppermute | solution.py:311
  168.4 3.2 %collective-permute-start.10 = (bf16[176,2048]{1,0:T(8,128)(2,1)S(1)}, bf16[176,2048]{1,0:T(8,128)(2,1)S(1)}, u32[]{:S(2)}, u32[]{:S(2)}) collective-permute-start(bf16[176,2048]{1,0:T(8,128)(2,1)S(1)} %collective-permute-done.8.refs_1_), channel_id=1, source_target_pairs={{0,128},{128,256},{256,384},{384,0},{1,129},{129,257},{257,385},{3... | collective-permute-start | bytes 2162696 | tf_op jit(solution)/shard_map/ppermute | solution.py:314
  171.6 8.3 %collective-permute-done.14.refs_9_ = bf16[176,2048]{1,0:T(8,128)(2,1)S(1)} collective-permute-done((bf16[176,2048]{1,0:T(8,128)(2,1)}, bf16[176,2048]{1,0:T(8,128)(2,1)S(1)}, u32[]{:S(2)}, u32[]{:S(2)}) %collective-permute-start.14) | collective-permute-done | bytes 720928 | tf_op jit(solution)/shard_map/ppermute | solution.py:310
  179.9 4.0 %collective-permute-start.13 = (bf16[176,2048]{1,0:T(8,128)(2,1)S(1)}, bf16[176,2048]{1,0:T(8,128)(2,1)S(1)}, u32[]{:S(2)}, u32[]{:S(2)}) collective-permute-start(bf16[176,2048]{1,0:T(8,128)(2,1)S(1)} %collective-permute-done.12.refs_6_), channel_id=1, source_target_pairs={{0,384},{128,0},{256,128},{384,256},{1,385},{129,1},{257,129},{385... | collective-permute-start | bytes 2162696 | tf_op jit(solution)/shard_map/ppermute | solution.py:315
  183.9 3.2 %collective-permute-start.16 = (bf16[176,1024]{1,0:T(8,128)(2,1)S(1)}, bf16[176,1024]{1,0:T(8,128)(2,1)S(1)}, u32[]{:S(2)}, u32[]{:S(2)}) collective-permute-start(bf16[176,1024]{1,0:T(8,128)(2,1)S(1)} %slice.8), channel_id=1, source_target_pairs={{0,128},{128,256},{256,384},{384,0},{1,129},{129,257},{257,385},{3... | collective-permute-start | bytes 1081352 | tf_op jit(solution)/shard_map/ppermute | solution.py:317
  187.1 8.2 %collective-permute-done.11.refs_5_ = bf16[176,2048]{1,0:T(8,128)(2,1)S(1)} collective-permute-done((bf16[176,2048]{1,0:T(8,128)(2,1)}, bf16[176,2048]{1,0:T(8,128)(2,1)S(1)}, u32[]{:S(2)}, u32[]{:S(2)}) %collective-permute-start.11) | collective-permute-done | bytes 720928 | tf_op jit(solution)/shard_map/ppermute | solution.py:310
  196.2 4.0 %collective-permute-start.17 = (bf16[176,1024]{1,0:T(8,128)(2,1)S(1)}, bf16[176,1024]{1,0:T(8,128)(2,1)S(1)}, u32[]{:S(2)}, u32[]{:S(2)}) collective-permute-start(bf16[176,1024]{1,0:T(8,128)(2,1)S(1)} %slice.9), channel_id=1, source_target_pairs={{0,384},{128,0},{256,128},{384,256},{1,385},{129,1},{257,129},{385... | collective-permute-start | bytes 1081352 | tf_op jit(solution)/shard_map/ppermute | solution.py:318
  201.1 16.5 %collective-permute-done.16.refs_11_ = bf16[176,1024]{1,0:T(8,128)(2,1)S(1)} collective-permute-done((bf16[176,1024]{1,0:T(8,128)(2,1)S(1)}, bf16[176,1024]{1,0:T(8,128)(2,1)S(1)}, u32[]{:S(2)}, u32[]{:S(2)}) %collective-permute-start.16) | collective-permute-done | bytes 360480 | tf_op jit(solution)/shard_map/ppermute | solution.py:317
  217.6 2.1 collective-permute-done.17.refs_12_
  222.2 2.1 collective-permute-start.18
  224.3 2.1 collective-permute-done.18.partner
  234.0 8.6 %experts.1 = (bf16[3072,128]{1,0:T(8,128)(2,1)S(1)}, bf16[3072,128]{1,0:T(8,128)(2,1)S(1)}) custom-call(bf16[3072,128]{1,0:T(8,128)(2,1)S(1)} %bitcast.19, bf16[3072,128]{1,0:T(8,128)(2,1)S(1)} %collective-permute-done.18.partner, bf16[176,2048]{1,0:T(8,128)(2,1)} %collective-permute-done.5.refs_0_, bf16[176,2048]{1,0:T(8,128)(2,1)S(1)} %copy-done.4, ...), custom_call_target="tpu_custom_call" | custom-call | flops 3321888768 | bytes 8650752 | tf_op jit(solution)/shard_map/experts/pallas_call | solution.py:208
  244.7 2.1 collective-permute-done.19
  247.9 15.0 %all-to-all-start.1 = ((bf16[64,48,128]{2,1,0:T(8,128)(2,1)}), bf16[64,48,128]{2,1,0:T(8,128)(2,1)S(1)}, u32[]{:S(2)}, u32[]{:S(2)}) async-start(bf16[64,48,128]{2,1,0:T(8,128)(2,1)} %bitcast.10), calls=%async_computation.1 | async-start | bytes 1572864 | tf_op jit(solution)/shard_map/all_to_all | solution.py:330
  263.0 43.1 %all-to-all-done.1 = bf16[64,48,128]{2,1,0:T(8,128)(2,1)S(1)} async-done(((bf16[64,48,128]{2,1,0:T(8,128)(2,1)}), bf16[64,48,128]{2,1,0:T(8,128)(2,1)S(1)}, u32[]{:S(2)}, u32[]{:S(2)}) %all-to-all-start.1) | async-done | bytes 786464 | tf_op jit(solution)/shard_map/all_to_all | solution.py:330
  (60 shorter events, 20.9 us)
Async XLA Ops:
  0.0 31.6 %collective-permute-start = (bf16[176,2048]{1,0:T(8,128)(2,1)}, bf16[176,2048]{1,0:T(8,128)(2,1)}, u32[]{:S(2)}, u32[]{:S(2)}) collective-permute-start(bf16[176,2048]{1,0:T(8,128)(2,1)} %bitcast.23), channel_id=1, source_target_pairs={{0,0},{258,2},{132,4},{390,6},{128,128},{386,130},{4,132},{262,134... | collective-permute-start | bytes 2162696 | tf_op jit(solution)/shard_map/ppermute | solution.py:296
  6.8 51.9 %copy-start.2 = (s32[128,1]{0,1:T(1,128)S(1)}, s32[128,1]{0,1:T(1,128)}, u32[]{:S(2)}) copy-start(s32[128,1]{0,1:T(1,128)} %param.14) | copy-start | bytes 1540
  6.8 52.0 %copy-start.17 = (bf16[128,2,2048]{2,1,0:T(2,128)(2,1)S(1)}, bf16[128,2,2048]{2,1,0:T(2,128)(2,1)}, u32[]{:S(2)}) copy-start(bf16[128,2,2048]{2,1,0:T(2,128)(2,1)} %param.11) | copy-start | bytes 3145732
  6.8 26.7 %collective-permute-start.1 = (bf16[176,2048]{1,0:T(8,128)(2,1)}, bf16[176,2048]{1,0:T(8,128)(2,1)}, u32[]{:S(2)}, u32[]{:S(2)}) collective-permute-start(bf16[176,2048]{1,0:T(8,128)(2,1)} %bitcast.24), channel_id=1, source_target_pairs={{0,0},{258,2},{132,4},{390,6},{128,128},{386,130},{4,132},{262,134... | collective-permute-start | bytes 2162696 | tf_op jit(solution)/shard_map/ppermute | solution.py:296
  13.8 30.6 %collective-permute-start.2 = (bf16[176,2048]{1,0:T(8,128)(2,1)}, bf16[176,2048]{1,0:T(8,128)(2,1)}, u32[]{:S(2)}, u32[]{:S(2)}) collective-permute-start(bf16[176,2048]{1,0:T(8,128)(2,1)} %param.19), channel_id=1, source_target_pairs={{0,0},{258,2},{132,4},{390,6},{128,128},{386,130},{4,132},{262,134... | collective-permute-start | bytes 2162696 | tf_op jit(solution)/shard_map/ppermute | solution.py:296
  23.3 51.6 %collective-permute-start.3 = (bf16[2,128,2048]{2,1,0:T(8,128)(2,1)}, bf16[2,128,2048]{2,1,0:T(8,128)(2,1)S(1)}, u32[]{:S(2)}, u32[]{:S(2)}) collective-permute-start(bf16[2,128,2048]{2,1,0:T(8,128)(2,1)} %bitcast.14), channel_id=1, source_target_pairs={{0,32},{32,64},{64,96},{96,128},{128,160},{160,192},{192,224},{224... | collective-permute-start | bytes 3145736 | tf_op jit(solution)/shard_map/ppermute | solution.py:276
  26.7 48.1 %collective-permute-start.4 = (bf16[2,128,2048]{2,1,0:T(8,128)(2,1)}, bf16[2,128,2048]{2,1,0:T(8,128)(2,1)S(1)}, u32[]{:S(2)}, u32[]{:S(2)}) collective-permute-start(bf16[2,128,2048]{2,1,0:T(8,128)(2,1)} %bitcast.14), channel_id=1, source_target_pairs={{0,64},{32,96},{64,128},{96,160},{128,192},{160,224},{192,256},{22... | collective-permute-start | bytes 3145736 | tf_op jit(solution)/shard_map/ppermute | solution.py:276
  31.6 50.7 %collective-permute-start.5 = (bf16[176,2048]{1,0:T(8,128)(2,1)}, bf16[176,2048]{1,0:T(8,128)(2,1)}, u32[]{:S(2)}, u32[]{:S(2)}) collective-permute-start(bf16[176,2048]{1,0:T(8,128)(2,1)} %collective-permute-done), channel_id=1, source_target_pairs={{0,0},{2,4},{4,2},{6,6},{128,130},{130,134},{132,128},{134,132},{2... | collective-permute-start | bytes 2162696 | tf_op jit(solution)/shard_map/ppermute | solution.py:299
  33.5 48.8 %collective-permute-start.6 = (bf16[176,2048]{1,0:T(8,128)(2,1)}, bf16[176,2048]{1,0:T(8,128)(2,1)}, u32[]{:S(2)}, u32[]{:S(2)}) collective-permute-start(bf16[176,2048]{1,0:T(8,128)(2,1)} %collective-permute-done.1), channel_id=1, source_target_pairs={{0,0},{2,4},{4,2},{6,6},{128,130},{130,134},{132,128},{134,132},{2... | collective-permute-start | bytes 2162696 | tf_op jit(solution)/shard_map/ppermute | solution.py:299
  44.4 39.4 %collective-permute-start.7 = (bf16[176,2048]{1,0:T(8,128)(2,1)}, bf16[176,2048]{1,0:T(8,128)(2,1)}, u32[]{:S(2)}, u32[]{:S(2)}) collective-permute-start(bf16[176,2048]{1,0:T(8,128)(2,1)} %collective-permute-done.2), channel_id=1, source_target_pairs={{0,0},{2,4},{4,2},{6,6},{128,130},{130,134},{132,128},{134,132},{2... | collective-permute-start | bytes 2162696 | tf_op jit(solution)/shard_map/ppermute | solution.py:299
  58.8 16.0 %copy-start = (bf16[128,2048]{1,0:T(8,128)(2,1)S(1)}, bf16[128,2048]{1,0:T(8,128)(2,1)}, u32[]{:S(2)}) copy-start(bf16[128,2048]{1,0:T(8,128)(2,1)} %queries) | copy-start | bytes 1572868
  58.9 16.0 %copy-start.1 = (f32[2048]{0:T(1024)S(1)}, f32[2048]{0:T(1024)}, u32[]{:S(2)}) copy-start(f32[2048]{0:T(1024)} %param.16) | copy-start | bytes 24580
  83.8 138.4 %all-to-all-start = ((bf16[64,48,128]{2,1,0:T(8,128)(2,1)}), bf16[64,48,128]{2,1,0:T(8,128)(2,1)S(1)}, u32[]{:S(2)}, u32[]{:S(2)}) async-start(bf16[64,48,128]{2,1,0:T(8,128)(2,1)} %bitcast.8), calls=%async_computation | async-start | bytes 1572864 | tf_op jit(solution)/shard_map/all_to_all | solution.py:326
  142.6 21.8 %collective-permute-start.8 = (bf16[176,2048]{1,0:T(8,128)(2,1)}, bf16[176,2048]{1,0:T(8,128)(2,1)S(1)}, u32[]{:S(2)}, u32[]{:S(2)}) collective-permute-start(bf16[176,2048]{1,0:T(8,128)(2,1)} %collective-permute-done.5.refs_0_), channel_id=1, source_target_pairs={{0,128},{128,256},{256,384},{384,0},{1,129},{129,257},{257,385},{3... | collective-permute-start | bytes 2162696 | tf_op jit(solution)/shard_map/ppermute | solution.py:310
  145.9 22.6 %collective-permute-start.12 = (bf16[176,2048]{1,0:T(8,128)(2,1)}, bf16[176,2048]{1,0:T(8,128)(2,1)S(1)}, u32[]{:S(2)}, u32[]{:S(2)}) collective-permute-start(bf16[176,2048]{1,0:T(8,128)(2,1)} %collective-permute-done.6.refs_4_), channel_id=1, source_target_pairs={{0,384},{128,0},{256,128},{384,256},{1,385},{129,1},{257,129},{385... | collective-permute-start | bytes 2162696 | tf_op jit(solution)/shard_map/ppermute | solution.py:311
  149.2 30.7 %collective-permute-start.14 = (bf16[176,2048]{1,0:T(8,128)(2,1)}, bf16[176,2048]{1,0:T(8,128)(2,1)S(1)}, u32[]{:S(2)}, u32[]{:S(2)}) collective-permute-start(bf16[176,2048]{1,0:T(8,128)(2,1)} %collective-permute-done.7.refs_8_), channel_id=1, source_target_pairs={{0,128},{128,256},{256,384},{384,0},{1,129},{129,257},{257,385},{3... | collective-permute-start | bytes 2162696 | tf_op jit(solution)/shard_map/ppermute | solution.py:310
  152.9 31.0 %collective-permute-start.15 = (bf16[176,2048]{1,0:T(8,128)(2,1)}, bf16[176,2048]{1,0:T(8,128)(2,1)S(1)}, u32[]{:S(2)}, u32[]{:S(2)}) collective-permute-start(bf16[176,2048]{1,0:T(8,128)(2,1)} %collective-permute-done.7.refs_8_), channel_id=1, source_target_pairs={{0,384},{128,0},{256,128},{384,256},{1,385},{129,1},{257,129},{385... | collective-permute-start | bytes 2162696 | tf_op jit(solution)/shard_map/ppermute | solution.py:311
  155.1 40.3 %collective-permute-start.11 = (bf16[176,2048]{1,0:T(8,128)(2,1)}, bf16[176,2048]{1,0:T(8,128)(2,1)S(1)}, u32[]{:S(2)}, u32[]{:S(2)}) collective-permute-start(bf16[176,2048]{1,0:T(8,128)(2,1)} %collective-permute-done.6.refs_4_), channel_id=1, source_target_pairs={{0,128},{128,256},{256,384},{384,0},{1,129},{129,257},{257,385},{3... | collective-permute-start | bytes 2162696 | tf_op jit(solution)/shard_map/ppermute | solution.py:310
  164.4 56.0 %copy-start.3 = (bf16[176,2048]{1,0:T(8,128)(2,1)}, bf16[176,2048]{1,0:T(8,128)(2,1)S(1)}, u32[]{:S(2)}) copy-start(bf16[176,2048]{1,0:T(8,128)(2,1)S(1)} %collective-permute-done.8.refs_1_) | copy-start | bytes 2162692
  164.5 35.7 %collective-permute-start.9 = (bf16[176,2048]{1,0:T(8,128)(2,1)}, bf16[176,2048]{1,0:T(8,128)(2,1)S(1)}, u32[]{:S(2)}, u32[]{:S(2)}) collective-permute-start(bf16[176,2048]{1,0:T(8,128)(2,1)} %collective-permute-done.5.refs_0_), channel_id=1, source_target_pairs={{0,384},{128,0},{256,128},{384,256},{1,385},{129,1},{257,129},{385... | collective-permute-start | bytes 2162696 | tf_op jit(solution)/shard_map/ppermute | solution.py:311
  168.4 52.0 %copy-start.5 = (bf16[176,2048]{1,0:T(8,128)(2,1)}, bf16[176,2048]{1,0:T(8,128)(2,1)S(1)}, u32[]{:S(2)}) copy-start(bf16[176,2048]{1,0:T(8,128)(2,1)S(1)} %collective-permute-done.12.refs_6_) | copy-start | bytes 2162692
  168.4 52.0 %collective-permute-start.10 = (bf16[176,2048]{1,0:T(8,128)(2,1)S(1)}, bf16[176,2048]{1,0:T(8,128)(2,1)S(1)}, u32[]{:S(2)}, u32[]{:S(2)}) collective-permute-start(bf16[176,2048]{1,0:T(8,128)(2,1)S(1)} %collective-permute-done.8.refs_1_), channel_id=1, source_target_pairs={{0,128},{128,256},{256,384},{384,0},{1,129},{129,257},{257,385},{3... | collective-permute-start | bytes 2162696 | tf_op jit(solution)/shard_map/ppermute | solution.py:314
  179.9 41.4 %collective-permute-start.13 = (bf16[176,2048]{1,0:T(8,128)(2,1)S(1)}, bf16[176,2048]{1,0:T(8,128)(2,1)S(1)}, u32[]{:S(2)}, u32[]{:S(2)}) collective-permute-start(bf16[176,2048]{1,0:T(8,128)(2,1)S(1)} %collective-permute-done.12.refs_6_), channel_id=1, source_target_pairs={{0,384},{128,0},{256,128},{384,256},{1,385},{129,1},{257,129},{385... | collective-permute-start | bytes 2162696 | tf_op jit(solution)/shard_map/ppermute | solution.py:315
  183.9 33.7 %collective-permute-start.16 = (bf16[176,1024]{1,0:T(8,128)(2,1)S(1)}, bf16[176,1024]{1,0:T(8,128)(2,1)S(1)}, u32[]{:S(2)}, u32[]{:S(2)}) collective-permute-start(bf16[176,1024]{1,0:T(8,128)(2,1)S(1)} %slice.8), channel_id=1, source_target_pairs={{0,128},{128,256},{256,384},{384,0},{1,129},{129,257},{257,385},{3... | collective-permute-start | bytes 1081352 | tf_op jit(solution)/shard_map/ppermute | solution.py:317
  196.2 23.5 %collective-permute-start.17 = (bf16[176,1024]{1,0:T(8,128)(2,1)S(1)}, bf16[176,1024]{1,0:T(8,128)(2,1)S(1)}, u32[]{:S(2)}, u32[]{:S(2)}) collective-permute-start(bf16[176,1024]{1,0:T(8,128)(2,1)S(1)} %slice.9), channel_id=1, source_target_pairs={{0,384},{128,0},{256,128},{384,256},{1,385},{129,1},{257,129},{385... | collective-permute-start | bytes 1081352 | tf_op jit(solution)/shard_map/ppermute | solution.py:318
  222.2 4.2 %collective-permute-start.18 = (bf16[3072,128]{1,0:T(8,128)(2,1)S(1)}, bf16[3072,128]{1,0:T(8,128)(2,1)S(1)}, u32[]{:S(2)}, u32[]{:S(2)}) collective-permute-start(bf16[3072,128]{1,0:T(8,128)(2,1)S(1)} %bitcast.18), channel_id=1, source_target_pairs={{0,1},{1,0},{2,3},{3,2},{4,5},{5,4},{6,7},{7,6},{8,9},{9,8},{10,11... | collective-permute-start | bytes 2359304 | tf_op jit(solution)/shard_map/ppermute | solution.py:272
  226.3 1.1 copy-start.4
  227.5 1.1 copy-start.6
  228.6 1.1 copy-start.8
  242.6 4.2 %collective-permute-start.19 = (bf16[3072,128]{1,0:T(8,128)(2,1)S(1)}, bf16[3072,128]{1,0:T(8,128)(2,1)S(1)}, u32[]{:S(2)}, u32[]{:S(2)}) collective-permute-start(bf16[3072,128]{1,0:T(8,128)(2,1)S(1)} %get-tuple-element.23), channel_id=1, source_target_pairs={{0,1},{1,0},{2,3},{3,2},{4,5},{5,4},{6,7},{7,6},{8,9},{9,8},{10,11... | collective-permute-start | bytes 2359304 | tf_op jit(solution)/shard_map/ppermute | solution.py:272
  247.9 15.0 %copy-start.18 = (f32[128,1]{0,1:T(1,128)S(1)}, f32[128,1]{0,1:T(1,128)}, u32[]{:S(2)}) copy-start(f32[128,1]{0,1:T(1,128)} %param.15) | copy-start | bytes 1540
  247.9 58.2 %all-to-all-start.1 = ((bf16[64,48,128]{2,1,0:T(8,128)(2,1)}), bf16[64,48,128]{2,1,0:T(8,128)(2,1)S(1)}, u32[]{:S(2)}, u32[]{:S(2)}) async-start(bf16[64,48,128]{2,1,0:T(8,128)(2,1)} %bitcast.10), calls=%async_computation.1 | async-start | bytes 1572864 | tf_op jit(solution)/shard_map/all_to_all | solution.py:330
  (9 other events, 8.5 us)

commit v5 on v4

--- a/solution.py
+++ b/solution.py
@@ -19,7 +19,7 @@
 
 
 def spread_pairs():
-    return [(PLACE[h][p] * 4 + p, h * 4 + p) for h in range(4) for p in range(4)]
+    return [(PLACE[h][p] * 4 + p, h * 4 + p) for h in range(4) for p in range(1, 4)]
 
 
 def lift_pairs():
@@ -216,7 +216,7 @@
             pltpu.VMEM((2 * count, features), jnp.bfloat16),
             pltpu.SemaphoreType.DMA((len(flat),)),
         ],
-        compiler_params=pltpu.CompilerParams(vmem_limit_bytes=2 * VMEM_BYTES),
+        compiler_params=pltpu.CompilerParams(vmem_limit_bytes=56 * 1024 * 1024),
         cost_estimate=pl.CostEstimate(
             flops=12 * count * features * units,
             bytes_accessed=6 * units * features,
@@ -266,6 +266,11 @@
 
 def after(value, *others):
     return lax.optimization_barrier((value, *others))[0]
+
+
+def spread(matrix):
+    moved = lax.ppermute(matrix, ("x", "p"), spread_pairs())
+    return jnp.where(lax.axis_index("p") == 0, matrix, moved)
 
 
 def swapped(rows):
@@ -293,22 +298,21 @@
     near = passed_along(kept, 1)
     far = passed_along(kept, 2)
     moved = [
-        lax.ppermute(matrix, ("x", "p"), spread_pairs())
-        for matrix in (gate_matrix.T, up_matrix.T, down_matrix)
+        spread(after(matrix, near, far)) for matrix in (gate_matrix.T, up_matrix.T, down_matrix)
     ]
     placed = [lax.ppermute(matrix, ("x", "p"), lift_pairs()) for matrix in moved]
     hidden, packed = attend(
         memory_source,
-        after(queries, *moved),
+        queries,
         key_value.transpose(1, 0, 2),
         near,
         far,
         routing,
         norm_gain.reshape(1, features),
     )
-    packed, *placed = lax.optimization_barrier((packed, *placed))
     left = [lax.ppermute(matrix, "x", ring(1)) for matrix in placed]
     right = [lax.ppermute(matrix, "x", ring(-1)) for matrix in placed]
+    packed = after(packed, *placed, *left[:2], *right[:2])
     middle = features // 2
     across = [
         [lax.ppermute(left[0], "x", ring(1))],
@@ -324,7 +328,7 @@
     ]
     chunks = packed.reshape(64, -1, LANES)
     arrived = lax.all_to_all(chunks, ("y", "s", "p"), 0, 0, tiled=True).reshape(packed.shape)
-    partner = swapped(after(arrived, *sum(weights, [])))
+    partner = swapped(after(arrived, *left, *right, *across[0], *across[1]))
     made, lent = experts(arrived, partner, weights)
     made = (made.astype(jnp.float32) + swapped(lent).astype(jnp.float32)).astype(jnp.bfloat16)
     returned = lax.all_to_all(made.reshape(chunks.shape), ("y", "s", "p"), 0, 0, tiled=True)

time: 313 us -> 323 us (1.032); the launches traced: 308 us -> 322 us
  waiting for transfers between devices: 103 us -> 136 us
  starting transfers between devices: 170 us -> 154 us
  local copies, waits for them, and re-layouts: 15.1 us -> 7.04 us
  other arithmetic: 1.11 us -> 4.53 us
    ppermute x2, waiting for transfers between devices: 15 us -> 43.1 us  [passed_along(): lax.ppermute(block, ('x', 'y'), [(i, (i + by) % 16) for i in range(16)])]
    ppermute x3, starting transfers between devices: 27.1 us -> 51.3 us  [per_device(): lax.ppermute(matrix, ('x', 'p'), lift_pairs())]
    all_to_all x1, starting transfers between devices: 58.8 us -> 39.5 us  [per_device(): lax.all_to_all(chunks, ('y', 's', 'p'), 0, 0, tiled=True)]
    ppermute x3, starting transfers between devices: 20.7 us -> 3.82 us  [spread(): moved = lax.ppermute(matrix, ('x', 'p'), spread_pairs())]
    ppermute x1, waiting for transfers between devices: 16.5 us -> 5.19 us  [per_device(): lax.ppermute(left[2][:, :middle], 'x', ring(1))]
    ppermute x1, waiting for transfers between devices: 0.01 us -> 10.7 us  [per_device(): lax.ppermute(right[1], 'x', ring(-1))]
    unnamed x42 -> x30, local copies, waits for them, and re-layouts: 15 us -> 6 us
    ppermute x3, waiting for transfers between devices: 0.01 us -> 5.5 us  [per_device(): right = [lax.ppermute(matrix, 'x', ring(-1)) for matrix in placed]]
  transfers between devices with their start and end apart: 22 -> 22, of which waited for: 10 -> 10; matrix products, arithmetic and copies ran while one was open for 1% -> 2% of each run, Pallas kernels for 2% -> 2%
where the time goes in v5:
time: 323 us; the launch traced here: 322 us
  starting transfers between devices  154 us (48%)
  waiting for transfers between devices  136 us (42%)
  Pallas kernels  19 us (6%)
  local copies, waits for them, and re-layouts  7.04 us (2%)
  other arithmetic  4.53 us (1%)
    ppermute x3, starting transfers between devices, per_device(): lax.ppermute(matrix, ('x', 'p'), lift_pairs())  51.3 us
    all_to_all x1, waiting for transfers between devices, per_device(): lax.all_to_all(made.reshape(chunks.shape), ('y', 's', 'p'), 0, 0, tiled=T...  43.1 us
    ppermute x2, waiting for transfers between devices, passed_along(): lax.ppermute(block, ('x', 'y'), [(i, (i + by) % 16) for i in range(16)])  43.1 us
    all_to_all x1, starting transfers between devices, per_device(): lax.all_to_all(chunks, ('y', 's', 'p'), 0, 0, tiled=True)  39.5 us
    ppermute x3, waiting for transfers between devices, per_device(): left = [lax.ppermute(matrix, 'x', ring(1)) for matrix in placed]  20 us
    ppermute x3, starting transfers between devices, per_device(): left = [lax.ppermute(matrix, 'x', ring(1)) for matrix in placed]  12.7 us
    all_to_all x1, starting transfers between devices, per_device(): lax.all_to_all(made.reshape(chunks.shape), ('y', 's', 'p'), 0, 0, tiled=T...  12.2 us
    ppermute x1, waiting for transfers between devices, per_device(): lax.ppermute(right[1], 'x', ring(-1))  10.7 us
  transfers between devices with their start and end apart: 22, of which 10 were waited for; matrix products, arithmetic and copies ran while one was open for 2% of the time, Pallas kernels for 2%

profile of v5, /device:TPU:6, one launch (start us, length us, event | category | flops | bytes accessed | tf_op | source)
XLA Modules:
  0.0 321.6 jit_solution(570774001700927816)
XLA Ops:
  1.7 3.5 %collective-permute-start = (bf16[2,128,2048]{2,1,0:T(8,128)(2,1)S(1)}, bf16[2,128,2048]{2,1,0:T(8,128)(2,1)S(1)}, u32[]{:S(2)}, u32[]{:S(2)}) collective-permute-start(bf16[2,128,2048]{2,1,0:T(8,128)(2,1)S(1)} %bitcast.21), channel_id=1, source_target_pairs={{0,32},{32,64},{64,96},{96,128},{128,160},{160,192},{192,224},{224... | collective-permute-start | bytes 3145736 | tf_op jit(solution)/shard_map/ppermute | solution.py:281
  5.1 4.8 %collective-permute-start.1 = (bf16[2,128,2048]{2,1,0:T(8,128)(2,1)S(1)}, bf16[2,128,2048]{2,1,0:T(8,128)(2,1)S(1)}, u32[]{:S(2)}, u32[]{:S(2)}) collective-permute-start(bf16[2,128,2048]{2,1,0:T(8,128)(2,1)S(1)} %bitcast.22), channel_id=1, source_target_pairs={{0,64},{32,96},{64,128},{96,160},{128,192},{160,224},{192,256},{22... | collective-permute-start | bytes 3145736 | tf_op jit(solution)/shard_map/ppermute | solution.py:281
  10.0 43.1 %collective-permute-done.near = bf16[2,128,2048]{2,1,0:T(8,128)(2,1)S(1)} collective-permute-done((bf16[2,128,2048]{2,1,0:T(8,128)(2,1)S(1)}, bf16[2,128,2048]{2,1,0:T(8,128)(2,1)S(1)}, u32[]{:S(2)}, u32[]{:S(2)}) %collective-permute-start) | collective-permute-done | bytes 1048608 | tf_op jit(solution)/shard_map/ppermute | solution.py:281
  57.0 26.2 %collective-permute-start.5 = (bf16[176,2048]{1,0:T(8,128)(2,1)S(1)}, bf16[176,2048]{1,0:T(8,128)(2,1)}, u32[]{:S(2)}, u32[]{:S(2)}) collective-permute-start(bf16[176,2048]{1,0:T(8,128)(2,1)S(1)} %broadcast_select_fusion.1), channel_id=1, source_target_pairs={{0,0},{2,4},{4,2},{6,6},{128,130},{130,134},{132,128},{134,132},{2... | collective-permute-start | bytes 2162696 | tf_op jit(solution)/shard_map/ppermute | solution.py:303
  84.4 14.1 %collective-permute-start.3 = (bf16[176,2048]{1,0:T(8,128)(2,1)S(1)}, bf16[176,2048]{1,0:T(8,128)(2,1)}, u32[]{:S(2)}, u32[]{:S(2)}) collective-permute-start(bf16[176,2048]{1,0:T(8,128)(2,1)S(1)} %broadcast_select_fusion.2), channel_id=1, source_target_pairs={{0,0},{2,4},{4,2},{6,6},{128,130},{130,134},{132,128},{134,132},{2... | collective-permute-start | bytes 2162696 | tf_op jit(solution)/shard_map/ppermute | solution.py:303
  99.5 11.1 %collective-permute-start.7 = (bf16[176,2048]{1,0:T(8,128)(2,1)}, bf16[176,2048]{1,0:T(8,128)(2,1)}, u32[]{:S(2)}, u32[]{:S(2)}) collective-permute-start(bf16[176,2048]{1,0:T(8,128)(2,1)} %broadcast_select_fusion), channel_id=1, source_target_pairs={{0,0},{2,4},{4,2},{6,6},{128,130},{130,134},{132,128},{134,132},{2... | collective-permute-start | bytes 2162696 | tf_op jit(solution)/shard_map/ppermute | solution.py:303
  110.6 1.9 collective-permute-start.11
  112.5 5.1 %collective-permute-start.8 = (bf16[176,2048]{1,0:T(8,128)(2,1)}, bf16[176,2048]{1,0:T(8,128)(2,1)}, u32[]{:S(2)}, u32[]{:S(2)}) collective-permute-start(bf16[176,2048]{1,0:T(8,128)(2,1)} %collective-permute-done.3.refs_0_), channel_id=1, source_target_pairs={{0,128},{128,256},{256,384},{384,0},{1,129},{129,257},{257,385},{3... | collective-permute-start | bytes 2162696 | tf_op jit(solution)/shard_map/ppermute | solution.py:313
  117.6 1.9 collective-permute-start.9
  119.6 3.9 %collective-permute-start.10 = (bf16[176,2048]{1,0:T(8,128)(2,1)}, bf16[176,2048]{1,0:T(8,128)(2,1)}, u32[]{:S(2)}, u32[]{:S(2)}) collective-permute-start(bf16[176,2048]{1,0:T(8,128)(2,1)} %collective-permute-done.3.refs_0_), channel_id=1, source_target_pairs={{0,384},{128,0},{256,128},{384,256},{1,385},{129,1},{257,129},{385... | collective-permute-start | bytes 2162696 | tf_op jit(solution)/shard_map/ppermute | solution.py:314
  125.9 7.5 %attend.1 = (bf16[128,2048]{1,0:T(8,128)(2,1)S(1)}, bf16[3072,128]{1,0:T(8,128)(2,1)}) custom-call(s32[1]{0:T(128)S(6)} %copy.20.source, bf16[128,2048]{1,0:T(8,128)(2,1)S(1)} %copy-done, bf16[2,128,2048]{2,1,0:T(8,128)(2,1)S(1)} %bitcast.16, bf16[2,128,2048]{2,1,0:T(8,128)(2,1)S(1)} %collective-permute-done.near, ...), custom_call_target="tpu_custom_call" | custom-call | flops 268435456 | bytes 2621440 | tf_op jit(solution)/shard_map/attend/pallas_call | solution.py:128
  134.5 11.0 %collective-permute-done.9.refs_5_ = bf16[176,2048]{1,0:T(8,128)(2,1)} collective-permute-done((bf16[176,2048]{1,0:T(8,128)(2,1)}, bf16[176,2048]{1,0:T(8,128)(2,1)}, u32[]{:S(2)}, u32[]{:S(2)}) %collective-permute-start.9) | collective-permute-done | bytes 720928 | tf_op jit(solution)/shard_map/ppermute | solution.py:313
  145.6 39.5 %all-to-all-start = ((bf16[64,48,128]{2,1,0:T(8,128)(2,1)}), bf16[64,48,128]{2,1,0:T(8,128)(2,1)S(1)}, u32[]{:S(2)}, u32[]{:S(2)}) async-start(bf16[64,48,128]{2,1,0:T(8,128)(2,1)} %bitcast.8), calls=%async_computation | async-start | bytes 1572864 | tf_op jit(solution)/shard_map/all_to_all | solution.py:330
  185.1 5.6 %collective-permute-start.12 = (bf16[176,2048]{1,0:T(8,128)(2,1)}, bf16[176,2048]{1,0:T(8,128)(2,1)S(1)}, u32[]{:S(2)}, u32[]{:S(2)}) collective-permute-start(bf16[176,2048]{1,0:T(8,128)(2,1)} %collective-permute-done.7.refs_8_), channel_id=1, source_target_pairs={{0,128},{128,256},{256,384},{384,0},{1,129},{129,257},{257,385},{3... | collective-permute-start | bytes 2162696 | tf_op jit(solution)/shard_map/ppermute | solution.py:313
  190.7 1.9 collective-permute-start.13
  192.6 1.9 collective-permute-start.15
  194.5 5.1 %collective-permute-start.14 = (bf16[176,2048]{1,0:T(8,128)(2,1)}, bf16[176,2048]{1,0:T(8,128)(2,1)}, u32[]{:S(2)}, u32[]{:S(2)}) collective-permute-start(bf16[176,2048]{1,0:T(8,128)(2,1)} %collective-permute-done.8.refs_1_), channel_id=1, source_target_pairs={{0,128},{128,256},{256,384},{384,0},{1,129},{129,257},{257,385},{3... | collective-permute-start | bytes 2162696 | tf_op jit(solution)/shard_map/ppermute | solution.py:318
  199.7 7.9 %collective-permute-done.12.refs_9_ = bf16[176,2048]{1,0:T(8,128)(2,1)S(1)} collective-permute-done((bf16[176,2048]{1,0:T(8,128)(2,1)}, bf16[176,2048]{1,0:T(8,128)(2,1)S(1)}, u32[]{:S(2)}, u32[]{:S(2)}) %collective-permute-start.12) | collective-permute-done | bytes 720928 | tf_op jit(solution)/shard_map/ppermute | solution.py:313
  207.6 5.5 %collective-permute-done.13.refs_10_ = bf16[176,2048]{1,0:T(8,128)(2,1)S(1)} collective-permute-done((bf16[176,2048]{1,0:T(8,128)(2,1)}, bf16[176,2048]{1,0:T(8,128)(2,1)S(1)}, u32[]{:S(2)}, u32[]{:S(2)}) %collective-permute-start.13) | collective-permute-done | bytes 720928 | tf_op jit(solution)/shard_map/ppermute | solution.py:314
  213.1 10.7 %collective-permute-done.15.refs_7_ = bf16[176,2048]{1,0:T(8,128)(2,1)S(1)} collective-permute-done((bf16[176,2048]{1,0:T(8,128)(2,1)}, bf16[176,2048]{1,0:T(8,128)(2,1)S(1)}, u32[]{:S(2)}, u32[]{:S(2)}) %collective-permute-start.15) | collective-permute-done | bytes 720928 | tf_op jit(solution)/shard_map/ppermute | solution.py:319
  224.7 1.9 collective-permute-start.16
  226.6 5.0 %collective-permute-start.17 = (bf16[176,1024]{1,0:T(8,128)(2,1)S(1)}, bf16[176,1024]{1,0:T(8,128)(2,1)S(1)}, u32[]{:S(2)}, u32[]{:S(2)}) collective-permute-start(bf16[176,1024]{1,0:T(8,128)(2,1)S(1)} %slice.8), channel_id=1, source_target_pairs={{0,128},{128,256},{256,384},{384,0},{1,129},{129,257},{257,385},{3... | collective-permute-start | bytes 1081352 | tf_op jit(solution)/shard_map/ppermute | solution.py:321
  232.6 2.1 collective-permute-start.18
  234.7 5.2 %collective-permute-done.17.refs_11_ = bf16[176,1024]{1,0:T(8,128)(2,1)S(1)} collective-permute-done((bf16[176,1024]{1,0:T(8,128)(2,1)S(1)}, bf16[176,1024]{1,0:T(8,128)(2,1)S(1)}, u32[]{:S(2)}, u32[]{:S(2)}) %collective-permute-start.17) | collective-permute-done | bytes 360480 | tf_op jit(solution)/shard_map/ppermute | solution.py:321
  239.9 6.3 %collective-permute-done.18.refs_12_ = bf16[176,1024]{1,0:T(8,128)(2,1)S(1)} collective-permute-done((bf16[176,1024]{1,0:T(8,128)(2,1)S(1)}, bf16[176,1024]{1,0:T(8,128)(2,1)S(1)}, u32[]{:S(2)}, u32[]{:S(2)}) %collective-permute-start.18) | collective-permute-done | bytes 360480 | tf_op jit(solution)/shard_map/ppermute | solution.py:322
  247.9 9.7 %experts.1 = (bf16[3072,128]{1,0:T(8,128)(2,1)}, bf16[3072,128]{1,0:T(8,128)(2,1)}) custom-call(bf16[3072,128]{1,0:T(8,128)(2,1)} %bitcast.24, bf16[3072,128]{1,0:T(8,128)(2,1)} %copy-done.9, bf16[176,2048]{1,0:T(8,128)(2,1)} %collective-permute-done.3.refs_0_, bf16[176,2048]{1,0:T(8,128)(2,1)} %collective-permute-done.8.refs_1_, ...), custom_call_target="tpu_custom_call" | custom-call | flops 3321888768 | bytes 8650752 | tf_op jit(solution)/shard_map/experts/pallas_call | solution.py:208
  257.6 1.9 collective-permute-start.19
  259.5 2.5 collective-permute-done.19
  262.0 2.3 add_convert_fusion
  264.3 12.2 %all-to-all-start.1 = ((bf16[64,48,128]{2,1,0:T(8,128)(2,1)}), bf16[64,48,128]{2,1,0:T(8,128)(2,1)S(1)}, u32[]{:S(2)}, u32[]{:S(2)}) async-start(bf16[64,48,128]{2,1,0:T(8,128)(2,1)} %bitcast.10), calls=%async_computation.1 | async-start | bytes 1572864 | tf_op jit(solution)/shard_map/all_to_all | solution.py:334
  276.6 43.1 %all-to-all-done.1 = bf16[64,48,128]{2,1,0:T(8,128)(2,1)S(1)} async-done(((bf16[64,48,128]{2,1,0:T(8,128)(2,1)}), bf16[64,48,128]{2,1,0:T(8,128)(2,1)S(1)}, u32[]{:S(2)}, u32[]{:S(2)}) %all-to-all-start.1) | async-done | bytes 786464 | tf_op jit(solution)/shard_map/all_to_all | solution.py:334
  319.7 1.9 combine.1
  (51 shorter events, 14.2 us)
Async XLA Ops:
  0.0 53.0 %copy-start.4 = (bf16[2048,176]{0,1:T(8,128)(2,1)S(1)}, bf16[2048,176]{0,1:T(8,128)(2,1)}, u32[]{:S(2)}) copy-start(bf16[2048,176]{0,1:T(8,128)(2,1)} %param.18) | copy-start | bytes 2162692
  1.7 51.4 %collective-permute-start = (bf16[2,128,2048]{2,1,0:T(8,128)(2,1)S(1)}, bf16[2,128,2048]{2,1,0:T(8,128)(2,1)S(1)}, u32[]{:S(2)}, u32[]{:S(2)}) collective-permute-start(bf16[2,128,2048]{2,1,0:T(8,128)(2,1)S(1)} %bitcast.21), channel_id=1, source_target_pairs={{0,32},{32,64},{64,96},{96,128},{128,160},{160,192},{192,224},{224... | collective-permute-start | bytes 3145736 | tf_op jit(solution)/shard_map/ppermute | solution.py:281
  5.1 47.9 %collective-permute-start.1 = (bf16[2,128,2048]{2,1,0:T(8,128)(2,1)S(1)}, bf16[2,128,2048]{2,1,0:T(8,128)(2,1)S(1)}, u32[]{:S(2)}, u32[]{:S(2)}) collective-permute-start(bf16[2,128,2048]{2,1,0:T(8,128)(2,1)S(1)} %bitcast.22), channel_id=1, source_target_pairs={{0,64},{32,96},{64,128},{96,160},{128,192},{160,224},{192,256},{22... | collective-permute-start | bytes 3145736 | tf_op jit(solution)/shard_map/ppermute | solution.py:281
  53.0 3.8 %collective-permute-start.4 = (bf16[176,2048]{1,0:T(8,128)(2,1)S(1)}, bf16[176,2048]{1,0:T(8,128)(2,1)}, u32[]{:S(2)}, u32[]{:S(2)}) collective-permute-start(bf16[176,2048]{1,0:T(8,128)(2,1)S(1)} %bitcast.25), channel_id=1, source_target_pairs={{258,2},{132,4},{390,6},{386,130},{4,132},{262,134},{2,258},{388,2... | collective-permute-start | bytes 2162696 | tf_op jit(solution)/shard_map/ppermute | solution.py:272
  54.6 28.6 %collective-permute-start.2 = (bf16[176,2048]{1,0:T(8,128)(2,1)}, bf16[176,2048]{1,0:T(8,128)(2,1)}, u32[]{:S(2)}, u32[]{:S(2)}) collective-permute-start(bf16[176,2048]{1,0:T(8,128)(2,1)} %bitcast.6), channel_id=1, source_target_pairs={{258,2},{132,4},{390,6},{386,130},{4,132},{262,134},{2,258},{388,2... | collective-permute-start | bytes 2162696 | tf_op jit(solution)/shard_map/ppermute | solution.py:272
  56.2 42.4 %collective-permute-start.6 = (bf16[176,2048]{1,0:T(8,128)(2,1)}, bf16[176,2048]{1,0:T(8,128)(2,1)S(1)}, u32[]{:S(2)}, u32[]{:S(2)}) collective-permute-start(bf16[176,2048]{1,0:T(8,128)(2,1)} %param.19), channel_id=1, source_target_pairs={{258,2},{132,4},{390,6},{386,130},{4,132},{262,134},{2,258},{388,2... | collective-permute-start | bytes 2162696 | tf_op jit(solution)/shard_map/ppermute | solution.py:272
  57.0 41.5 %copy-start.5 = (bf16[176,2048]{1,0:T(8,128)(2,1)S(1)}, bf16[176,2048]{1,0:T(8,128)(2,1)}, u32[]{:S(2)}) copy-start(bf16[176,2048]{1,0:T(8,128)(2,1)} %param.19) | copy-start | bytes 2162692
  57.0 53.6 %collective-permute-start.5 = (bf16[176,2048]{1,0:T(8,128)(2,1)S(1)}, bf16[176,2048]{1,0:T(8,128)(2,1)}, u32[]{:S(2)}, u32[]{:S(2)}) collective-permute-start(bf16[176,2048]{1,0:T(8,128)(2,1)S(1)} %broadcast_select_fusion.1), channel_id=1, source_target_pairs={{0,0},{2,4},{4,2},{6,6},{128,130},{130,134},{132,128},{134,132},{2... | collective-permute-start | bytes 2162696 | tf_op jit(solution)/shard_map/ppermute | solution.py:303
  84.4 39.1 %copy-start.2 = (s32[128,1]{0,1:T(1,128)S(1)}, s32[128,1]{0,1:T(1,128)}, u32[]{:S(2)}) copy-start(s32[128,1]{0,1:T(1,128)} %param.14) | copy-start | bytes 1540
  84.4 28.1 %collective-permute-start.3 = (bf16[176,2048]{1,0:T(8,128)(2,1)S(1)}, bf16[176,2048]{1,0:T(8,128)(2,1)}, u32[]{:S(2)}, u32[]{:S(2)}) collective-permute-start(bf16[176,2048]{1,0:T(8,128)(2,1)S(1)} %broadcast_select_fusion.2), channel_id=1, source_target_pairs={{0,0},{2,4},{4,2},{6,6},{128,130},{130,134},{132,128},{134,132},{2... | collective-permute-start | bytes 2162696 | tf_op jit(solution)/shard_map/ppermute | solution.py:303
  99.5 33.9 %collective-permute-start.7 = (bf16[176,2048]{1,0:T(8,128)(2,1)}, bf16[176,2048]{1,0:T(8,128)(2,1)}, u32[]{:S(2)}, u32[]{:S(2)}) collective-permute-start(bf16[176,2048]{1,0:T(8,128)(2,1)} %broadcast_select_fusion), channel_id=1, source_target_pairs={{0,0},{2,4},{4,2},{6,6},{128,130},{130,134},{132,128},{134,132},{2... | collective-permute-start | bytes 2162696 | tf_op jit(solution)/shard_map/ppermute | solution.py:303
  110.6 22.9 %collective-permute-start.11 = (bf16[176,2048]{1,0:T(8,128)(2,1)}, bf16[176,2048]{1,0:T(8,128)(2,1)}, u32[]{:S(2)}, u32[]{:S(2)}) collective-permute-start(bf16[176,2048]{1,0:T(8,128)(2,1)} %collective-permute-done.5.refs_4_), channel_id=1, source_target_pairs={{0,384},{128,0},{256,128},{384,256},{1,385},{129,1},{257,129},{385... | collective-permute-start | bytes 2162696 | tf_op jit(solution)/shard_map/ppermute | solution.py:314
  112.5 22.0 %collective-permute-start.8 = (bf16[176,2048]{1,0:T(8,128)(2,1)}, bf16[176,2048]{1,0:T(8,128)(2,1)}, u32[]{:S(2)}, u32[]{:S(2)}) collective-permute-start(bf16[176,2048]{1,0:T(8,128)(2,1)} %collective-permute-done.3.refs_0_), channel_id=1, source_target_pairs={{0,128},{128,256},{256,384},{384,0},{1,129},{129,257},{257,385},{3... | collective-permute-start | bytes 2162696 | tf_op jit(solution)/shard_map/ppermute | solution.py:313
  117.6 27.9 %collective-permute-start.9 = (bf16[176,2048]{1,0:T(8,128)(2,1)}, bf16[176,2048]{1,0:T(8,128)(2,1)}, u32[]{:S(2)}, u32[]{:S(2)}) collective-permute-start(bf16[176,2048]{1,0:T(8,128)(2,1)} %collective-permute-done.5.refs_4_), channel_id=1, source_target_pairs={{0,128},{128,256},{256,384},{384,0},{1,129},{129,257},{257,385},{3... | collective-permute-start | bytes 2162696 | tf_op jit(solution)/shard_map/ppermute | solution.py:313
  119.6 26.0 %collective-permute-start.10 = (bf16[176,2048]{1,0:T(8,128)(2,1)}, bf16[176,2048]{1,0:T(8,128)(2,1)}, u32[]{:S(2)}, u32[]{:S(2)}) collective-permute-start(bf16[176,2048]{1,0:T(8,128)(2,1)} %collective-permute-done.3.refs_0_), channel_id=1, source_target_pairs={{0,384},{128,0},{256,128},{384,256},{1,385},{129,1},{257,129},{385... | collective-permute-start | bytes 2162696 | tf_op jit(solution)/shard_map/ppermute | solution.py:314
  123.6 2.3 copy-start
  123.6 2.3 copy-start.1
  145.6 79.1 %all-to-all-start = ((bf16[64,48,128]{2,1,0:T(8,128)(2,1)}), bf16[64,48,128]{2,1,0:T(8,128)(2,1)S(1)}, u32[]{:S(2)}, u32[]{:S(2)}) async-start(bf16[64,48,128]{2,1,0:T(8,128)(2,1)} %bitcast.8), calls=%async_computation | async-start | bytes 1572864 | tf_op jit(solution)/shard_map/all_to_all | solution.py:330
  185.1 22.5 %collective-permute-start.12 = (bf16[176,2048]{1,0:T(8,128)(2,1)}, bf16[176,2048]{1,0:T(8,128)(2,1)S(1)}, u32[]{:S(2)}, u32[]{:S(2)}) collective-permute-start(bf16[176,2048]{1,0:T(8,128)(2,1)} %collective-permute-done.7.refs_8_), channel_id=1, source_target_pairs={{0,128},{128,256},{256,384},{384,0},{1,129},{129,257},{257,385},{3... | collective-permute-start | bytes 2162696 | tf_op jit(solution)/shard_map/ppermute | solution.py:313
  190.7 22.4 %collective-permute-start.13 = (bf16[176,2048]{1,0:T(8,128)(2,1)}, bf16[176,2048]{1,0:T(8,128)(2,1)S(1)}, u32[]{:S(2)}, u32[]{:S(2)}) collective-permute-start(bf16[176,2048]{1,0:T(8,128)(2,1)} %collective-permute-done.7.refs_8_), channel_id=1, source_target_pairs={{0,384},{128,0},{256,128},{384,256},{1,385},{129,1},{257,129},{385... | collective-permute-start | bytes 2162696 | tf_op jit(solution)/shard_map/ppermute | solution.py:314
  192.6 31.2 %collective-permute-start.15 = (bf16[176,2048]{1,0:T(8,128)(2,1)}, bf16[176,2048]{1,0:T(8,128)(2,1)S(1)}, u32[]{:S(2)}, u32[]{:S(2)}) collective-permute-start(bf16[176,2048]{1,0:T(8,128)(2,1)} %collective-permute-done.11.refs_6_), channel_id=1, source_target_pairs={{0,384},{128,0},{256,128},{384,256},{1,385},{129,1},{257,129},{385... | collective-permute-start | bytes 2162696 | tf_op jit(solution)/shard_map/ppermute | solution.py:319
  194.5 30.1 %collective-permute-start.14 = (bf16[176,2048]{1,0:T(8,128)(2,1)}, bf16[176,2048]{1,0:T(8,128)(2,1)}, u32[]{:S(2)}, u32[]{:S(2)}) collective-permute-start(bf16[176,2048]{1,0:T(8,128)(2,1)} %collective-permute-done.8.refs_1_), channel_id=1, source_target_pairs={{0,128},{128,256},{256,384},{384,0},{1,129},{129,257},{257,385},{3... | collective-permute-start | bytes 2162696 | tf_op jit(solution)/shard_map/ppermute | solution.py:318
  207.6 38.7 %copy-start.6 = (bf16[176,2048]{1,0:T(8,128)(2,1)}, bf16[176,2048]{1,0:T(8,128)(2,1)S(1)}, u32[]{:S(2)}) copy-start(bf16[176,2048]{1,0:T(8,128)(2,1)S(1)} %collective-permute-done.12.refs_9_) | copy-start | bytes 2162692
  213.1 11.6 %copy-start.7 = (bf16[176,2048]{1,0:T(8,128)(2,1)}, bf16[176,2048]{1,0:T(8,128)(2,1)S(1)}, u32[]{:S(2)}) copy-start(bf16[176,2048]{1,0:T(8,128)(2,1)S(1)} %collective-permute-done.13.refs_10_) | copy-start | bytes 2162692
  224.6 21.6 %copy-start.3 = (bf16[64,48,128]{2,1,0:T(8,128)(2,1)}, bf16[64,48,128]{2,1,0:T(8,128)(2,1)S(1)}, u32[]{:S(2)}) copy-start(bf16[64,48,128]{2,1,0:T(8,128)(2,1)S(1)} %all-to-all-done) | copy-start | bytes 2359300
  224.7 21.6 %collective-permute-start.16 = (bf16[3072,128]{1,0:T(8,128)(2,1)S(1)}, bf16[3072,128]{1,0:T(8,128)(2,1)S(1)}, u32[]{:S(2)}, u32[]{:S(2)}) collective-permute-start(bf16[3072,128]{1,0:T(8,128)(2,1)S(1)} %bitcast.23), channel_id=1, source_target_pairs={{0,1},{1,0},{2,3},{3,2},{4,5},{5,4},{6,7},{7,6},{8,9},{9,8},{10,11... | collective-permute-start | bytes 2359304 | tf_op jit(solution)/shard_map/ppermute | solution.py:277
  226.6 13.3 %collective-permute-start.17 = (bf16[176,1024]{1,0:T(8,128)(2,1)S(1)}, bf16[176,1024]{1,0:T(8,128)(2,1)S(1)}, u32[]{:S(2)}, u32[]{:S(2)}) collective-permute-start(bf16[176,1024]{1,0:T(8,128)(2,1)S(1)} %slice.8), channel_id=1, source_target_pairs={{0,128},{128,256},{256,384},{384,0},{1,129},{129,257},{257,385},{3... | collective-permute-start | bytes 1081352 | tf_op jit(solution)/shard_map/ppermute | solution.py:321
  232.6 13.6 %collective-permute-start.18 = (bf16[176,1024]{1,0:T(8,128)(2,1)S(1)}, bf16[176,1024]{1,0:T(8,128)(2,1)S(1)}, u32[]{:S(2)}, u32[]{:S(2)}) collective-permute-start(bf16[176,1024]{1,0:T(8,128)(2,1)S(1)} %slice.9), channel_id=1, source_target_pairs={{0,384},{128,0},{256,128},{384,256},{1,385},{129,1},{257,129},{385... | collective-permute-start | bytes 1081352 | tf_op jit(solution)/shard_map/ppermute | solution.py:322
  239.9 6.4 %copy-start.11 = (bf16[176,1024]{1,0:T(8,128)(2,1)}, bf16[176,1024]{1,0:T(8,128)(2,1)S(1)}, u32[]{:S(2)}) copy-start(bf16[176,1024]{1,0:T(8,128)(2,1)S(1)} %collective-permute-done.17.refs_11_) | copy-start | bytes 1081348
  257.6 4.4 %collective-permute-start.19 = (bf16[3072,128]{1,0:T(8,128)(2,1)}, bf16[3072,128]{1,0:T(8,128)(2,1)S(1)}, u32[]{:S(2)}, u32[]{:S(2)}) collective-permute-start(bf16[3072,128]{1,0:T(8,128)(2,1)} %get-tuple-element.21), channel_id=1, source_target_pairs={{0,1},{1,0},{2,3},{3,2},{4,5},{5,4},{6,7},{7,6},{8,9},{9,8},{10,11... | collective-permute-start | bytes 2359304 | tf_op jit(solution)/shard_map/ppermute | solution.py:277
  264.3 12.2 %copy-start.8 = (f32[128,1]{0,1:T(1,128)S(1)}, f32[128,1]{0,1:T(1,128)}, u32[]{:S(2)}) copy-start(f32[128,1]{0,1:T(1,128)} %param.15) | copy-start | bytes 1540
  264.3 55.5 %all-to-all-start.1 = ((bf16[64,48,128]{2,1,0:T(8,128)(2,1)}), bf16[64,48,128]{2,1,0:T(8,128)(2,1)S(1)}, u32[]{:S(2)}, u32[]{:S(2)}) async-start(bf16[64,48,128]{2,1,0:T(8,128)(2,1)} %bitcast.10), calls=%async_computation.1 | async-start | bytes 1572864 | tf_op jit(solution)/shard_map/all_to_all | solution.py:334
  (3 other events, 2.5 us)

commit v6 on v1

--- a/solution.py
+++ b/solution.py
@@ -20,7 +20,7 @@
 
 
 def spread_pairs():
-    return [(PLACE[h][p] * 4 + p, h * 4 + p) for h in range(4) for p in range(4)]
+    return [(PLACE[h][p] * 4 + p, h * 4 + p) for h in range(4) for p in range(1, 4)]
 
 
 def lift_pairs():
@@ -41,40 +41,33 @@
 def attend_kernel(
     source,
     queries,
-    own_keys,
-    own_values,
-    near_keys,
-    near_values,
-    far_keys,
-    far_values,
+    own,
+    near,
+    far_off,
     chosen_column,
     chosen_row,
     gain,
     hidden_out,
     packed_out,
-    keys,
-    values,
+    recalled,
     normed,
     rows,
-    sems,
+    sem,
 ):
     tokens, features = queries.shape
 
-    def fetch(from_keys, from_values):
-        first = pltpu.make_async_copy(from_keys, keys, sems.at[0])
-        second = pltpu.make_async_copy(from_values, values, sems.at[1])
-        first.start()
-        second.start()
-        first.wait()
-        second.wait()
+    def fetch(block):
+        copy = pltpu.make_async_copy(block, recalled, sem)
+        copy.start()
+        copy.wait()
 
     @pl.when(source[0] == 0)
     def _():
-        fetch(near_keys, near_values)
+        fetch(near)
 
     @pl.when(source[0] != 0)
     def _():
-        fetch(far_keys, far_values)
+        fetch(far_off)
 
     later = lax.broadcasted_iota(jnp.int32, (tokens, tokens), 1) > lax.broadcasted_iota(
         jnp.int32, (tokens, tokens), 0
@@ -86,22 +79,22 @@
         at = slice(head * LANES, (head + 1) * LANES)
         query = queries[:, at]
         far = scale * lax.dot_general(
-            query, keys[:, at], transposed, preferred_element_type=jnp.float32
-        )
-        own = scale * lax.dot_general(
-            query, own_keys[:, at], transposed, preferred_element_type=jnp.float32
-        )
-        own = jnp.where(later, -1e30, own)
-        top = jnp.max(jnp.maximum(far, own), axis=1, keepdims=True)
+            query, recalled[0, :, at], transposed, preferred_element_type=jnp.float32
+        )
+        here = scale * lax.dot_general(
+            query, own[0, :, at], transposed, preferred_element_type=jnp.float32
+        )
+        here = jnp.where(later, -1e30, here)
+        top = jnp.max(jnp.maximum(far, here), axis=1, keepdims=True)
         far = jnp.exp(far - top)
-        own = jnp.exp(own - top)
-        share = 1.0 / jnp.sum(far + own, axis=1, keepdims=True)
+        here = jnp.exp(here - top)
+        share = 1.0 / jnp.sum(far + here, axis=1, keepdims=True)
         hidden = jnp.dot(
-            (far * share).astype(jnp.bfloat16), values[:, at], preferred_element_type=jnp.float32
+            (far * share).astype(jnp.bfloat16),
+            recalled[1, :, at],
+            preferred_element_type=jnp.float32,
         ) + jnp.dot(
-            (own * share).astype(jnp.bfloat16),
-            own_values[:, at],
-            preferred_element_type=jnp.float32,
+            (here * share).astype(jnp.bfloat16), own[1, :, at], preferred_element_type=jnp.float32
         )
         hidden = hidden.astype(jnp.bfloat16)
         hidden_out[:, at] = hidden
@@ -140,16 +133,15 @@
             jax.ShapeDtypeStruct((count * blocks, LANES), jnp.bfloat16),
         ),
         in_specs=[pl.BlockSpec(memory_space=pltpu.SMEM)]
-        + [vmem] * 3
-        + [anywhere] * 4
+        + [vmem] * 2
+        + [anywhere] * 2
         + [vmem] * 3,
         out_specs=(vmem, vmem),
         scratch_shapes=[
-            pltpu.VMEM((tokens, features), jnp.bfloat16),
-            pltpu.VMEM((tokens, features), jnp.bfloat16),
+            pltpu.VMEM((2, tokens, features), jnp.bfloat16),
             pltpu.VMEM((tokens, features), jnp.bfloat16),
             pltpu.VMEM((count * blocks, LANES), jnp.float32),
-            pltpu.SemaphoreType.DMA((2,)),
+            pltpu.SemaphoreType.DMA,
         ],
         compiler_params=pltpu.CompilerParams(vmem_limit_bytes=VMEM_BYTES),
         cost_estimate=pl.CostEstimate(
@@ -158,7 +150,7 @@
             transcendentals=2 * HEADS * tokens * tokens,
         ),
         name="attend",
-    )(source, queries, *own, *near, *far, chosen, chosen.reshape(1, tokens), gain)
+    )(source, queries, own, near, far, chosen, chosen.reshape(1, tokens), gain)
 
 
 def experts_kernel(pieces, arrived, *refs):
@@ -280,6 +272,7 @@
 
 def gathered(matrix, which):
     moved = lax.ppermute(matrix, ("x", "p"), spread_pairs())
+    moved = jnp.where(lax.axis_index("p") == 0, matrix, moved)
     own = lax.ppermute(moved, ("x", "p"), lift_pairs())
     left = lax.ppermute(own, "x", ring(1))
     right = lax.ppermute(own, "x", ring(-1))
@@ -312,14 +305,14 @@
     down_matrix,
 ):
     features = queries.shape[1]
-    kept = [memory[0, :, 0], memory[0, :, 1]]
-    near = [passed_along(block, 1) for block in kept]
-    far = [passed_along(block, 2) for block in kept]
+    kept = memory[0].transpose(1, 0, 2)
+    near = passed_along(kept, 1)
+    far = passed_along(kept, 2)
     weights = [
         gathered(matrix, which)
         for which, matrix in enumerate((gate_matrix.T, up_matrix.T, down_matrix))
     ]
-    own = [key_value[:, 0], key_value[:, 1]]
+    own = key_value.transpose(1, 0, 2)
     hidden, packed = attend(
         memory_source, queries, own, near, far, routing, norm_gain.reshape(1, features)
     )

time: 286 us -> 330 us (1.15)
  starting transfers between devices: 176 us -> 212 us
  waiting for transfers between devices: 74.3 us -> 84.2 us
  local copies, waits for them, and re-layouts: 10.6 us -> 5.67 us
    all_to_all x1, starting transfers between devices: 43.3 us -> 83.1 us  [per_device(): arrived = lax.all_to_all(chunks, ('y', 's', 'p'), 0, 0, tiled=True)]
    ppermute x1, waiting for transfers between devices: 0.74 us -> 10.1 us  [gathered(): lax.ppermute(right[cut:], 'x', ring(-1))]
    ppermute x3, waiting for transfers between devices: 12.1 us -> 20.1 us  [gathered(): right = lax.ppermute(own, 'x', ring(-1))]
    ppermute x3, waiting for transfers between devices: 6.3 us -> 0.01 us  [gathered(): left = lax.ppermute(own, 'x', ring(1))]
    ppermute x4 -> x2, starting transfers between devices: 14.1 us -> 8.29 us  [passed_along(): lax.ppermute(block, ('x', 'y'), [(i, (i + by) % 16) for i in range(16)])]
    slice x2 -> x0, local copies, waits for them, and re-layouts: 4.85 us -> none  [the longest x1 3.35 us: per_device(): kept = [memory[0, :, 0], memory[0, :, 1]]]
  transfers between devices with their start and end apart: 35 -> 33, of which waited for: 8 -> 7; matrix products, arithmetic and copies ran while one was open for 3% -> 2% of each run, Pallas kernels for 3% -> 3%
where the time goes in v6:
time: 330 us; the launch traced here: 328 us
  starting transfers between devices  212 us (64%)
  waiting for transfers between devices  84.2 us (26%)
  Pallas kernels  22 us (7%)
  local copies, waits for them, and re-layouts  5.67 us (2%)
    all_to_all x1, starting transfers between devices, per_device(): arrived = lax.all_to_all(chunks, ('y', 's', 'p'), 0, 0, tiled=True)  83.1 us
    all_to_all x1, waiting for transfers between devices, per_device(): lax.all_to_all(made.reshape(chunks.shape), ('y', 's', 'p'), 0, 0, tiled=T...  43.4 us
    ppermute x3, starting transfers between devices, gathered(): own = lax.ppermute(moved, ('x', 'p'), lift_pairs())  43.3 us
    ppermute x13, starting transfers between devices, gathered(): other = lambda piece: lax.ppermute(piece, 'c', [(0, 1), (1, 0)])  26.6 us
    ppermute x3, waiting for transfers between devices, gathered(): right = lax.ppermute(own, 'x', ring(-1))  20.1 us
    all_to_all x1, starting transfers between devices, per_device(): lax.all_to_all(made.reshape(chunks.shape), ('y', 's', 'p'), 0, 0, tiled=T...  14.9 us
    pallas_call x1, Pallas kernels, experts(): pl.pallas_call(functools.partial(experts_kernel, pieces), out_shape=jax.S...  10.4 us
    ppermute x1, waiting for transfers between devices, gathered(): lax.ppermute(right[cut:], 'x', ring(-1))  10.1 us
  transfers between devices with their start and end apart: 33, of which 7 were waited for; matrix products, arithmetic and copies ran while one was open for 2% of the time, Pallas kernels for 3%

profile of v6, /device:TPU:6, one launch (start us, length us, event | category | flops | bytes accessed | tf_op | source)
XLA Modules:
  0.0 328.3 jit_solution(10587510896284420309)
XLA Ops:
  4.8 3.5 %collective-permute-start = (bf16[2,128,2048]{2,1,0:T(8,128)(2,1)S(1)}, bf16[2,128,2048]{2,1,0:T(8,128)(2,1)S(1)}, u32[]{:S(2)}, u32[]{:S(2)}) collective-permute-start(bf16[2,128,2048]{2,1,0:T(8,128)(2,1)S(1)} %bitcast.25), channel_id=1, source_target_pairs={{0,32},{32,64},{64,96},{96,128},{128,160},{160,192},{192,224},{224... | collective-permute-start | bytes 3145736 | tf_op jit(solution)/shard_map/ppermute | solution.py:292
  8.3 4.8 %collective-permute-start.1 = (bf16[2,128,2048]{2,1,0:T(8,128)(2,1)S(1)}, bf16[2,128,2048]{2,1,0:T(8,128)(2,1)}, u32[]{:S(2)}, u32[]{:S(2)}) collective-permute-start(bf16[2,128,2048]{2,1,0:T(8,128)(2,1)S(1)} %bitcast.26), channel_id=1, source_target_pairs={{0,64},{32,96},{64,128},{96,160},{128,192},{160,224},{192,256},{22... | collective-permute-start | bytes 3145736 | tf_op jit(solution)/shard_map/ppermute | solution.py:292
  14.7 15.6 %collective-permute-start.3 = (bf16[176,2048]{1,0:T(8,128)(2,1)S(1)}, bf16[176,2048]{1,0:T(8,128)(2,1)}, u32[]{:S(2)}, u32[]{:S(2)}) collective-permute-start(bf16[176,2048]{1,0:T(8,128)(2,1)S(1)} %broadcast_select_fusion.2), channel_id=1, source_target_pairs={{0,0},{2,4},{4,2},{6,6},{128,130},{130,134},{132,128},{134,132},{2... | collective-permute-start | bytes 2162696 | tf_op jit(solution)/shard_map/ppermute | solution.py:276
  31.3 15.4 %collective-permute-start.21 = (bf16[176,2048]{1,0:T(8,128)(2,1)}, bf16[176,2048]{1,0:T(8,128)(2,1)}, u32[]{:S(2)}, u32[]{:S(2)}) collective-permute-start(bf16[176,2048]{1,0:T(8,128)(2,1)} %broadcast_select_fusion), channel_id=1, source_target_pairs={{0,0},{2,4},{4,2},{6,6},{128,130},{130,134},{132,128},{134,132},{2... | collective-permute-start | bytes 2162696 | tf_op jit(solution)/shard_map/ppermute | solution.py:276
  46.8 2.1 broadcast_select_fusion.1
  48.8 12.3 %collective-permute-start.12 = (bf16[176,2048]{1,0:T(8,128)(2,1)}, bf16[176,2048]{1,0:T(8,128)(2,1)}, u32[]{:S(2)}, u32[]{:S(2)}) collective-permute-start(bf16[176,2048]{1,0:T(8,128)(2,1)} %broadcast_select_fusion.1), channel_id=1, source_target_pairs={{0,0},{2,4},{4,2},{6,6},{128,130},{130,134},{132,128},{134,132},{2... | collective-permute-start | bytes 2162696 | tf_op jit(solution)/shard_map/ppermute | solution.py:276
  61.1 1.9 collective-permute-start.4
  63.1 1.9 collective-permute-start.5
  67.8 9.8 %attend.1 = (bf16[128,2048]{1,0:T(8,128)(2,1)S(1)}, bf16[3072,128]{1,0:T(8,128)(2,1)}) custom-call(s32[1]{0:T(128)S(6)} %copy.20.source, bf16[128,2048]{1,0:T(8,128)(2,1)S(1)} %copy-done, bf16[2,128,2048]{2,1,0:T(8,128)(2,1)} %bitcast.22, bf16[2,128,2048]{2,1,0:T(8,128)(2,1)} %copy-done.7, bf16[2,128,2048]{2,1,0:T(8,128)(2,1)} %collective-permute-done.1.far_off, ...), custom_call_target="tpu_custom_call" | custom-call | flops 268435456 | bytes 2621440 | tf_op jit(solution)/shard_map/attend/pallas_call | solution.py:129
  77.6 83.1 %all-to-all-start = ((bf16[64,48,128]{2,1,0:T(8,128)(2,1)}), bf16[64,48,128]{2,1,0:T(8,128)(2,1)S(1)}, u32[]{:S(2)}, u32[]{:S(2)}) async-start(bf16[64,48,128]{2,1,0:T(8,128)(2,1)} %bitcast.6), calls=%async_computation | async-start | bytes 1572864 | tf_op jit(solution)/shard_map/all_to_all | solution.py:320
  160.7 3.9 %collective-permute-start.7 = (bf16[176,2048]{1,0:T(8,128)(2,1)}, bf16[176,2048]{1,0:T(8,128)(2,1)S(1)}, u32[]{:S(2)}, u32[]{:S(2)}) collective-permute-start(bf16[176,2048]{1,0:T(8,128)(2,1)} %collective-permute-done.3.refs_0_), channel_id=1, source_target_pairs={{0,384},{128,0},{256,128},{384,256},{1,385},{129,1},{257,129},{385... | collective-permute-start | bytes 2162696 | tf_op jit(solution)/shard_map/ppermute | solution.py:278
  164.6 1.9 collective-permute-start.25
  166.6 5.1 %collective-permute-start.22 = (bf16[176,2048]{1,0:T(8,128)(2,1)}, bf16[176,2048]{1,0:T(8,128)(2,1)S(1)}, u32[]{:S(2)}, u32[]{:S(2)}) collective-permute-start(bf16[176,2048]{1,0:T(8,128)(2,1)} %collective-permute-done.21.refs_16_), channel_id=1, source_target_pairs={{0,128},{128,256},{256,384},{384,0},{1,129},{129,257},{257,385},{3... | collective-permute-start | bytes 2162696 | tf_op jit(solution)/shard_map/ppermute | solution.py:277
  171.7 1.9 collective-permute-start.13
  173.7 1.9 collective-permute-start.14
  175.6 7.4 %collective-permute-done.7.refs_4_ = bf16[176,2048]{1,0:T(8,128)(2,1)S(1)} collective-permute-done((bf16[176,2048]{1,0:T(8,128)(2,1)}, bf16[176,2048]{1,0:T(8,128)(2,1)S(1)}, u32[]{:S(2)}, u32[]{:S(2)}) %collective-permute-start.7) | collective-permute-done | bytes 720928 | tf_op jit(solution)/shard_map/ppermute | solution.py:278
  183.0 2.7 collective-permute-start.16
  185.7 12.7 %collective-permute-done.25.refs_20_ = bf16[176,2048]{1,0:T(8,128)(2,1)S(1)} collective-permute-done((bf16[176,2048]{1,0:T(8,128)(2,1)}, bf16[176,2048]{1,0:T(8,128)(2,1)S(1)}, u32[]{:S(2)}, u32[]{:S(2)}) %collective-permute-start.25) | collective-permute-done | bytes 720928 | tf_op jit(solution)/shard_map/ppermute | solution.py:278
  200.4 2.7 collective-permute-start.27
  203.2 5.0 %collective-permute-start.26 = (bf16[96,2048]{1,0:T(8,128)(2,1)S(1)}, bf16[96,2048]{1,0:T(8,128)(2,1)S(1)}, u32[]{:S(2)}, u32[]{:S(2)}) collective-permute-start(bf16[96,2048]{1,0:T(8,128)(2,1)S(1)} %slice.8), channel_id=1, source_target_pairs={{0,128},{128,256},{256,384},{384,0},{1,129},{129,257},{257,385},{3... | collective-permute-start | bytes 1179656 | tf_op jit(solution)/shard_map/ppermute | solution.py:285
  210.1 10.1 %collective-permute-done.27.refs_22_ = bf16[80,2048]{1,0:T(8,128)(2,1)S(1)} collective-permute-done((bf16[80,2048]{1,0:T(8,128)(2,1)S(1)}, bf16[80,2048]{1,0:T(8,128)(2,1)S(1)}, u32[]{:S(2)}, u32[]{:S(2)}) %collective-permute-start.27) | collective-permute-done | bytes 327712 | tf_op jit(solution)/shard_map/ppermute | solution.py:285
  224.1 2.4 collective-permute-start.9
  226.5 1.9 collective-permute-start.15
  228.4 3.9 %collective-permute-start.17 = (bf16[176,2048]{1,0:T(8,128)(2,1)S(1)}, bf16[176,2048]{1,0:T(8,128)(2,1)S(1)}, u32[]{:S(2)}, u32[]{:S(2)}) collective-permute-start(bf16[176,2048]{1,0:T(8,128)(2,1)S(1)} %collective-permute-done.16.refs_12_), channel_id=1, source_target_pairs={{0,384},{128,0},{256,128},{384,256},{1,385},{129,1},{257,129},{385... | collective-permute-start | bytes 2162696 | tf_op jit(solution)/shard_map/ppermute | solution.py:282
  232.4 1.9 collective-permute-start.18
  234.3 8.5 %collective-permute-done.8.refs_5_ = bf16[176,2048]{1,0:T(8,128)(2,1)S(1)} collective-permute-done((bf16[176,2048]{1,0:T(8,128)(2,1)}, bf16[176,2048]{1,0:T(8,128)(2,1)S(1)}, u32[]{:S(2)}, u32[]{:S(2)}) %collective-permute-start.8) | collective-permute-done | bytes 720928 | tf_op jit(solution)/shard_map/ppermute | solution.py:280
  244.7 2.4 collective-permute-start.28
  247.1 1.9 collective-permute-start.10
  252.0 2.6 collective-permute-start.29
  257.6 10.4 %experts.1 = bf16[3072,128]{1,0:T(8,128)(2,1)} custom-call(bf16[3072,128]{1,0:T(8,128)(2,1)} %bitcast.23, bf16[176,2048]{1,0:T(8,128)(2,1)} %collective-permute-done.3.refs_0_, bf16[176,2048]{1,0:T(8,128)(2,1)} %collective-permute-done.4.refs_1_, bf16[176,2048]{1,0:T(8,128)(2,1)} %collective-permute-done.5.refs_2_, bf16[176,2048]{1,0:T(8,128)(2,1)} %copy-done.13, ...), custom_call_target="tpu_custom_call" | custom-call | flops 3321888768 | bytes 17301504 | tf_op jit(solution)/shard_map/experts/pallas_call | solution.py:214
  268.0 14.9 %all-to-all-start.1 = ((bf16[64,48,128]{2,1,0:T(8,128)(2,1)}), bf16[64,48,128]{2,1,0:T(8,128)(2,1)S(1)}, u32[]{:S(2)}, u32[]{:S(2)}) async-start(bf16[64,48,128]{2,1,0:T(8,128)(2,1)} %bitcast.24), calls=%async_computation.1 | async-start | bytes 1572864 | tf_op jit(solution)/shard_map/all_to_all | solution.py:322
  283.0 43.4 %all-to-all-done.1 = bf16[64,48,128]{2,1,0:T(8,128)(2,1)S(1)} async-done(((bf16[64,48,128]{2,1,0:T(8,128)(2,1)}), bf16[64,48,128]{2,1,0:T(8,128)(2,1)S(1)}, u32[]{:S(2)}, u32[]{:S(2)}) %all-to-all-start.1) | async-done | bytes 786464 | tf_op jit(solution)/shard_map/all_to_all | solution.py:322
  (96 shorter events, 27.0 us)
Async XLA Ops:
  0.0 14.6 %collective-permute-start.2 = (bf16[176,2048]{1,0:T(8,128)(2,1)}, bf16[176,2048]{1,0:T(8,128)(2,1)}, u32[]{:S(2)}, u32[]{:S(2)}) collective-permute-start(bf16[176,2048]{1,0:T(8,128)(2,1)} %bitcast.27), channel_id=1, source_target_pairs={{258,2},{132,4},{390,6},{386,130},{4,132},{262,134},{2,258},{388,2... | collective-permute-start | bytes 2162696 | tf_op jit(solution)/shard_map/ppermute | solution.py:274
  1.7 28.7 %collective-permute-start.20 = (bf16[176,2048]{1,0:T(8,128)(2,1)}, bf16[176,2048]{1,0:T(8,128)(2,1)}, u32[]{:S(2)}, u32[]{:S(2)}) collective-permute-start(bf16[176,2048]{1,0:T(8,128)(2,1)} %param.19), channel_id=1, source_target_pairs={{258,2},{132,4},{390,6},{386,130},{4,132},{262,134},{2,258},{388,2... | collective-permute-start | bytes 2162696 | tf_op jit(solution)/shard_map/ppermute | solution.py:274
  4.8 58.3 %collective-permute-start = (bf16[2,128,2048]{2,1,0:T(8,128)(2,1)S(1)}, bf16[2,128,2048]{2,1,0:T(8,128)(2,1)S(1)}, u32[]{:S(2)}, u32[]{:S(2)}) collective-permute-start(bf16[2,128,2048]{2,1,0:T(8,128)(2,1)S(1)} %bitcast.25), channel_id=1, source_target_pairs={{0,32},{32,64},{64,96},{96,128},{128,160},{160,192},{192,224},{224... | collective-permute-start | bytes 3145736 | tf_op jit(solution)/shard_map/ppermute | solution.py:292
  8.3 58.9 %collective-permute-start.1 = (bf16[2,128,2048]{2,1,0:T(8,128)(2,1)S(1)}, bf16[2,128,2048]{2,1,0:T(8,128)(2,1)}, u32[]{:S(2)}, u32[]{:S(2)}) collective-permute-start(bf16[2,128,2048]{2,1,0:T(8,128)(2,1)S(1)} %bitcast.26), channel_id=1, source_target_pairs={{0,64},{32,96},{64,128},{96,160},{128,192},{160,224},{192,256},{22... | collective-permute-start | bytes 3145736 | tf_op jit(solution)/shard_map/ppermute | solution.py:292
  13.1 33.7 %collective-permute-start.11 = (bf16[176,2048]{1,0:T(8,128)(2,1)}, bf16[176,2048]{1,0:T(8,128)(2,1)}, u32[]{:S(2)}, u32[]{:S(2)}) collective-permute-start(bf16[176,2048]{1,0:T(8,128)(2,1)} %bitcast.9), channel_id=1, source_target_pairs={{258,2},{132,4},{390,6},{386,130},{4,132},{262,134},{2,258},{388,2... | collective-permute-start | bytes 2162696 | tf_op jit(solution)/shard_map/ppermute | solution.py:274
  14.7 46.4 %collective-permute-start.3 = (bf16[176,2048]{1,0:T(8,128)(2,1)S(1)}, bf16[176,2048]{1,0:T(8,128)(2,1)}, u32[]{:S(2)}, u32[]{:S(2)}) collective-permute-start(bf16[176,2048]{1,0:T(8,128)(2,1)S(1)} %broadcast_select_fusion.2), channel_id=1, source_target_pairs={{0,0},{2,4},{4,2},{6,6},{128,130},{130,134},{132,128},{134,132},{2... | collective-permute-start | bytes 2162696 | tf_op jit(solution)/shard_map/ppermute | solution.py:276
  31.3 133.3 %collective-permute-start.21 = (bf16[176,2048]{1,0:T(8,128)(2,1)}, bf16[176,2048]{1,0:T(8,128)(2,1)}, u32[]{:S(2)}, u32[]{:S(2)}) collective-permute-start(bf16[176,2048]{1,0:T(8,128)(2,1)} %broadcast_select_fusion), channel_id=1, source_target_pairs={{0,0},{2,4},{4,2},{6,6},{128,130},{130,134},{132,128},{134,132},{2... | collective-permute-start | bytes 2162696 | tf_op jit(solution)/shard_map/ppermute | solution.py:276
  48.8 117.7 %collective-permute-start.12 = (bf16[176,2048]{1,0:T(8,128)(2,1)}, bf16[176,2048]{1,0:T(8,128)(2,1)}, u32[]{:S(2)}, u32[]{:S(2)}) collective-permute-start(bf16[176,2048]{1,0:T(8,128)(2,1)} %broadcast_select_fusion.1), channel_id=1, source_target_pairs={{0,0},{2,4},{4,2},{6,6},{128,130},{130,134},{132,128},{134,132},{2... | collective-permute-start | bytes 2162696 | tf_op jit(solution)/shard_map/ppermute | solution.py:276
  61.1 110.6 %collective-permute-start.4 = (bf16[176,2048]{1,0:T(8,128)(2,1)}, bf16[176,2048]{1,0:T(8,128)(2,1)}, u32[]{:S(2)}, u32[]{:S(2)}) collective-permute-start(bf16[176,2048]{1,0:T(8,128)(2,1)} %collective-permute-done.3.refs_0_), channel_id=1, source_target_pairs={{0,128},{128,256},{256,384},{384,0},{1,129},{129,257},{257,385},{3... | collective-permute-start | bytes 2162696 | tf_op jit(solution)/shard_map/ppermute | solution.py:277
  63.1 110.6 %collective-permute-start.5 = (bf16[176,2048]{1,0:T(8,128)(2,1)}, bf16[176,2048]{1,0:T(8,128)(2,1)}, u32[]{:S(2)}, u32[]{:S(2)}) collective-permute-start(bf16[176,2048]{1,0:T(8,128)(2,1)} %collective-permute-done.3.refs_0_), channel_id=1, source_target_pairs={{0,1},{1,0},{2,3},{3,2},{4,5},{5,4},{6,7},{7,6},{8,9},{9,8},{10,11... | collective-permute-start | bytes 2162696 | tf_op jit(solution)/shard_map/ppermute | solution.py:286
  77.6 179.1 %all-to-all-start = ((bf16[64,48,128]{2,1,0:T(8,128)(2,1)}), bf16[64,48,128]{2,1,0:T(8,128)(2,1)S(1)}, u32[]{:S(2)}, u32[]{:S(2)}) async-start(bf16[64,48,128]{2,1,0:T(8,128)(2,1)} %bitcast.6), calls=%async_computation | async-start | bytes 1572864 | tf_op jit(solution)/shard_map/all_to_all | solution.py:320
  160.7 22.3 %collective-permute-start.7 = (bf16[176,2048]{1,0:T(8,128)(2,1)}, bf16[176,2048]{1,0:T(8,128)(2,1)S(1)}, u32[]{:S(2)}, u32[]{:S(2)}) collective-permute-start(bf16[176,2048]{1,0:T(8,128)(2,1)} %collective-permute-done.3.refs_0_), channel_id=1, source_target_pairs={{0,384},{128,0},{256,128},{384,256},{1,385},{129,1},{257,129},{385... | collective-permute-start | bytes 2162696 | tf_op jit(solution)/shard_map/ppermute | solution.py:278
  164.6 33.8 %collective-permute-start.25 = (bf16[176,2048]{1,0:T(8,128)(2,1)}, bf16[176,2048]{1,0:T(8,128)(2,1)S(1)}, u32[]{:S(2)}, u32[]{:S(2)}) collective-permute-start(bf16[176,2048]{1,0:T(8,128)(2,1)} %collective-permute-done.21.refs_16_), channel_id=1, source_target_pairs={{0,384},{128,0},{256,128},{384,256},{1,385},{129,1},{257,129},{385... | collective-permute-start | bytes 2162696 | tf_op jit(solution)/shard_map/ppermute | solution.py:278
  166.6 33.8 %collective-permute-start.22 = (bf16[176,2048]{1,0:T(8,128)(2,1)}, bf16[176,2048]{1,0:T(8,128)(2,1)S(1)}, u32[]{:S(2)}, u32[]{:S(2)}) collective-permute-start(bf16[176,2048]{1,0:T(8,128)(2,1)} %collective-permute-done.21.refs_16_), channel_id=1, source_target_pairs={{0,128},{128,256},{256,384},{384,0},{1,129},{129,257},{257,385},{3... | collective-permute-start | bytes 2162696 | tf_op jit(solution)/shard_map/ppermute | solution.py:277
  171.7 31.4 %collective-permute-start.13 = (bf16[176,2048]{1,0:T(8,128)(2,1)}, bf16[176,2048]{1,0:T(8,128)(2,1)S(1)}, u32[]{:S(2)}, u32[]{:S(2)}) collective-permute-start(bf16[176,2048]{1,0:T(8,128)(2,1)} %collective-permute-done.12.refs_8_), channel_id=1, source_target_pairs={{0,128},{128,256},{256,384},{384,0},{1,129},{129,257},{257,385},{3... | collective-permute-start | bytes 2162696 | tf_op jit(solution)/shard_map/ppermute | solution.py:277
  173.7 34.5 %collective-permute-start.14 = (bf16[176,2048]{1,0:T(8,128)(2,1)}, bf16[176,2048]{1,0:T(8,128)(2,1)S(1)}, u32[]{:S(2)}, u32[]{:S(2)}) collective-permute-start(bf16[176,2048]{1,0:T(8,128)(2,1)} %collective-permute-done.12.refs_8_), channel_id=1, source_target_pairs={{0,1},{1,0},{2,3},{3,2},{4,5},{5,4},{6,7},{7,6},{8,9},{9,8},{10,11... | collective-permute-start | bytes 2162696 | tf_op jit(solution)/shard_map/ppermute | solution.py:286
  183.0 39.1 %collective-permute-start.16 = (bf16[176,2048]{1,0:T(8,128)(2,1)}, bf16[176,2048]{1,0:T(8,128)(2,1)S(1)}, u32[]{:S(2)}, u32[]{:S(2)}) collective-permute-start(bf16[176,2048]{1,0:T(8,128)(2,1)} %collective-permute-done.12.refs_8_), channel_id=1, source_target_pairs={{0,384},{128,0},{256,128},{384,256},{1,385},{129,1},{257,129},{385... | collective-permute-start | bytes 2162696 | tf_op jit(solution)/shard_map/ppermute | solution.py:278
  198.4 25.6 %collective-permute-start.23 = (bf16[176,2048]{1,0:T(8,128)(2,1)}, bf16[176,2048]{1,0:T(8,128)(2,1)S(1)}, u32[]{:S(2)}, u32[]{:S(2)}) collective-permute-start(bf16[176,2048]{1,0:T(8,128)(2,1)} %collective-permute-done.21.refs_16_), channel_id=1, source_target_pairs={{0,1},{1,0},{2,3},{3,2},{4,5},{5,4},{6,7},{7,6},{8,9},{9,8},{10,11... | collective-permute-start | bytes 2162696 | tf_op jit(solution)/shard_map/ppermute | solution.py:286
  200.4 19.8 %collective-permute-start.27 = (bf16[80,2048]{1,0:T(8,128)(2,1)S(1)}, bf16[80,2048]{1,0:T(8,128)(2,1)S(1)}, u32[]{:S(2)}, u32[]{:S(2)}) collective-permute-start(bf16[80,2048]{1,0:T(8,128)(2,1)S(1)} %slice.9), channel_id=1, source_target_pairs={{0,384},{128,0},{256,128},{384,256},{1,385},{129,1},{257,129},{385... | collective-permute-start | bytes 983048 | tf_op jit(solution)/shard_map/ppermute | solution.py:285
  203.2 23.3 %collective-permute-start.26 = (bf16[96,2048]{1,0:T(8,128)(2,1)S(1)}, bf16[96,2048]{1,0:T(8,128)(2,1)S(1)}, u32[]{:S(2)}, u32[]{:S(2)}) collective-permute-start(bf16[96,2048]{1,0:T(8,128)(2,1)S(1)} %slice.8), channel_id=1, source_target_pairs={{0,128},{128,256},{256,384},{384,0},{1,129},{129,257},{257,385},{3... | collective-permute-start | bytes 1179656 | tf_op jit(solution)/shard_map/ppermute | solution.py:285
  208.2 24.2 %collective-permute-start.6 = (bf16[176,2048]{1,0:T(8,128)(2,1)}, bf16[176,2048]{1,0:T(8,128)(2,1)S(1)}, u32[]{:S(2)}, u32[]{:S(2)}) collective-permute-start(bf16[176,2048]{1,0:T(8,128)(2,1)} %collective-permute-done.4.refs_1_), channel_id=1, source_target_pairs={{0,1},{1,0},{2,3},{3,2},{4,5},{5,4},{6,7},{7,6},{8,9},{9,8},{10,11... | collective-permute-start | bytes 2162696 | tf_op jit(solution)/shard_map/ppermute | solution.py:286
  220.2 8.2 %collective-permute-start.30 = (bf16[80,2048]{1,0:T(8,128)(2,1)S(1)}, bf16[80,2048]{1,0:T(8,128)(2,1)S(1)}, u32[]{:S(2)}, u32[]{:S(2)}) collective-permute-start(bf16[80,2048]{1,0:T(8,128)(2,1)S(1)} %collective-permute-done.27.refs_22_), channel_id=1, source_target_pairs={{0,1},{1,0},{2,3},{3,2},{4,5},{5,4},{6,7},{7,6},{8,9},{9,8},{10,11... | collective-permute-start | bytes 983048 | tf_op jit(solution)/shard_map/ppermute | solution.py:286
  222.1 20.6 %collective-permute-start.8 = (bf16[176,2048]{1,0:T(8,128)(2,1)}, bf16[176,2048]{1,0:T(8,128)(2,1)S(1)}, u32[]{:S(2)}, u32[]{:S(2)}) collective-permute-start(bf16[176,2048]{1,0:T(8,128)(2,1)} %collective-permute-done.4.refs_1_), channel_id=1, source_target_pairs={{0,128},{128,256},{256,384},{384,0},{1,129},{129,257},{257,385},{3... | collective-permute-start | bytes 2162696 | tf_op jit(solution)/shard_map/ppermute | solution.py:280
  224.1 20.6 %collective-permute-start.9 = (bf16[176,2048]{1,0:T(8,128)(2,1)S(1)}, bf16[176,2048]{1,0:T(8,128)(2,1)S(1)}, u32[]{:S(2)}, u32[]{:S(2)}) collective-permute-start(bf16[176,2048]{1,0:T(8,128)(2,1)S(1)} %collective-permute-done.7.refs_4_), channel_id=1, source_target_pairs={{0,1},{1,0},{2,3},{3,2},{4,5},{5,4},{6,7},{7,6},{8,9},{9,8},{10,11... | collective-permute-start | bytes 2162696 | tf_op jit(solution)/shard_map/ppermute | solution.py:286
  226.5 20.6 %collective-permute-start.15 = (bf16[176,2048]{1,0:T(8,128)(2,1)S(1)}, bf16[176,2048]{1,0:T(8,128)(2,1)S(1)}, u32[]{:S(2)}, u32[]{:S(2)}) collective-permute-start(bf16[176,2048]{1,0:T(8,128)(2,1)S(1)} %collective-permute-done.13.refs_9_), channel_id=1, source_target_pairs={{0,1},{1,0},{2,3},{3,2},{4,5},{5,4},{6,7},{7,6},{8,9},{9,8},{10,11... | collective-permute-start | bytes 2162696 | tf_op jit(solution)/shard_map/ppermute | solution.py:286
  228.4 21.6 %collective-permute-start.17 = (bf16[176,2048]{1,0:T(8,128)(2,1)S(1)}, bf16[176,2048]{1,0:T(8,128)(2,1)S(1)}, u32[]{:S(2)}, u32[]{:S(2)}) collective-permute-start(bf16[176,2048]{1,0:T(8,128)(2,1)S(1)} %collective-permute-done.16.refs_12_), channel_id=1, source_target_pairs={{0,384},{128,0},{256,128},{384,256},{1,385},{129,1},{257,129},{385... | collective-permute-start | bytes 2162696 | tf_op jit(solution)/shard_map/ppermute | solution.py:282
  232.4 19.6 %collective-permute-start.18 = (bf16[176,2048]{1,0:T(8,128)(2,1)S(1)}, bf16[176,2048]{1,0:T(8,128)(2,1)S(1)}, u32[]{:S(2)}, u32[]{:S(2)}) collective-permute-start(bf16[176,2048]{1,0:T(8,128)(2,1)S(1)} %collective-permute-done.16.refs_12_), channel_id=1, source_target_pairs={{0,1},{1,0},{2,3},{3,2},{4,5},{5,4},{6,7},{7,6},{8,9},{9,8},{10,11... | collective-permute-start | bytes 2162696 | tf_op jit(solution)/shard_map/ppermute | solution.py:286
  242.8 11.8 %collective-permute-start.24 = (bf16[176,2048]{1,0:T(8,128)(2,1)S(1)}, bf16[176,2048]{1,0:T(8,128)(2,1)S(1)}, u32[]{:S(2)}, u32[]{:S(2)}) collective-permute-start(bf16[176,2048]{1,0:T(8,128)(2,1)S(1)} %collective-permute-done.22.refs_17_), channel_id=1, source_target_pairs={{0,1},{1,0},{2,3},{3,2},{4,5},{5,4},{6,7},{7,6},{8,9},{9,8},{10,11... | collective-permute-start | bytes 2162696 | tf_op jit(solution)/shard_map/ppermute | solution.py:286
  244.7 9.9 %collective-permute-start.28 = (bf16[176,2048]{1,0:T(8,128)(2,1)S(1)}, bf16[176,2048]{1,0:T(8,128)(2,1)S(1)}, u32[]{:S(2)}, u32[]{:S(2)}) collective-permute-start(bf16[176,2048]{1,0:T(8,128)(2,1)S(1)} %collective-permute-done.25.refs_20_), channel_id=1, source_target_pairs={{0,1},{1,0},{2,3},{3,2},{4,5},{5,4},{6,7},{7,6},{8,9},{9,8},{10,11... | collective-permute-start | bytes 2162696 | tf_op jit(solution)/shard_map/ppermute | solution.py:286
  247.1 8.6 %collective-permute-start.10 = (bf16[176,2048]{1,0:T(8,128)(2,1)S(1)}, bf16[176,2048]{1,0:T(8,128)(2,1)S(1)}, u32[]{:S(2)}, u32[]{:S(2)}) collective-permute-start(bf16[176,2048]{1,0:T(8,128)(2,1)S(1)} %collective-permute-done.8.refs_5_), channel_id=1, source_target_pairs={{0,1},{1,0},{2,3},{3,2},{4,5},{5,4},{6,7},{7,6},{8,9},{9,8},{10,11... | collective-permute-start | bytes 2162696 | tf_op jit(solution)/shard_map/ppermute | solution.py:286
  250.1 6.7 %collective-permute-start.19 = (bf16[176,2048]{1,0:T(8,128)(2,1)S(1)}, bf16[176,2048]{1,0:T(8,128)(2,1)}, u32[]{:S(2)}, u32[]{:S(2)}) collective-permute-start(bf16[176,2048]{1,0:T(8,128)(2,1)S(1)} %collective-permute-done.17.refs_13_), channel_id=1, source_target_pairs={{0,1},{1,0},{2,3},{3,2},{4,5},{5,4},{6,7},{7,6},{8,9},{9,8},{10,11... | collective-permute-start | bytes 2162696 | tf_op jit(solution)/shard_map/ppermute | solution.py:286
  268.0 58.4 %all-to-all-start.1 = ((bf16[64,48,128]{2,1,0:T(8,128)(2,1)}), bf16[64,48,128]{2,1,0:T(8,128)(2,1)S(1)}, u32[]{:S(2)}, u32[]{:S(2)}) async-start(bf16[64,48,128]{2,1,0:T(8,128)(2,1)} %bitcast.24), calls=%async_computation.1 | async-start | bytes 1572864 | tf_op jit(solution)/shard_map/all_to_all | solution.py:322
  (26 other events, 456.4 us)
